TPU v7x, 32 devices: a whole 2x2x4 slice. The times are simulated.
32 devices in a mesh: groups: 2 (over y), dp: 8 (over z, x), pipe: 2 (over core).
Axes of the slice: x: 2, y: 2, z: 4, core: 2. Of those that a mesh axis runs over, the one named last changes fastest.
Arguments:
- inputs: bfloat16 [2, 32, 256, 512], P('pipe', ('groups', 'dp')), parts along dimension 1, may hold values from -24 to 24
- out_grad: bfloat16 [2, 32, 256, 512], P('pipe', ('groups', 'dp')), parts along dimension 1, may hold values from -6 to 6
- lengths: int32 [2, 32], P('pipe', ('groups', 'dp')), parts along dimension 1, may hold values from 64 to 256, as said below
- master: float32 [2, 4096, 512], P('pipe', ('groups', 'dp')), parts along dimension 1, may hold values from -16 to 16
- moment_first: float32 [2, 4096, 512], P('pipe', ('groups', 'dp')), parts along dimension 1, may hold values from -16 to 16
- moment_second: float32 [2, 4096, 512], P('pipe', ('groups', 'dp')), parts along dimension 1, may hold values from 0.0005 to 2000
Outputs:
- new_master: float32 [2, 4096, 512], P('pipe', ('groups', 'dp')), parts along dimension 1
- new_first: float32 [2, 4096, 512], P('pipe', ('groups', 'dp')), parts along dimension 1
- new_second: float32 [2, 4096, 512], P('pipe', ('groups', 'dp')), parts along dimension 1
There are 2 independent parts, one for each index of `groups`. A program takes and returns all parts, laid end to end along the dimension named above; each array names one. Nothing has to cross between parts.
Inputs may be any that keep to these rules, and one draw needn't show every extreme that they name: `lengths`: every draw has a sequence of all 256 tokens.
All inputs are finite; a program needn't handle non-finite values.
Results may differ from a plain program's by a relative error of at most 0.0055.
Values may be sent and summed in bfloat16 or wider, within the bound.
No kernel may reach another device: no remote copies, remote signals or barrier semaphores. Data moves between devices by JAX's collectives and lax.ppermute only.
A program may use at most 128 MiB of HBM per device.

v0:
```python
import jax
import jax.numpy as jnp
from jax import lax
from jax.sharding import PartitionSpec as P

HEAD = 64
STEP = 10


def swapped(value, axis, bit):
    return lax.ppermute(value, axis, [(i, i ^ 1 << bit) for i in range(lax.axis_size(axis))])


def layer_norm(resid):
    centre = resid - jnp.mean(resid, axis=-1, keepdims=True)
    return centre * lax.rsqrt(jnp.mean(centre * centre, axis=-1, keepdims=True) + 1e-05)


def attention(query, keys, values, live):
    length, width = query.shape
    heads = width // HEAD
    q_heads = query.reshape(length, heads, HEAD)
    k_heads = keys.reshape(length, heads, HEAD)
    v_heads = values.reshape(length, heads, HEAD)
    scores = jnp.einsum(
        "qhd,khd->hqk", q_heads, k_heads, preferred_element_type=jnp.float32
    ) * HEAD ** (-0.5)
    keep = jnp.arange(length) < live
    scores = jnp.where(keep[None, None, :], scores, -1e30)
    scores = scores - jnp.max(scores, axis=-1, keepdims=True)
    expo = jnp.exp(scores)
    probs = (expo / jnp.sum(expo, axis=-1, keepdims=True)).astype(jnp.bfloat16)
    mixed = jnp.einsum("hqk,khd->qhd", probs, v_heads, preferred_element_type=jnp.float32)
    return mixed.reshape(length, width).astype(jnp.bfloat16)


def section_forward(weights, inputs, live):
    width = inputs.shape[1]
    factor = width ** (-0.5)
    query = (jnp.dot(inputs, weights[:width], preferred_element_type=jnp.float32) * factor).astype(
        jnp.bfloat16
    )
    keys = (
        jnp.dot(inputs, weights[width : 2 * width], preferred_element_type=jnp.float32) * factor
    ).astype(jnp.bfloat16)
    values = (
        jnp.dot(inputs, weights[2 * width : 3 * width], preferred_element_type=jnp.float32) * factor
    ).astype(jnp.bfloat16)
    mixed = attention(query, keys, values, live)
    resid = (
        inputs.astype(jnp.float32)
        + jnp.dot(mixed, weights[3 * width :], preferred_element_type=jnp.float32) * factor
    )
    return (layer_norm(resid).astype(jnp.bfloat16), (inputs, query, keys, values, mixed, resid))


def section_backward(weights, saved, grad_out, live, want_input):
    inputs, query, keys, values, mixed, resid = saved
    width = inputs.shape[1]
    factor = width ** (-0.5)
    _, norm_back = jax.vjp(layer_norm, resid)
    grad_resid = norm_back(grad_out.astype(jnp.float32))[0]
    grad_attn = grad_resid.astype(jnp.bfloat16)
    grad_wo = jnp.dot(mixed.T, grad_attn, preferred_element_type=jnp.float32) * factor
    grad_mixed = (
        jnp.dot(grad_attn, weights[3 * width :].T, preferred_element_type=jnp.float32) * factor
    ).astype(jnp.bfloat16)
    _, core_back = jax.vjp(lambda a, b, c: attention(a, b, c, live), query, keys, values)
    grad_q, grad_k, grad_v = core_back(grad_mixed)
    grad_wq = jnp.dot(inputs.T, grad_q, preferred_element_type=jnp.float32) * factor
    grad_wk = jnp.dot(inputs.T, grad_k, preferred_element_type=jnp.float32) * factor
    grad_wv = jnp.dot(inputs.T, grad_v, preferred_element_type=jnp.float32) * factor
    grads = jnp.concatenate([grad_wq, grad_wk, grad_wv, grad_wo], axis=0)
    if want_input:
        back = jnp.dot(grad_q, weights[:width].T, preferred_element_type=jnp.float32)
        back = back + jnp.dot(
            grad_k, weights[width : 2 * width].T, preferred_element_type=jnp.float32
        )
        back = back + jnp.dot(
            grad_v, weights[2 * width : 3 * width].T, preferred_element_type=jnp.float32
        )
        return ((grad_resid + back * factor).astype(jnp.bfloat16), grads)
    return (None, grads)


def masked(target, live):
    keep = (jnp.arange(target.shape[0]) < live)[:, None]
    return jnp.where(keep, target, jnp.zeros_like(target))


def on_device(inputs, out_grad, lengths, master, moment_first, moment_second):
    side = lax.axis_index("pipe")
    weights = master[0]
    width = weights.shape[1]
    weight_part = jnp.sum(weights * weights)
    mine = weights.astype(jnp.bfloat16)
    whole = lax.all_gather(mine, "dp", axis=0, tiled=True)
    partner = swapped(whole, "pipe", 0)
    leading = jnp.where(side == 0, whole, partner)
    trailing = jnp.where(side == 0, partner, whole)
    micro = inputs.shape[1]
    grads_lead = jnp.zeros((4 * width, width), jnp.float32)
    grads_trail = jnp.zeros((4 * width, width), jnp.float32)
    for index in range(micro):
        live = lengths[0, index]
        hidden, saved_lead = section_forward(leading, inputs[0, index], live)
        arrived, live_far = swapped((hidden, live), "pipe", 0)
        _, saved_trail = section_forward(trailing, arrived, live_far)
        target = masked(out_grad[0, index], live_far)
        back, grad_trail = section_backward(trailing, saved_trail, target, live_far, True)
        returned = swapped(back, "pipe", 0)
        _, grad_lead = section_backward(leading, saved_lead, returned, live, False)
        grads_lead = grads_lead + grad_lead
        grads_trail = grads_trail + grad_trail
    own_grads = jnp.where(side == 0, grads_lead, grads_trail)
    other_grads = jnp.where(side == 0, grads_trail, grads_lead)
    total = own_grads + swapped(other_grads.astype(jnp.bfloat16), "pipe", 0).astype(
        other_grads.dtype
    )
    grad_rows = lax.psum_scatter(total, "dp", scatter_dimension=0, tiled=True)
    new_first = 0.9 * moment_first[0] + 0.1 * grad_rows
    new_second = 0.999 * moment_second[0] + 0.001 * grad_rows * grad_rows
    corrected = new_first / (1.0 - 0.9**STEP)
    spread = new_second / (1.0 - 0.999**STEP)
    update = corrected / (jnp.sqrt(spread) + 1e-06) + 0.05 * weights
    update_part = jnp.sum(update * update)
    weight_sq, update_sq = lax.psum((weight_part, update_part), "dp")
    trust = jnp.sqrt(weight_sq) / (jnp.sqrt(update_sq) + 1e-06)
    new_master = weights - 0.05 * trust * update
    return (new_master[None], new_first[None], new_second[None])


def solution(mesh):
    in_specs = (
        P("pipe", ("groups", "dp"), None, None),
        P("pipe", ("groups", "dp"), None, None),
        P("pipe", ("groups", "dp")),
        P("pipe", ("groups", "dp"), None),
        P("pipe", ("groups", "dp"), None),
        P("pipe", ("groups", "dp"), None),
    )
    out_specs = (
        P("pipe", ("groups", "dp"), None),
        P("pipe", ("groups", "dp"), None),
        P("pipe", ("groups", "dp"), None),
    )
    return jax.shard_map(
        on_device, mesh=mesh, in_specs=in_specs, out_specs=out_specs, check_vma=False
    )
```

profile of v0, /device:TPU:0, one launch (start us, length us, event | category | flops | bytes accessed | tf_op | source)
XLA Modules:
  0.0 344.1 jit_solution(3730674439148973998)
XLA Ops:
  9.1 53.7 %all-gather.2.cloned.1.call-done = bf16[2048,512]{1,0:T(8,128)(2,1)} async-done(((bf16[256,512]{1,0:T(8,128)(2,1)}), bf16[2048,512]{1,0:T(8,128)(2,1)}) %all-gather.2.cloned.1.call-update) | async-done | bytes 2097168 | tf_op jit(solution)/shard_map/all_gather | solution.py:97
  68.4 1.9 broadcast_select_fusion
  82.1 2.0 fusion.46
  89.2 2.1 fusion.55
  93.1 2.1 fusion.54
  95.2 1.8 copy.69
  100.3 2.0 fusion.45
  105.7 2.2 fusion.212
  107.9 2.1 fusion.53
  110.1 1.8 copy.68
  118.6 2.1 fusion.56
  120.7 1.8 copy.72
  122.6 2.5 convolution_convert_fusion.5
  125.0 2.6 fusion.11
  128.6 1.8 fusion.61
  130.5 1.8 fusion.60
  133.6 2.1 fusion.48
  139.3 2.5 fusion.3
  153.4 12.5 %convolution_multiply_fusion.3 = f32[512,512]{1,0:T(8,128)} fusion(bf16[256,512]{1,0:T(8,128)(2,1)} %collective-permute-done.5, bf16[256,512]{0,1:T(8,128)(2,1)S(1)} %bitcast.287), kind=kOutput, calls=%fused_computation.57 | convolution fusion | flops 134479872 | bytes 1572864 | tf_op jit(solution)/shard_map/dot_general | solution.py:70
  165.9 2.3 convolution_multiply_fusion.2
  168.3 2.4 convolution_multiply_fusion.1
  177.7 2.4 convolution_convert_fusion.4
  180.0 3.3 fusion.15
  186.8 2.3 convert_reduce_fusion
  192.5 1.8 fusion.62
  202.7 2.6 copy.65
  205.3 7.0 %select_convert_fusion = bf16[2048,512]{1,0:T(8,128)(2,1)} fusion(pred[]{:T(512)S(6)} %eq.10, f32[512,512]{1,0:T(8,128)S(1)} %copy-done.9, f32[512,512]{1,0:T(8,128)} %convolution_multiply_fusion.1, f32[512,512]{1,0:T(8,128)} %convolution_multiply_fusion.2, f32[512,512]{1,0:T(8,128)} %convolution_multiply_fusion.3, f32[512,512]{1,0:T(8,128)S(1)} %copy-done.10, ...), kind=kLoop, calls=%fused_computation.3 | loop fusion | flops 16777216 | bytes 18874368 | tf_op jit(solution)/shard_map/convert_element_type | solution.py:117
  212.7 4.2 %collective-permute-done.7 = bf16[2048,512]{1,0:T(8,128)(2,1)} collective-permute-done((bf16[2048,512]{1,0:T(8,128)(2,1)}, bf16[2048,512]{1,0:T(8,128)(2,1)}, u32[]{:S(2)}, u32[]{:S(2)}) %collective-permute-start.7) | collective-permute-done | bytes 2097184 | tf_op jit(solution)/shard_map/ppermute | solution.py:11
  216.9 6.6 %convert_add_fusion = f32[2048,512]{1,0:T(8,128)} fusion(bf16[2048,512]{1,0:T(8,128)(2,1)} %collective-permute-done.7, pred[]{:T(512)S(6)} %eq.10, f32[512,512]{1,0:T(8,128)S(1)} %copy-done.9, f32[512,512]{1,0:T(8,128)} %convolution_multiply_fusion.1, f32[512,512]{1,0:T(8,128)S(1)} %copy-done.15, f32[512,512]{1,0:T(8,128)S(1)} %copy-done.14, ...), kind=kLoop, calls=%fused_computation.2 | loop fusion | flops 17825792 | bytes 23068672 | tf_op jit(solution)/shard_map/add | solution.py:117
  223.6 87.1 %reduce-scatter.2.cloned.1.call-done = f32[256,512]{1,0:T(8,128)} async-done(((f32[2048,512]{1,0:T(8,128)}), f32[256,512]{1,0:T(8,128)}) %reduce-scatter.2.cloned.1.call-update) | async-done | bytes 524304 | tf_op jit(solution)/shard_map/reduce_scatter | solution.py:120
  310.7 3.1 multiply_reduce_fusion
  313.8 20.9 %all-reduce = (f32[]{:T(128)}, f32[]{:T(128)}) all-reduce(f32[]{:T(128)} %get-tuple-element.35, f32[]{:T(128)} %get-tuple-element.9), channel_id=1, replica_groups=mesh['groups'=2,'dp'=8,'pipe'=2] {'dp'}, use_global_device_ids=true, to_apply=%region_1.2 | all-reduce | flops 2 | bytes 16 | tf_op jit(solution)/shard_map/psum | solution.py:127
  (262 shorter events, 79.7 us)
Async XLA Ops:
  7.2 55.6 %all-gather.2.cloned.1.call-start = ((), (), s32[]{:S(2)}) async-start(), calls=%async_computation.1 | async-start | bytes 2359296 | tf_op jit(solution)/shard_map/all_gather | solution.py:97
  9.0 301.7 %reduce-scatter.2.cloned.1.call-start = ((), (), s32[]{:S(2)}) async-start(), calls=%async_computation.2 | async-start | bytes 4718592 | tf_op jit(solution)/shard_map/reduce_scatter | solution.py:120
  62.7 5.7 %collective-permute-start.1 = (bf16[2048,512]{1,0:T(8,128)(2,1)}, bf16[2048,512]{1,0:T(8,128)(2,1)S(1)}, u32[]{:S(2)}, u32[]{:S(2)}) collective-permute-start(bf16[2048,512]{1,0:T(8,128)(2,1)} %all-gather.2.cloned.1.call-done), channel_id=1, source_target_pairs={{0,1},{1,0},{2,3},{3,2},{4,5},{5,4},{6,7},{7,6},{8,9},{9,8},{10,11... | collective-permute-start | bytes 6291464 | tf_op jit(solution)/shard_map/ppermute | solution.py:11
  64.0 3.1 collective-permute-start
  64.5 3.2 collective-permute-start.4
  65.9 9.4 %copy-start.65 = (pred[256]{0:T(512)(128)(4,1)}, pred[256]{0:T(512)(128)(4,1)S(1)}, u32[]{:S(2)}) copy-start(pred[256]{0:T(512)(128)(4,1)S(1)} %iota_compare_fusion.1) | copy-start | bytes 772
  70.3 7.2 %copy-start.25 = (bf16[2048,512]{1,0:T(8,128)(2,1)}, bf16[2048,512]{1,0:T(8,128)(2,1)S(1)}, u32[]{:S(2)}) copy-start(bf16[2048,512]{1,0:T(8,128)(2,1)S(1)} %get-tuple-element.28) | copy-start | bytes 6291460
  70.3 8.9 %copy-start.6 = (bf16[2048,512]{1,0:T(8,128)(2,1)}, bf16[2048,512]{1,0:T(8,128)(2,1)S(1)}, u32[]{:S(2)}) copy-start(bf16[2048,512]{1,0:T(8,128)(2,1)S(1)} %get-tuple-element.27) | copy-start | bytes 6291460
  70.7 6.5 %copy-start.38 = (bf16[512,256]{1,0:T(8,128)(2,1)}, bf16[512,256]{1,0:T(8,128)(2,1)S(1)}, u32[]{:S(2)}) copy-start(bf16[512,256]{1,0:T(8,128)(2,1)S(1)} %fusion.50) | copy-start | bytes 786436
  71.1 4.2 %copy-start.62 = (bf16[512,256]{1,0:T(8,128)(2,1)}, bf16[512,256]{1,0:T(8,128)(2,1)S(1)}, u32[]{:S(2)}) copy-start(bf16[512,256]{1,0:T(8,128)(2,1)S(1)} %fusion.51) | copy-start | bytes 786436
  71.4 3.8 %copy-start.60 = (bf16[512,256]{1,0:T(8,128)(2,1)}, bf16[512,256]{1,0:T(8,128)(2,1)S(1)}, u32[]{:S(2)}) copy-start(bf16[512,256]{1,0:T(8,128)(2,1)S(1)} %fusion.52) | copy-start | bytes 786436
  74.8 4.4 %collective-permute-start.2 = (bf16[256,512]{1,0:T(8,128)(2,1)S(1)}, bf16[256,512]{1,0:T(8,128)(2,1)S(1)}, u32[]{:S(2)}, u32[]{:S(2)}) collective-permute-start(bf16[256,512]{1,0:T(8,128)(2,1)S(1)} %multiply_convert_fusion.1), channel_id=1, source_target_pairs={{0,1},{1,0},{2,3},{3,2},{4,5},{5,4},{6,7},{7,6},{8,9},{9,8},{10,11... | collective-permute-start | bytes 786440 | tf_op jit(solution)/shard_map/ppermute | solution.py:11
  79.0 10.2 %collective-permute-start.5 = (bf16[256,512]{1,0:T(8,128)(2,1)}, bf16[256,512]{1,0:T(8,128)(2,1)}, u32[]{:S(2)}, u32[]{:S(2)}) collective-permute-start(bf16[256,512]{1,0:T(8,128)(2,1)} %multiply_convert_fusion), channel_id=1, source_target_pairs={{0,1},{1,0},{2,3},{3,2},{4,5},{5,4},{6,7},{7,6},{8,9},{9,8},{10,11... | collective-permute-start | bytes 786440 | tf_op jit(solution)/shard_map/ppermute | solution.py:11
  79.2 21.1 %copy-start.33 = (bf16[256,512]{1,0:T(8,128)(2,1)}, bf16[256,512]{1,0:T(8,128)(2,1)S(1)}, u32[]{:S(2)}) copy-start(bf16[256,512]{1,0:T(8,128)(2,1)S(1)} %collective-permute-done.2) | copy-start | bytes 786436
  111.9 4.0 %copy-start.35 = (bf16[1,2,256,512]{3,2,1,0:T(8,128)(2,1)S(1)}, bf16[1,2,256,512]{3,2,1,0:T(8,128)(2,1)}, u32[]{:S(2)}) copy-start(bf16[1,2,256,512]{3,2,1,0:T(8,128)(2,1)} %param.7) | copy-start | bytes 1572868
  111.9 4.0 %copy-start.36 = (f32[256,512]{1,0:T(8,128)S(1)}, f32[256,512]{1,0:T(8,128)}, u32[]{:S(2)}) copy-start(f32[256,512]{1,0:T(8,128)} %get-tuple-element.57) | copy-start | bytes 1572868
  130.5 3.2 copy-start.19
  148.0 22.7 %collective-permute-start.6 = (bf16[256,512]{1,0:T(8,128)(2,1)S(1)}, bf16[256,512]{1,0:T(8,128)(2,1)S(1)}, u32[]{:S(2)}, u32[]{:S(2)}) collective-permute-start(bf16[256,512]{1,0:T(8,128)(2,1)S(1)} %fusion.67), channel_id=1, source_target_pairs={{0,1},{1,0},{2,3},{3,2},{4,5},{5,4},{6,7},{7,6},{8,9},{9,8},{10,11... | collective-permute-start | bytes 786440 | tf_op jit(solution)/shard_map/ppermute | solution.py:11
  149.1 24.5 %collective-permute-start.3 = (bf16[256,512]{1,0:T(8,128)(2,1)S(1)}, bf16[256,512]{1,0:T(8,128)(2,1)S(1)}, u32[]{:S(2)}, u32[]{:S(2)}) collective-permute-start(bf16[256,512]{1,0:T(8,128)(2,1)S(1)} %fusion.66), channel_id=1, source_target_pairs={{0,1},{1,0},{2,3},{3,2},{4,5},{5,4},{6,7},{7,6},{8,9},{9,8},{10,11... | collective-permute-start | bytes 786440 | tf_op jit(solution)/shard_map/ppermute | solution.py:11
  153.4 17.3 %copy-start.24 = (f32[256,512]{1,0:T(8,128)S(1)}, f32[256,512]{1,0:T(8,128)}, u32[]{:S(2)}) copy-start(f32[256,512]{1,0:T(8,128)} %copy-done.23) | copy-start | bytes 1572868
  197.3 4.0 %copy-start.30 = (bf16[1,2,256,512]{3,2,1,0:T(8,128)(2,1)S(1)}, bf16[1,2,256,512]{3,2,1,0:T(8,128)(2,1)}, u32[]{:S(2)}) copy-start(bf16[1,2,256,512]{3,2,1,0:T(8,128)(2,1)} %param.6) | copy-start | bytes 1572868
  201.4 3.9 %copy-start.9 = (f32[512,512]{1,0:T(8,128)S(1)}, f32[512,512]{1,0:T(8,128)}, u32[]{:S(2)}) copy-start(f32[512,512]{1,0:T(8,128)} %convolution_multiply_fusion) | copy-start | bytes 3145732
  201.4 3.9 %copy-start.10 = (f32[512,512]{1,0:T(8,128)S(1)}, f32[512,512]{1,0:T(8,128)}, u32[]{:S(2)}) copy-start(f32[512,512]{1,0:T(8,128)} %convolution_multiply_fusion.4) | copy-start | bytes 3145732
  201.4 3.9 %copy-start.11 = (f32[512,512]{1,0:T(8,128)S(1)}, f32[512,512]{1,0:T(8,128)}, u32[]{:S(2)}) copy-start(f32[512,512]{1,0:T(8,128)} %convolution_multiply_fusion.7) | copy-start | bytes 3145732
  205.3 11.6 %copy-start.12 = (f32[512,512]{1,0:T(8,128)S(1)}, f32[512,512]{1,0:T(8,128)}, u32[]{:S(2)}) copy-start(f32[512,512]{1,0:T(8,128)} %convolution_multiply_fusion.6) | copy-start | bytes 3145732
  205.3 11.6 %copy-start.13 = (f32[512,512]{1,0:T(8,128)S(1)}, f32[512,512]{1,0:T(8,128)}, u32[]{:S(2)}) copy-start(f32[512,512]{1,0:T(8,128)} %convolution_multiply_fusion.5) | copy-start | bytes 3145732
  205.3 11.6 %copy-start.14 = (f32[512,512]{1,0:T(8,128)S(1)}, f32[512,512]{1,0:T(8,128)}, u32[]{:S(2)}) copy-start(f32[512,512]{1,0:T(8,128)} %convolution_multiply_fusion.3) | copy-start | bytes 3145732
  205.3 11.6 %copy-start.15 = (f32[512,512]{1,0:T(8,128)S(1)}, f32[512,512]{1,0:T(8,128)}, u32[]{:S(2)}) copy-start(f32[512,512]{1,0:T(8,128)} %convolution_multiply_fusion.2) | copy-start | bytes 3145732
  212.3 4.6 %collective-permute-start.7 = (bf16[2048,512]{1,0:T(8,128)(2,1)}, bf16[2048,512]{1,0:T(8,128)(2,1)}, u32[]{:S(2)}, u32[]{:S(2)}) collective-permute-start(bf16[2048,512]{1,0:T(8,128)(2,1)} %select_convert_fusion), channel_id=1, source_target_pairs={{0,1},{1,0},{2,3},{3,2},{4,5},{5,4},{6,7},{7,6},{8,9},{9,8},{10,11... | collective-permute-start | bytes 6291464 | tf_op jit(solution)/shard_map/ppermute | solution.py:11
  223.5 87.2 %copy-start.27 = (f32[1,256,512]{2,1,0:T(8,128)S(1)}, f32[1,256,512]{2,1,0:T(8,128)}, u32[]{:S(2)}) copy-start(f32[1,256,512]{2,1,0:T(8,128)} %param.9) | copy-start | bytes 1572868
  223.5 87.2 %copy-start.54 = (f32[1,256,512]{2,1,0:T(8,128)S(1)}, f32[1,256,512]{2,1,0:T(8,128)}, u32[]{:S(2)}) copy-start(f32[1,256,512]{2,1,0:T(8,128)} %param.11) | copy-start | bytes 1572868
  223.5 87.2 %copy-start.55 = (f32[1,256,512]{2,1,0:T(8,128)S(1)}, f32[1,256,512]{2,1,0:T(8,128)}, u32[]{:S(2)}) copy-start(f32[1,256,512]{2,1,0:T(8,128)} %param.10) | copy-start | bytes 1572868
  (45 other events, 72.4 us)
Sparse Core Ops, SparseCore 0:
  10.7 51.9 all-gather.1
  223.7 86.9 reduce-scatter.1
where the time goes:
time: 349 us; the launch traced here: 344 us
  waiting for transfers between devices  146 us (42%)
  matrix products  96.4 us (28%)
  other arithmetic  37.2 us (11%)
  local copies, waits for them, and re-layouts  24.5 us (7%)
  blocking collectives  20.9 us (6%)
  between operations  16.8 us (5%)
    reduce_scatter x1, waiting for transfers between devices, on_device(): grad_rows = lax.psum_scatter(total, 'dp', scatter_dimension=0, tiled=True)  87.1 us
    all_gather x1, waiting for transfers between devices, on_device(): whole = lax.all_gather(mine, 'dp', axis=0, tiled=True)  53.7 us
    dot_general x12, matrix products, attention(): jnp.einsum('hqk,khd->qhd', probs, v_heads, preferred_element_type=jnp.flo...  20.9 us
    psum x1, blocking collectives, on_device(): weight_sq, update_sq = lax.psum((weight_part, update_part), 'dp')  20.9 us
    dot_general x4, matrix products, section_backward(): jnp.dot(inputs.T, grad_q, preferred_element_type=jnp.float32) * factor  16.6 us
    dot_general x12, matrix products, attention(): jnp.einsum('qhd,khd->hqk', q_heads, k_heads, preferred_element_type=jnp.f...  15.2 us
    convert_element_type x1, other arithmetic, on_device(): other_grads.astype(jnp.bfloat16)  7.03 us
  transfers between devices with their start and end apart: 10, of which 4 were waited for; matrix products, arithmetic and copies ran while one was open for 12% of the time, Pallas kernels for 0%

commit v1 on v0

v1 whole, which is shorter than its diff:
```python
import functools

import jax
import jax.numpy as jnp
from jax import lax
from jax.experimental import pallas as pl
from jax.experimental.pallas import tpu as pltpu
from jax.sharding import PartitionSpec as P

HEAD = 64
PAIR = 128
STEP = 10
F32 = jnp.float32
BF16 = jnp.bfloat16


def dot(a, b):
    return lax.dot_general(a, b, (((1,), (0,)), ((), ())), preferred_element_type=F32)


def dot_nt(a, b):
    return lax.dot_general(a, b, (((1,), (1,)), ((), ())), preferred_element_type=F32)


def half_masks(length):
    lane = lax.broadcasted_iota(jnp.int32, (length, PAIR), 1)
    return lane < HEAD, lane >= HEAD


def forward(sec, micro, length, width, scal, x_ref, w, q, k, v, v_t, p, mixed_t, xhat, rstd, h_ref):
    factor = width ** (-0.5)
    pairs = width // PAIR
    x2 = x_ref[...]
    q[sec] = (dot(x2, w[sec, 0:width]) * factor).astype(BF16) * jnp.asarray(HEAD ** (-0.5), BF16)
    k[sec] = (dot(x2, w[sec, width : 2 * width]) * factor).astype(BF16)
    values = (dot(x2, w[sec, 2 * width : 3 * width]) * factor).astype(BF16)
    v[sec] = values
    v_t[...] = values.T

    for seq in range(micro):
        live = scal[1 + seq]
        rows = slice(seq * length, (seq + 1) * length)

        def body(pair, carry):
            lanes = pl.ds(pl.multiple_of(pair * PAIR, PAIR), PAIR)
            kp = k[sec, rows, lanes]
            qp = q[sec, rows, lanes]
            masks = half_masks(length)
            keep = lax.broadcasted_iota(jnp.int32, (length, length), 0) < live
            parts = []
            for half in range(2):
                qm = jnp.where(masks[half], qp, jnp.zeros_like(qp))
                score = jnp.where(keep, dot_nt(kp, qm), -1e30)
                expo = jnp.exp(score - jnp.max(score, axis=0, keepdims=True))
                prob = expo * (1.0 / jnp.sum(expo, axis=0, keepdims=True))
                p[sec, seq * 2 * pairs + pair * 2 + half] = prob
                vh = v_t[pl.ds(pl.multiple_of(pair * PAIR + half * HEAD, HEAD), HEAD), rows]
                parts.append(dot(vh, prob.astype(BF16)))
            mixed_t[sec, lanes, rows] = jnp.concatenate(parts, axis=0).astype(BF16)
            return carry

        lax.fori_loop(0, pairs, body, 0)
    mixed = mixed_t[sec].T
    resid = x2.astype(F32) + dot(mixed, w[sec, 3 * width : 4 * width]) * factor
    centre = resid - jnp.mean(resid, axis=-1, keepdims=True)
    scale = lax.rsqrt(jnp.mean(centre * centre, axis=-1, keepdims=True) + 1e-05)
    normed = centre * scale
    xhat[sec] = normed
    rstd[sec] = jnp.broadcast_to(scale, rstd.shape[1:])
    if h_ref is not None:
        h_ref[...] = normed.astype(BF16)


def backward(sec, micro, length, width, grad, x_ref, w, q, k, v, k_t, p, mixed_t, xhat, rstd, dm, dq_t, dk, dv, emit, want):
    factor = width ** (-0.5)
    pairs = width // PAIR
    normed = xhat[sec]
    dres = rstd[sec][:, :1] * (
        grad
        - jnp.mean(grad, axis=-1, keepdims=True)
        - normed * jnp.mean(grad * normed, axis=-1, keepdims=True)
    )
    da = dres.astype(BF16)
    emit(sec, 3, dot(mixed_t[sec], da) * factor)
    dm[...] = (dot_nt(da, w[sec, 3 * width : 4 * width]) * factor).astype(BF16)
    k_t[...] = k[sec].T
    for seq in range(micro):
        rows = slice(seq * length, (seq + 1) * length)

        def body(pair, carry):
            lanes = pl.ds(pl.multiple_of(pair * PAIR, PAIR), PAIR)
            vp = v[sec, rows, lanes]
            qp = q[sec, rows, lanes]
            gp = dm[rows, lanes]
            masks = half_masks(length)
            parts = []
            gv = jnp.zeros((length, PAIR), F32)
            gk = jnp.zeros((length, PAIR), F32)
            for half in range(2):
                gm = jnp.where(masks[half], gp, jnp.zeros_like(gp))
                qm = jnp.where(masks[half], qp, jnp.zeros_like(qp))
                dp = dot_nt(vp, gm).astype(BF16).astype(F32)
                prob = p[sec, seq * 2 * pairs + pair * 2 + half]
                gv += dot(prob.astype(BF16), gm)
                total = jnp.sum(prob * dp, axis=0, keepdims=True)
                ds = (prob * (dp - total)).astype(BF16)
                gk += dot(ds, qm)
                kh = k_t[pl.ds(pl.multiple_of(pair * PAIR + half * HEAD, HEAD), HEAD), rows]
                parts.append(dot(kh, ds))
            dv[rows, lanes] = gv.astype(BF16)
            dk[rows, lanes] = gk.astype(BF16)
            dq_t[lanes, rows] = (jnp.concatenate(parts, axis=0) * HEAD ** (-0.5)).astype(BF16)
            return carry

        lax.fori_loop(0, pairs, body, 0)
    dq = dq_t[...].T
    x_t = x_ref[...].T
    emit(sec, 0, dot(x_t, dq) * factor)
    emit(sec, 1, dot(x_t, dk[...]) * factor)
    emit(sec, 2, dot(x_t, dv[...]) * factor)
    if not want:
        return None
    back = dot_nt(dq, w[sec, 0:width])
    back += dot_nt(dk[...], w[sec, width : 2 * width])
    back += dot_nt(dv[...], w[sec, 2 * width : 3 * width])
    return (dres + back * factor).astype(BF16)


def layers(micro, length, width, rows, places, scal, x_ref, g_ref, *refs):
    count = len(places)
    own_w, other_w = refs[:count], refs[count : 2 * count]
    own_g, other_g = refs[2 * count : 2 * count + 2]
    w, hid, q, k, v, tr, p, mixed_t, xhat, rstd, dm, dq_t, dk, dv = refs[2 * count + 2 :]
    side = scal[0]
    base = 1 + micro

    for group, sec in ((own_w, side), (other_w, 1 - side)):
        for (slot, shift), ref in zip(places, group):
            if rows:
                at = pl.multiple_of(scal[base + slot] * rows + shift, 16)
            else:
                at = 0
            w[sec, pl.ds(at, ref.shape[0])] = ref[...]

    def emit(sec, part, value):
        for b in range(width // rows if rows else 1):
            size = rows if rows else width
            if rows:
                index = part * (width // rows) + b
                at = pl.multiple_of(scal[base + 4 * width // rows + index] * rows, 16)
            else:
                at = part * width
            block = value[b * size : (b + 1) * size]

            @pl.when(side == sec)
            def _():
                own_g[pl.ds(at, size)] = block

            @pl.when(side != sec)
            def _():
                other_g[pl.ds(at, size)] = block.astype(BF16)

    dims = (micro, length, width)
    forward(0, *dims, scal, x_ref, w, q, k, v, tr, p, mixed_t, xhat, rstd, hid)
    forward(1, *dims, scal, hid, w, q, k, v, tr, p, mixed_t, xhat, rstd, None)
    pieces = []
    for seq in range(micro):
        pos = lax.broadcasted_iota(jnp.int32, (length, width), 0)
        piece = g_ref[seq * length : (seq + 1) * length].astype(F32)
        pieces.append(jnp.where(pos < scal[1 + seq], piece, 0.0))
    grad = jnp.concatenate(pieces, axis=0)
    back = backward(1, *dims, grad, hid, w, q, k, v, tr, p, mixed_t, xhat, rstd, dm, dq_t, dk, dv, emit, True)
    backward(0, *dims, back.astype(F32), x_ref, w, q, k, v, tr, p, mixed_t, xhat, rstd, dm, dq_t, dk, dv, emit, False)


def run_layers(scal, x, target, own, other, places, rows, micro, length, width):
    tokens = micro * length
    heads = width // HEAD
    vmem = pl.BlockSpec(memory_space=pltpu.VMEM)
    return pl.pallas_call(
        functools.partial(layers, micro, length, width, rows, places),
        out_shape=(
            jax.ShapeDtypeStruct((4 * width, width), F32),
            jax.ShapeDtypeStruct((4 * width, width), BF16),
        ),
        in_specs=[pl.BlockSpec(memory_space=pltpu.SMEM)] + [vmem] * (2 + 2 * len(own)),
        out_specs=(vmem, vmem),
        scratch_shapes=[
            pltpu.VMEM((2, 4 * width, width), BF16),
            pltpu.VMEM((tokens, width), BF16),
            pltpu.VMEM((2, tokens, width), BF16),
            pltpu.VMEM((2, tokens, width), BF16),
            pltpu.VMEM((2, tokens, width), BF16),
            pltpu.VMEM((width, tokens), BF16),
            pltpu.VMEM((2, micro * heads, length, length), F32),
            pltpu.VMEM((2, width, tokens), BF16),
            pltpu.VMEM((2, tokens, width), F32),
            pltpu.VMEM((2, tokens, PAIR), F32),
            pltpu.VMEM((tokens, width), BF16),
            pltpu.VMEM((width, tokens), BF16),
            pltpu.VMEM((tokens, width), BF16),
            pltpu.VMEM((tokens, width), BF16),
        ],
        compiler_params=pltpu.CompilerParams(vmem_limit_bytes=52 * 1024 * 1024),
    )(scal, x, target, *own, *other)


def swapped(value):
    return lax.ppermute(value, "pipe", [(0, 1), (1, 0)])


def ring_order(count):
    return list(range(0, count, 2)) + list(range(count - 1, 0, -2))


def on_device(inputs, out_grad, lengths, master, moment_first, moment_second):
    side = lax.axis_index("pipe")
    place = lax.axis_index("dp")
    count = lax.axis_size("dp")
    weights = master[0]
    rows, width = weights.shape
    micro, length = inputs.shape[1:3]
    ringed = count == 8 and rows % 32 == 0 and width % rows == 0
    ring = ring_order(count)
    onward = [(ring[i], ring[(i + 1) % count]) for i in range(count)]
    backward_way = [(b, a) for a, b in onward]

    def ahead(value):
        return lax.ppermute(value, "dp", onward)

    def behind(value):
        return lax.ppermute(value, "dp", backward_way)

    mine = weights.astype(BF16)
    target = swapped(out_grad[0]).reshape(micro * length, width)
    x = inputs[0].reshape(micro * length, width)
    scalars = [side[None], lengths[0]]
    half = rows // 2
    if ringed:
        own = [mine]
        places = [(0, 0)]
        fore, aft = mine, mine
        for step in range(1, count // 2):
            fore, aft = ahead(fore), behind(aft)
            own += [fore, aft]
            places += [(count - step, 0), (step, 0)]
        own += [ahead(fore[:half]), behind(aft[half:])]
        places += [(count // 2, 0), (count // 2, half)]
        position = jnp.asarray([ring.index(i) for i in range(count)], jnp.int32)
        me = position[place]
        scalars.append(jnp.asarray(ring, jnp.int32)[(me + jnp.arange(count, dtype=jnp.int32)) % count])
        scalars.append((position - me + count) % count)
    else:
        own = [lax.all_gather(mine, "dp", axis=0, tiled=True)]
        places = [(0, 0)]
    other = [swapped(value) for value in own]
    scal = jnp.concatenate([s.astype(jnp.int32) for s in scalars])
    own_g, other_g = run_layers(
        scal, x, target, own, other, places, rows if ringed else 0, micro, length, width
    )
    total = own_g + swapped(other_g).astype(F32)
    if ringed:
        mid = count // 2

        def block(index):
            return total[index * rows : (index + 1) * rows]

        fore = ahead(block(mid)[:half].astype(BF16)).astype(F32)
        aft = behind(block(mid)[half:].astype(BF16)).astype(F32)
        up, down = block(mid - 1), block(mid + 1)
        fore = jnp.concatenate([up[:half] + fore, up[half:]], axis=0)
        aft = jnp.concatenate([down[:half], down[half:] + aft], axis=0)
        for step in range(mid - 1, 0, -1):
            fore = ahead(fore.astype(BF16)).astype(F32)
            aft = behind(aft.astype(BF16)).astype(F32)
            if step > 1:
                fore = fore + block(step - 1)
                aft = aft + block(count - step + 1)
        grad_rows = block(0) + fore + aft
    else:
        grad_rows = lax.psum_scatter(total, "dp", scatter_dimension=0, tiled=True)
    new_first = 0.9 * moment_first[0] + 0.1 * grad_rows
    new_second = 0.999 * moment_second[0] + 0.001 * grad_rows * grad_rows
    corrected = new_first / (1.0 - 0.9**STEP)
    spread = new_second / (1.0 - 0.999**STEP)
    update = corrected / (jnp.sqrt(spread) + 1e-06) + 0.05 * weights
    squares = jnp.stack([jnp.sum(weights * weights), jnp.sum(update * update)])
    if ringed:
        hop = 1
        while hop < count:
            squares = squares + lax.ppermute(squares, "dp", [(i, i ^ hop) for i in range(count)])
            hop *= 2
    else:
        squares = lax.psum(squares, "dp")
    trust = jnp.sqrt(squares[0]) / (jnp.sqrt(squares[1]) + 1e-06)
    new_master = weights - 0.05 * trust * update
    return (new_master[None], new_first[None], new_second[None])


def solution(mesh):
    rows = P("pipe", ("groups", "dp"), None)
    in_specs = (
        P("pipe", ("groups", "dp"), None, None),
        P("pipe", ("groups", "dp"), None, None),
        P("pipe", ("groups", "dp")),
        rows,
        rows,
        rows,
    )
    return jax.shard_map(
        on_device, mesh=mesh, in_specs=in_specs, out_specs=(rows, rows, rows), check_vma=False
    )
```

time: 349 us -> 137 us (0.39); the launches traced: 344 us -> 137 us
  matrix products: 96.4 us -> 0 us
  waiting for transfers between devices: 146 us -> 52.6 us
  Pallas kernels: 0 us -> 39.8 us
  other arithmetic: 37.2 us -> 14.2 us
  starting transfers between devices: 2.11 us -> 24.4 us
  local copies, waits for them, and re-layouts: 24.5 us -> 3.27 us
  blocking collectives: 20.9 us -> 0 us
  between operations: 16.8 us -> 2.28 us
    dot_general x66 -> x0, matrix products: 96.4 us -> none  [the longest x12 20.9 us: attention(): jnp.einsum('hqk,khd->qhd', probs, v_heads, preferred_element_type=jnp.flo...]
    reduce_scatter x1 -> x0, waiting for transfers between devices: 87.1 us -> none  [on_device(): grad_rows = lax.psum_scatter(total, 'dp', scatter_dimension=0, tiled=True)]
    all_gather x1 -> x0, waiting for transfers between devices: 53.7 us -> none  [on_device(): whole = lax.all_gather(mine, 'dp', axis=0, tiled=True)]
    ppermute x8 -> x30, waiting for transfers between devices: 5.44 us -> 52.6 us  [the longest x8 23.5 us: behind(): return lax.ppermute(value, 'dp', backward_way)]
    pallas_call x0 -> x1, Pallas kernels: none -> 39.8 us  [run_layers(): pl.pallas_call(functools.partial(layers, micro, length, width, rows, plac...]
    ppermute x8 -> x30, starting transfers between devices: 2.03 us -> 24.4 us  [the longest x8 13.9 us: behind(): return lax.ppermute(value, 'dp', backward_way)]
    psum x1 -> x0, blocking collectives: 20.9 us -> none  [on_device(): weight_sq, update_sq = lax.psum((weight_part, update_part), 'dp')]
    convert_element_type x10 -> x0, local copies, waits for them, and re-layouts: 15.8 us -> none  [the longest x4 5.77 us: section_backward(): grad_mixed = (jnp.dot(grad_attn, weights[3 * width:].T, preferred_element...]
  transfers between devices with their start and end apart: 10 -> 30, of which waited for: 4 -> 18; matrix products, arithmetic and copies ran while one was open for 12% -> 4% of each run, Pallas kernels for 0% -> 0%
where the time goes in v1:
time: 137 us
  waiting for transfers between devices  52.6 us (38%)
  Pallas kernels  39.8 us (29%)
  starting transfers between devices  24.4 us (18%)
  other arithmetic  14.2 us (10%)
  local copies, waits for them, and re-layouts  3.27 us (2%)
  between operations  2.28 us (2%)
    pallas_call x1, Pallas kernels, run_layers(): pl.pallas_call(functools.partial(layers, micro, length, width, rows, plac...  39.8 us
    ppermute x8, waiting for transfers between devices, behind(): return lax.ppermute(value, 'dp', backward_way)  23.5 us
    ppermute x8, waiting for transfers between devices, ahead(): return lax.ppermute(value, 'dp', onward)  18.6 us
    ppermute x8, starting transfers between devices, behind(): return lax.ppermute(value, 'dp', backward_way)  13.9 us
    ppermute x3, waiting for transfers between devices, on_device(): lax.ppermute(squares, 'dp', [(i, i ^ hop) for i in range(count)])  6.45 us
    ppermute x3, starting transfers between devices, on_device(): lax.ppermute(squares, 'dp', [(i, i ^ hop) for i in range(count)])  5.09 us
    ppermute x11, waiting for transfers between devices, swapped(): return lax.ppermute(value, 'pipe', [(0, 1), (1, 0)])  4.02 us
    ppermute x8, starting transfers between devices, ahead(): return lax.ppermute(value, 'dp', onward)  3.7 us
  transfers between devices with their start and end apart: 30, of which 18 were waited for; matrix products, arithmetic and copies ran while one was open for 4% of the time, Pallas kernels for 0%

profile of v1, /device:TPU:0, one launch (start us, length us, event | category | flops | bytes accessed | tf_op | source)
XLA Modules:
  0.0 136.6 jit_solution(15269391466482294965)
XLA Ops:
  1.7 3.0 %collective-permute-start.2 = (bf16[256,512]{1,0:T(8,128)(2,1)S(1)}, bf16[256,512]{1,0:T(8,128)(2,1)S(1)}, u32[]{:S(2)}, u32[]{:S(2)}) collective-permute-start(bf16[256,512]{1,0:T(8,128)(2,1)S(1)} %bitcast_convert_fusion.refs_0_), channel_id=1, source_target_pairs={{4,0},{8,4},{12,8},{14,12},{10,14},{6,10},{2,6},{0,2},{5,1},{9,5},... | collective-permute-start | bytes 786440 | tf_op jit(solution)/shard_map/ppermute | solution.py:232
  4.9 6.2 %collective-permute-done.2.refs_2_ = bf16[256,512]{1,0:T(8,128)(2,1)S(1)} collective-permute-done((bf16[256,512]{1,0:T(8,128)(2,1)S(1)}, bf16[256,512]{1,0:T(8,128)(2,1)S(1)}, u32[]{:S(2)}, u32[]{:S(2)}) %collective-permute-start.2) | collective-permute-done | bytes 262176 | tf_op jit(solution)/shard_map/ppermute | solution.py:232
  11.1 1.7 %collective-permute-start.4 = (bf16[256,512]{1,0:T(8,128)(2,1)S(1)}, bf16[256,512]{1,0:T(8,128)(2,1)S(1)}, u32[]{:S(2)}, u32[]{:S(2)}) collective-permute-start(bf16[256,512]{1,0:T(8,128)(2,1)S(1)} %collective-permute-done.2.refs_2_), channel_id=1, source_target_pairs={{4,0},{8,4},{12,8},{14,12},{10,14},{6,10},{2,6},{0,2},{5,1},{9,5},... | collective-permute-start | bytes 786440 | tf_op jit(solution)/shard_map/ppermute | solution.py:232
  13.1 5.5 %collective-permute-done.4.refs_4_ = bf16[256,512]{1,0:T(8,128)(2,1)S(1)} collective-permute-done((bf16[256,512]{1,0:T(8,128)(2,1)S(1)}, bf16[256,512]{1,0:T(8,128)(2,1)S(1)}, u32[]{:S(2)}, u32[]{:S(2)}) %collective-permute-start.4) | collective-permute-done | bytes 262176 | tf_op jit(solution)/shard_map/ppermute | solution.py:232
  18.6 1.3 collective-permute-start.6
  21.1 4.0 %collective-permute-done.6.refs_6_ = bf16[256,512]{1,0:T(8,128)(2,1)S(1)} collective-permute-done((bf16[256,512]{1,0:T(8,128)(2,1)S(1)}, bf16[256,512]{1,0:T(8,128)(2,1)S(1)}, u32[]{:S(2)}, u32[]{:S(2)}) %collective-permute-start.6) | collective-permute-done | bytes 262176 | tf_op jit(solution)/shard_map/ppermute | solution.py:232
  25.2 3.5 %collective-permute-done.5.refs_5_ = bf16[256,512]{1,0:T(8,128)(2,1)S(1)} collective-permute-done((bf16[256,512]{1,0:T(8,128)(2,1)S(1)}, bf16[256,512]{1,0:T(8,128)(2,1)S(1)}, u32[]{:S(2)}, u32[]{:S(2)}) %collective-permute-start.5) | collective-permute-done | bytes 262176 | tf_op jit(solution)/shard_map/ppermute | solution.py:229
  30.0 1.6 %collective-permute-start.8 = (bf16[128,512]{1,0:T(8,128)(2,1)S(1)}, bf16[128,512]{1,0:T(8,128)(2,1)S(1)}, u32[]{:S(2)}, u32[]{:S(2)}) collective-permute-start(bf16[128,512]{1,0:T(8,128)(2,1)S(1)} %slice.77), channel_id=1, source_target_pairs={{4,0},{8,4},{12,8},{14,12},{10,14},{6,10},{2,6},{0,2},{5,1},{9,5},... | collective-permute-start | bytes 393224 | tf_op jit(solution)/shard_map/ppermute | solution.py:232
  32.1 1.3 and_select_fusion
  35.9 1.3 collective-permute-done.7.refs_7_
  37.2 1.3 gather_fusion
  39.4 39.8 %shard_map.103 = (f32[2048,512]{1,0:T(8,128)}, bf16[2048,512]{1,0:T(8,128)(2,1)}) custom-call(s32[19]{0:T(128)S(1)} %pad_add_fusion.scal, bf16[512,512]{1,0:T(8,128)(2,1)} %bitcast.43, bf16[512,512]{1,0:T(8,128)(2,1)} %bitcast.44, bf16[256,512]{1,0:T(8,128)(2,1)S(1)} %bitcast_convert_fusion.refs_0_, bf16[256,512]{1,0:T(8,128)(2,1)S(1)} %collective-permute-done.1.refs_1_, ...), custom_call_target="tpu_custom_call" | custom-call | tf_op jit(solution)/shard_map/pallas_call | solution.py:180
  79.7 4.0 %collective-permute-done.18 = bf16[2048,512]{1,0:T(8,128)(2,1)S(1)} collective-permute-done((bf16[2048,512]{1,0:T(8,128)(2,1)}, bf16[2048,512]{1,0:T(8,128)(2,1)S(1)}, u32[]{:S(2)}, u32[]{:S(2)}) %collective-permute-start.18) | collective-permute-done | bytes 2097184 | tf_op jit(solution)/shard_map/ppermute | solution.py:209
  83.7 2.9 %fusion.17 = (bf16[2048,512]{1,0:T(8,128)(2,1)S(1)}, f32[2048,512]{1,0:T(8,128)S(1)}) fusion(f32[2048,512]{1,0:T(8,128)} %get-tuple-element.5, bf16[2048,512]{1,0:T(8,128)(2,1)S(1)} %collective-permute-done.18), kind=kLoop, calls=%fused_computation.44 | loop fusion | flops 3145728 | bytes 12582912 | tf_op jit(solution)/shard_map/convert.7
  87.2 1.6 %collective-permute-start.23 = (bf16[128,512]{1,0:T(8,128)(2,1)S(1)}, bf16[128,512]{1,0:T(8,128)(2,1)S(1)}, u32[]{:S(2)}, u32[]{:S(2)}) collective-permute-start(bf16[128,512]{1,0:T(8,128)(2,1)S(1)} %get-tuple-element.20), channel_id=1, source_target_pairs={{4,0},{8,4},{12,8},{14,12},{10,14},{6,10},{2,6},{0,2},{5,1},{9,5},... | collective-permute-start | bytes 393224 | tf_op jit(solution)/shard_map/ppermute | solution.py:232
  88.8 3.7 %collective-permute-done.19 = bf16[128,512]{1,0:T(8,128)(2,1)S(1)} collective-permute-done((bf16[128,512]{1,0:T(8,128)(2,1)S(1)}, bf16[128,512]{1,0:T(8,128)(2,1)S(1)}, u32[]{:S(2)}, u32[]{:S(2)}) %collective-permute-start.19) | collective-permute-done | bytes 131104 | tf_op jit(solution)/shard_map/ppermute | solution.py:229
  92.8 1.6 %collective-permute-start.24 = (bf16[256,512]{1,0:T(8,128)(2,1)S(1)}, bf16[256,512]{1,0:T(8,128)(2,1)S(1)}, u32[]{:S(2)}, u32[]{:S(2)}) collective-permute-start(bf16[256,512]{1,0:T(8,128)(2,1)S(1)} %pad_maximum_fusion.1), channel_id=1, source_target_pairs={{4,0},{8,4},{12,8},{14,12},{10,14},{6,10},{2,6},{0,2},{5,1},{9,5},... | collective-permute-start | bytes 786440 | tf_op jit(solution)/shard_map/ppermute | solution.py:232
  95.0 5.5 %collective-permute-done.24 = bf16[256,512]{1,0:T(8,128)(2,1)S(1)} collective-permute-done((bf16[256,512]{1,0:T(8,128)(2,1)S(1)}, bf16[256,512]{1,0:T(8,128)(2,1)S(1)}, u32[]{:S(2)}, u32[]{:S(2)}) %collective-permute-start.24) | collective-permute-done | bytes 262176 | tf_op jit(solution)/shard_map/ppermute | solution.py:232
  100.5 1.4 %collective-permute-done.20 = bf16[256,512]{1,0:T(8,128)(2,1)S(1)} collective-permute-done((bf16[256,512]{1,0:T(8,128)(2,1)S(1)}, bf16[256,512]{1,0:T(8,128)(2,1)S(1)}, u32[]{:S(2)}, u32[]{:S(2)}) %collective-permute-start.20) | collective-permute-done | bytes 262176 | tf_op jit(solution)/shard_map/ppermute | solution.py:229
  102.5 1.6 %collective-permute-start.25 = (bf16[256,512]{1,0:T(8,128)(2,1)S(1)}, bf16[256,512]{1,0:T(8,128)(2,1)S(1)}, u32[]{:S(2)}, u32[]{:S(2)}) collective-permute-start(bf16[256,512]{1,0:T(8,128)(2,1)S(1)} %get-tuple-element.16), channel_id=1, source_target_pairs={{4,0},{8,4},{12,8},{14,12},{10,14},{6,10},{2,6},{0,2},{5,1},{9,5},... | collective-permute-start | bytes 786440 | tf_op jit(solution)/shard_map/ppermute | solution.py:232
  104.1 4.4 %collective-permute-done.21 = bf16[256,512]{1,0:T(8,128)(2,1)S(1)} collective-permute-done((bf16[256,512]{1,0:T(8,128)(2,1)S(1)}, bf16[256,512]{1,0:T(8,128)(2,1)S(1)}, u32[]{:S(2)}, u32[]{:S(2)}) %collective-permute-start.21) | collective-permute-done | bytes 262176 | tf_op jit(solution)/shard_map/ppermute | solution.py:229
  109.6 1.6 %collective-permute-start.26 = (bf16[256,512]{1,0:T(8,128)(2,1)S(1)}, bf16[256,512]{1,0:T(8,128)(2,1)S(1)}, u32[]{:S(2)}, u32[]{:S(2)}) collective-permute-start(bf16[256,512]{1,0:T(8,128)(2,1)S(1)} %get-tuple-element.14), channel_id=1, source_target_pairs={{4,0},{8,4},{12,8},{14,12},{10,14},{6,10},{2,6},{0,2},{5,1},{9,5},... | collective-permute-start | bytes 786440 | tf_op jit(solution)/shard_map/ppermute | solution.py:232
  111.2 4.3 %collective-permute-done.22 = bf16[256,512]{1,0:T(8,128)(2,1)S(1)} collective-permute-done((bf16[256,512]{1,0:T(8,128)(2,1)S(1)}, bf16[256,512]{1,0:T(8,128)(2,1)S(1)}, u32[]{:S(2)}, u32[]{:S(2)}) %collective-permute-start.22) | collective-permute-done | bytes 262176 | tf_op jit(solution)/shard_map/ppermute | solution.py:229
  116.0 2.1 %multiply_reduce_fusion = (f32[]{:T(128)}, f32[256,512]{1,0:T(8,128)S(1)}, f32[1,256,512]{2,1,0:T(8,128)}, f32[1,256,512]{2,1,0:T(8,128)}, f32[]{:T(128)}) fusion(f32[1,256,512]{2,1,0:T(8,128)S(1)} %copy-done, f32[1,256,512]{2,1,0:T(8,128)S(1)} %copy-done.3, bf16[256,512]{1,0:T(8,128)(2,1)S(1)} %collective-permute-done.26, ...), kind=kLoop, calls=%fused_computation.22 | loop fusion | flops 2752510 | bytes 4194312 | tf_op jit(solution)/shard_map/reduce_sum | solution.py:287
  118.1 1.4 pad_maximum_fusion.2
  119.4 1.6 %collective-permute-start.27 = (f32[2]{0:T(128)S(1)}, f32[2]{0:T(128)S(1)}, u32[]{:S(2)}, u32[]{:S(2)}) collective-permute-start(f32[2]{0:T(128)S(1)} %pad_maximum_fusion.2), channel_id=1, source_target_pairs={{0,2},{2,0},{4,6},{6,4},{8,10},{10,8},{12,14},{14,12},{1,3},{3,1},... | collective-permute-start | bytes 32 | tf_op jit(solution)/shard_map/ppermute | solution.py:291
  121.0 2.0 %collective-permute-done.27 = f32[2]{0:T(128)S(1)} collective-permute-done((f32[2]{0:T(128)S(1)}, f32[2]{0:T(128)S(1)}, u32[]{:S(2)}, u32[]{:S(2)}) %collective-permute-start.27) | collective-permute-done | bytes 40 | tf_op jit(solution)/shard_map/ppermute | solution.py:291
  123.0 1.4 fusion.20
  125.6 2.3 %collective-permute-done.28 = f32[2]{0:T(128)S(1)} collective-permute-done((f32[2]{0:T(128)S(1)}, f32[2]{0:T(128)S(1)}, u32[]{:S(2)}, u32[]{:S(2)}) %collective-permute-start.28) | collective-permute-done | bytes 40 | tf_op jit(solution)/shard_map/ppermute | solution.py:291
  127.9 1.4 fusion.21
  129.2 2.3 %collective-permute-start.29 = (f32[2]{0:T(128)S(1)}, f32[2]{0:T(128)S(1)}, u32[]{:S(2)}, u32[]{:S(2)}) collective-permute-start(f32[2]{0:T(128)S(1)} %fusion.21), channel_id=1, source_target_pairs={{0,8},{2,10},{4,12},{6,14},{8,0},{10,2},{12,4},{14,6},{1,9},{3,11}... | collective-permute-start | bytes 32 | tf_op jit(solution)/shard_map/ppermute | solution.py:291
  131.5 2.2 %collective-permute-done.29 = f32[2]{0:T(128)S(1)} collective-permute-done((f32[2]{0:T(128)S(1)}, f32[2]{0:T(128)S(1)}, u32[]{:S(2)}, u32[]{:S(2)}) %collective-permute-start.29) | collective-permute-done | bytes 40 | tf_op jit(solution)/shard_map/ppermute | solution.py:291
  (70 shorter events, 14.7 us)
Async XLA Ops:
  1.7 9.4 %collective-permute-start.2 = (bf16[256,512]{1,0:T(8,128)(2,1)S(1)}, bf16[256,512]{1,0:T(8,128)(2,1)S(1)}, u32[]{:S(2)}, u32[]{:S(2)}) collective-permute-start(bf16[256,512]{1,0:T(8,128)(2,1)S(1)} %bitcast_convert_fusion.refs_0_), channel_id=1, source_target_pairs={{4,0},{8,4},{12,8},{14,12},{10,14},{6,10},{2,6},{0,2},{5,1},{9,5},... | collective-permute-start | bytes 786440 | tf_op jit(solution)/shard_map/ppermute | solution.py:232
  4.7 8.0 %collective-permute-start.1 = (bf16[256,512]{1,0:T(8,128)(2,1)S(1)}, bf16[256,512]{1,0:T(8,128)(2,1)S(1)}, u32[]{:S(2)}, u32[]{:S(2)}) collective-permute-start(bf16[256,512]{1,0:T(8,128)(2,1)S(1)} %bitcast_convert_fusion.refs_0_), channel_id=1, source_target_pairs={{0,4},{4,8},{8,12},{12,14},{14,10},{10,6},{6,2},{2,0},{1,5},{5,9},... | collective-permute-start | bytes 786440 | tf_op jit(solution)/shard_map/ppermute | solution.py:229
  11.1 7.5 %collective-permute-start.4 = (bf16[256,512]{1,0:T(8,128)(2,1)S(1)}, bf16[256,512]{1,0:T(8,128)(2,1)S(1)}, u32[]{:S(2)}, u32[]{:S(2)}) collective-permute-start(bf16[256,512]{1,0:T(8,128)(2,1)S(1)} %collective-permute-done.2.refs_2_), channel_id=1, source_target_pairs={{4,0},{8,4},{12,8},{14,12},{10,14},{6,10},{2,6},{0,2},{5,1},{9,5},... | collective-permute-start | bytes 786440 | tf_op jit(solution)/shard_map/ppermute | solution.py:232
  12.7 7.2 %collective-permute-start.3 = (bf16[256,512]{1,0:T(8,128)(2,1)S(1)}, bf16[256,512]{1,0:T(8,128)(2,1)S(1)}, u32[]{:S(2)}, u32[]{:S(2)}) collective-permute-start(bf16[256,512]{1,0:T(8,128)(2,1)S(1)} %collective-permute-done.1.refs_1_), channel_id=1, source_target_pairs={{0,4},{4,8},{8,12},{12,14},{14,10},{10,6},{6,2},{2,0},{1,5},{5,9},... | collective-permute-start | bytes 786440 | tf_op jit(solution)/shard_map/ppermute | solution.py:229
  18.6 6.6 %collective-permute-start.6 = (bf16[256,512]{1,0:T(8,128)(2,1)S(1)}, bf16[256,512]{1,0:T(8,128)(2,1)S(1)}, u32[]{:S(2)}, u32[]{:S(2)}) collective-permute-start(bf16[256,512]{1,0:T(8,128)(2,1)S(1)} %collective-permute-done.4.refs_4_), channel_id=1, source_target_pairs={{4,0},{8,4},{12,8},{14,12},{10,14},{6,10},{2,6},{0,2},{5,1},{9,5},... | collective-permute-start | bytes 786440 | tf_op jit(solution)/shard_map/ppermute | solution.py:232
  19.9 13.6 %collective-permute-start = (bf16[2,256,512]{2,1,0:T(8,128)(2,1)}, bf16[2,256,512]{2,1,0:T(8,128)(2,1)S(1)}, u32[]{:S(2)}, u32[]{:S(2)}) collective-permute-start(bf16[2,256,512]{2,1,0:T(8,128)(2,1)} %bitcast.46), channel_id=1, source_target_pairs={{0,1},{1,0},{2,3},{3,2},{4,5},{5,4},{6,7},{7,6},{8,9},{9,8},{10,11... | collective-permute-start | bytes 1572872 | tf_op jit(solution)/shard_map/ppermute | solution.py:209
  19.9 8.7 %collective-permute-start.5 = (bf16[256,512]{1,0:T(8,128)(2,1)S(1)}, bf16[256,512]{1,0:T(8,128)(2,1)S(1)}, u32[]{:S(2)}, u32[]{:S(2)}) collective-permute-start(bf16[256,512]{1,0:T(8,128)(2,1)S(1)} %collective-permute-done.3.refs_3_), channel_id=1, source_target_pairs={{0,4},{4,8},{8,12},{12,14},{14,10},{10,6},{6,2},{2,0},{1,5},{5,9},... | collective-permute-start | bytes 786440 | tf_op jit(solution)/shard_map/ppermute | solution.py:229
  20.6 9.4 %collective-permute-start.9 = (bf16[256,512]{1,0:T(8,128)(2,1)S(1)}, bf16[256,512]{1,0:T(8,128)(2,1)S(1)}, u32[]{:S(2)}, u32[]{:S(2)}) collective-permute-start(bf16[256,512]{1,0:T(8,128)(2,1)S(1)} %bitcast_convert_fusion.refs_0_), channel_id=1, source_target_pairs={{0,1},{1,0},{2,3},{3,2},{4,5},{5,4},{6,7},{7,6},{8,9},{9,8},{10,11... | collective-permute-start | bytes 786440 | tf_op jit(solution)/shard_map/ppermute | solution.py:209
  20.8 10.8 %collective-permute-start.11 = (bf16[256,512]{1,0:T(8,128)(2,1)S(1)}, bf16[256,512]{1,0:T(8,128)(2,1)S(1)}, u32[]{:S(2)}, u32[]{:S(2)}) collective-permute-start(bf16[256,512]{1,0:T(8,128)(2,1)S(1)} %collective-permute-done.2.refs_2_), channel_id=1, source_target_pairs={{0,1},{1,0},{2,3},{3,2},{4,5},{5,4},{6,7},{7,6},{8,9},{9,8},{10,11... | collective-permute-start | bytes 786440 | tf_op jit(solution)/shard_map/ppermute | solution.py:209
  25.2 8.2 %collective-permute-start.10 = (bf16[256,512]{1,0:T(8,128)(2,1)S(1)}, bf16[256,512]{1,0:T(8,128)(2,1)S(1)}, u32[]{:S(2)}, u32[]{:S(2)}) collective-permute-start(bf16[256,512]{1,0:T(8,128)(2,1)S(1)} %collective-permute-done.1.refs_1_), channel_id=1, source_target_pairs={{0,1},{1,0},{2,3},{3,2},{4,5},{5,4},{6,7},{7,6},{8,9},{9,8},{10,11... | collective-permute-start | bytes 786440 | tf_op jit(solution)/shard_map/ppermute | solution.py:209
  28.6 5.3 %collective-permute-start.13 = (bf16[256,512]{1,0:T(8,128)(2,1)S(1)}, bf16[256,512]{1,0:T(8,128)(2,1)}, u32[]{:S(2)}, u32[]{:S(2)}) collective-permute-start(bf16[256,512]{1,0:T(8,128)(2,1)S(1)} %collective-permute-done.4.refs_4_), channel_id=1, source_target_pairs={{0,1},{1,0},{2,3},{3,2},{4,5},{5,4},{6,7},{7,6},{8,9},{9,8},{10,11... | collective-permute-start | bytes 786440 | tf_op jit(solution)/shard_map/ppermute | solution.py:209
  30.0 5.9 %collective-permute-start.8 = (bf16[128,512]{1,0:T(8,128)(2,1)S(1)}, bf16[128,512]{1,0:T(8,128)(2,1)S(1)}, u32[]{:S(2)}, u32[]{:S(2)}) collective-permute-start(bf16[128,512]{1,0:T(8,128)(2,1)S(1)} %slice.77), channel_id=1, source_target_pairs={{4,0},{8,4},{12,8},{14,12},{10,14},{6,10},{2,6},{0,2},{5,1},{9,5},... | collective-permute-start | bytes 393224 | tf_op jit(solution)/shard_map/ppermute | solution.py:232
  31.6 5.6 %collective-permute-start.7 = (bf16[128,512]{1,0:T(8,128)(2,1)S(1)}, bf16[128,512]{1,0:T(8,128)(2,1)S(1)}, u32[]{:S(2)}, u32[]{:S(2)}) collective-permute-start(bf16[128,512]{1,0:T(8,128)(2,1)S(1)} %slice.76), channel_id=1, source_target_pairs={{0,4},{4,8},{8,12},{12,14},{14,10},{10,6},{6,2},{2,0},{1,5},{5,9},... | collective-permute-start | bytes 393224 | tf_op jit(solution)/shard_map/ppermute | solution.py:229
  33.4 5.9 %collective-permute-start.12 = (bf16[256,512]{1,0:T(8,128)(2,1)S(1)}, bf16[256,512]{1,0:T(8,128)(2,1)}, u32[]{:S(2)}, u32[]{:S(2)}) collective-permute-start(bf16[256,512]{1,0:T(8,128)(2,1)S(1)} %collective-permute-done.3.refs_3_), channel_id=1, source_target_pairs={{0,1},{1,0},{2,3},{3,2},{4,5},{5,4},{6,7},{7,6},{8,9},{9,8},{10,11... | collective-permute-start | bytes 786440 | tf_op jit(solution)/shard_map/ppermute | solution.py:209
  33.5 5.8 %collective-permute-start.15 = (bf16[256,512]{1,0:T(8,128)(2,1)S(1)}, bf16[256,512]{1,0:T(8,128)(2,1)}, u32[]{:S(2)}, u32[]{:S(2)}) collective-permute-start(bf16[256,512]{1,0:T(8,128)(2,1)S(1)} %collective-permute-done.6.refs_6_), channel_id=1, source_target_pairs={{0,1},{1,0},{2,3},{3,2},{4,5},{5,4},{6,7},{7,6},{8,9},{9,8},{10,11... | collective-permute-start | bytes 786440 | tf_op jit(solution)/shard_map/ppermute | solution.py:209
  34.0 5.3 %collective-permute-start.14 = (bf16[256,512]{1,0:T(8,128)(2,1)S(1)}, bf16[256,512]{1,0:T(8,128)(2,1)}, u32[]{:S(2)}, u32[]{:S(2)}) collective-permute-start(bf16[256,512]{1,0:T(8,128)(2,1)S(1)} %collective-permute-done.5.refs_5_), channel_id=1, source_target_pairs={{0,1},{1,0},{2,3},{3,2},{4,5},{5,4},{6,7},{7,6},{8,9},{9,8},{10,11... | collective-permute-start | bytes 786440 | tf_op jit(solution)/shard_map/ppermute | solution.py:209
  35.9 3.4 %collective-permute-start.17 = (bf16[128,512]{1,0:T(8,128)(2,1)S(1)}, bf16[128,512]{1,0:T(8,128)(2,1)S(1)}, u32[]{:S(2)}, u32[]{:S(2)}) collective-permute-start(bf16[128,512]{1,0:T(8,128)(2,1)S(1)} %collective-permute-done.8.refs_8_), channel_id=1, source_target_pairs={{0,1},{1,0},{2,3},{3,2},{4,5},{5,4},{6,7},{7,6},{8,9},{9,8},{10,11... | collective-permute-start | bytes 393224 | tf_op jit(solution)/shard_map/ppermute | solution.py:209
  37.2 2.1 %collective-permute-start.16 = (bf16[128,512]{1,0:T(8,128)(2,1)S(1)}, bf16[128,512]{1,0:T(8,128)(2,1)S(1)}, u32[]{:S(2)}, u32[]{:S(2)}) collective-permute-start(bf16[128,512]{1,0:T(8,128)(2,1)S(1)} %collective-permute-done.7.refs_7_), channel_id=1, source_target_pairs={{0,1},{1,0},{2,3},{3,2},{4,5},{5,4},{6,7},{7,6},{8,9},{9,8},{10,11... | collective-permute-start | bytes 393224 | tf_op jit(solution)/shard_map/ppermute | solution.py:209
  79.2 4.5 %collective-permute-start.18 = (bf16[2048,512]{1,0:T(8,128)(2,1)}, bf16[2048,512]{1,0:T(8,128)(2,1)S(1)}, u32[]{:S(2)}, u32[]{:S(2)}) collective-permute-start(bf16[2048,512]{1,0:T(8,128)(2,1)} %get-tuple-element.6), channel_id=1, source_target_pairs={{0,1},{1,0},{2,3},{3,2},{4,5},{5,4},{6,7},{7,6},{8,9},{9,8},{10,11... | collective-permute-start | bytes 6291464 | tf_op jit(solution)/shard_map/ppermute | solution.py:209
  86.6 29.4 %copy-start = (f32[1,256,512]{2,1,0:T(8,128)S(1)}, f32[1,256,512]{2,1,0:T(8,128)}, u32[]{:S(2)}) copy-start(f32[1,256,512]{2,1,0:T(8,128)} %param.11) | copy-start | bytes 1572868
  86.6 29.3 %copy-start.3 = (f32[1,256,512]{2,1,0:T(8,128)S(1)}, f32[1,256,512]{2,1,0:T(8,128)}, u32[]{:S(2)}) copy-start(f32[1,256,512]{2,1,0:T(8,128)} %param.13) | copy-start | bytes 1572868
  86.7 5.8 %collective-permute-start.19 = (bf16[128,512]{1,0:T(8,128)(2,1)S(1)}, bf16[128,512]{1,0:T(8,128)(2,1)S(1)}, u32[]{:S(2)}, u32[]{:S(2)}) collective-permute-start(bf16[128,512]{1,0:T(8,128)(2,1)S(1)} %get-tuple-element.19), channel_id=1, source_target_pairs={{0,4},{4,8},{8,12},{12,14},{14,10},{10,6},{6,2},{2,0},{1,5},{5,9},... | collective-permute-start | bytes 393224 | tf_op jit(solution)/shard_map/ppermute | solution.py:229
  87.2 5.5 %collective-permute-start.23 = (bf16[128,512]{1,0:T(8,128)(2,1)S(1)}, bf16[128,512]{1,0:T(8,128)(2,1)S(1)}, u32[]{:S(2)}, u32[]{:S(2)}) collective-permute-start(bf16[128,512]{1,0:T(8,128)(2,1)S(1)} %get-tuple-element.20), channel_id=1, source_target_pairs={{4,0},{8,4},{12,8},{14,12},{10,14},{6,10},{2,6},{0,2},{5,1},{9,5},... | collective-permute-start | bytes 393224 | tf_op jit(solution)/shard_map/ppermute | solution.py:232
  92.8 7.7 %collective-permute-start.24 = (bf16[256,512]{1,0:T(8,128)(2,1)S(1)}, bf16[256,512]{1,0:T(8,128)(2,1)S(1)}, u32[]{:S(2)}, u32[]{:S(2)}) collective-permute-start(bf16[256,512]{1,0:T(8,128)(2,1)S(1)} %pad_maximum_fusion.1), channel_id=1, source_target_pairs={{4,0},{8,4},{12,8},{14,12},{10,14},{6,10},{2,6},{0,2},{5,1},{9,5},... | collective-permute-start | bytes 786440 | tf_op jit(solution)/shard_map/ppermute | solution.py:232
  94.5 7.4 %collective-permute-start.20 = (bf16[256,512]{1,0:T(8,128)(2,1)S(1)}, bf16[256,512]{1,0:T(8,128)(2,1)S(1)}, u32[]{:S(2)}, u32[]{:S(2)}) collective-permute-start(bf16[256,512]{1,0:T(8,128)(2,1)S(1)} %pad_maximum_fusion), channel_id=1, source_target_pairs={{0,4},{4,8},{8,12},{12,14},{14,10},{10,6},{6,2},{2,0},{1,5},{5,9},... | collective-permute-start | bytes 786440 | tf_op jit(solution)/shard_map/ppermute | solution.py:229
  102.0 6.4 %collective-permute-start.21 = (bf16[256,512]{1,0:T(8,128)(2,1)S(1)}, bf16[256,512]{1,0:T(8,128)(2,1)S(1)}, u32[]{:S(2)}, u32[]{:S(2)}) collective-permute-start(bf16[256,512]{1,0:T(8,128)(2,1)S(1)} %get-tuple-element.15), channel_id=1, source_target_pairs={{0,4},{4,8},{8,12},{12,14},{14,10},{10,6},{6,2},{2,0},{1,5},{5,9},... | collective-permute-start | bytes 786440 | tf_op jit(solution)/shard_map/ppermute | solution.py:229
  102.5 6.4 %collective-permute-start.25 = (bf16[256,512]{1,0:T(8,128)(2,1)S(1)}, bf16[256,512]{1,0:T(8,128)(2,1)S(1)}, u32[]{:S(2)}, u32[]{:S(2)}) collective-permute-start(bf16[256,512]{1,0:T(8,128)(2,1)S(1)} %get-tuple-element.16), channel_id=1, source_target_pairs={{4,0},{8,4},{12,8},{14,12},{10,14},{6,10},{2,6},{0,2},{5,1},{9,5},... | collective-permute-start | bytes 786440 | tf_op jit(solution)/shard_map/ppermute | solution.py:232
  109.1 6.4 %collective-permute-start.22 = (bf16[256,512]{1,0:T(8,128)(2,1)S(1)}, bf16[256,512]{1,0:T(8,128)(2,1)S(1)}, u32[]{:S(2)}, u32[]{:S(2)}) collective-permute-start(bf16[256,512]{1,0:T(8,128)(2,1)S(1)} %get-tuple-element.13), channel_id=1, source_target_pairs={{0,4},{4,8},{8,12},{12,14},{14,10},{10,6},{6,2},{2,0},{1,5},{5,9},... | collective-permute-start | bytes 786440 | tf_op jit(solution)/shard_map/ppermute | solution.py:229
  109.6 6.4 %collective-permute-start.26 = (bf16[256,512]{1,0:T(8,128)(2,1)S(1)}, bf16[256,512]{1,0:T(8,128)(2,1)S(1)}, u32[]{:S(2)}, u32[]{:S(2)}) collective-permute-start(bf16[256,512]{1,0:T(8,128)(2,1)S(1)} %get-tuple-element.14), channel_id=1, source_target_pairs={{4,0},{8,4},{12,8},{14,12},{10,14},{6,10},{2,6},{0,2},{5,1},{9,5},... | collective-permute-start | bytes 786440 | tf_op jit(solution)/shard_map/ppermute | solution.py:232
  119.4 3.5 %collective-permute-start.27 = (f32[2]{0:T(128)S(1)}, f32[2]{0:T(128)S(1)}, u32[]{:S(2)}, u32[]{:S(2)}) collective-permute-start(f32[2]{0:T(128)S(1)} %pad_maximum_fusion.2), channel_id=1, source_target_pairs={{0,2},{2,0},{4,6},{6,4},{8,10},{10,8},{12,14},{14,12},{1,3},{3,1},... | collective-permute-start | bytes 32 | tf_op jit(solution)/shard_map/ppermute | solution.py:291
  124.3 3.5 %collective-permute-start.28 = (f32[2]{0:T(128)S(1)}, f32[2]{0:T(128)S(1)}, u32[]{:S(2)}, u32[]{:S(2)}) collective-permute-start(f32[2]{0:T(128)S(1)} %fusion.20), channel_id=1, source_target_pairs={{0,4},{2,6},{4,0},{6,2},{8,12},{10,14},{12,8},{14,10},{1,5},{3,7},... | collective-permute-start | bytes 32 | tf_op jit(solution)/shard_map/ppermute | solution.py:291
  129.2 4.4 %collective-permute-start.29 = (f32[2]{0:T(128)S(1)}, f32[2]{0:T(128)S(1)}, u32[]{:S(2)}, u32[]{:S(2)}) collective-permute-start(f32[2]{0:T(128)S(1)} %fusion.21), channel_id=1, source_target_pairs={{0,8},{2,10},{4,12},{6,14},{8,0},{10,2},{12,4},{14,6},{1,9},{3,11}... | collective-permute-start | bytes 32 | tf_op jit(solution)/shard_map/ppermute | solution.py:291
  (7 other events, 78.5 us)

commit v2 on v1

v2 whole, which is shorter than its diff:
```python
import functools

import jax
import jax.numpy as jnp
from jax import lax
from jax.experimental import pallas as pl
from jax.experimental.pallas import tpu as pltpu
from jax.sharding import PartitionSpec as P

HEAD = 64
PAIR = 128
AHEAD = 2
CUTS = 4
STEP = 10
F32 = jnp.float32
BF16 = jnp.bfloat16


def dot(a, b):
    return lax.dot_general(a, b, (((1,), (0,)), ((), ())), preferred_element_type=F32)


def dot_nt(a, b):
    return lax.dot_general(a, b, (((1,), (1,)), ((), ())), preferred_element_type=F32)


def padded(part, half):
    zero = jnp.zeros_like(part)
    return jnp.concatenate([part, zero] if half == 0 else [zero, part], axis=0)


def forward(sec, micro, length, width, live_ref, x_ref, w, q_t, k, v, tr, p, mixed_t, xhat, rstd, h_ref):
    factor = width ** (-0.5)
    x2 = x_ref[...]
    queries = (dot(x2, w[sec, 0:width]) * factor).astype(BF16) * jnp.asarray(HEAD ** (-0.5), BF16)
    q_t[sec] = queries.T
    k[sec] = (dot(x2, w[sec, width : 2 * width]) * factor).astype(BF16)
    values = (dot(x2, w[sec, 2 * width : 3 * width]) * factor).astype(BF16)
    v[sec] = values
    tr[...] = values.T
    lane = lax.broadcasted_iota(jnp.int32, (length, PAIR), 1)
    spot = lax.broadcasted_iota(jnp.int32, (length, PAIR), 0)
    first = (lax.broadcasted_iota(jnp.int32, (HEAD, length), 0) == 0).astype(F32).astype(BF16)
    heads = width // HEAD
    bias = [jnp.where(spot < live_ref[0, seq], 0.0, -1e30).astype(BF16) for seq in range(micro)]

    def scores(index):
        seq, head = divmod(index, heads)
        rows = slice(seq * length, (seq + 1) * length)
        kp = k[sec, rows, (head // 2) * PAIR : (head // 2 + 1) * PAIR]
        k_ext = jnp.where(lane == (0 if head % 2 else HEAD), bias[seq], kp)
        qh = q_t[sec, head * HEAD : (head + 1) * HEAD, rows]
        return dot(k_ext, jnp.concatenate([first, qh] if head % 2 else [qh, first], axis=0))

    waiting = [scores(index) for index in range(AHEAD)]
    for index in range(micro * heads):
        if index + AHEAD < micro * heads:
            waiting.append(scores(index + AHEAD))
        score = waiting.pop(0)
        seq, head = divmod(index, heads)
        rows = slice(seq * length, (seq + 1) * length)
        feats = slice(head * HEAD, (head + 1) * HEAD)
        expo = jnp.exp(score - jnp.max(score, axis=0, keepdims=True))
        prob = expo * (1.0 / jnp.sum(expo, axis=0, keepdims=True))
        p[sec, index] = prob
        mixed_t[sec, feats, rows] = dot(tr[feats, rows], prob.astype(BF16))
    mixed = mixed_t[sec].astype(BF16).T
    resid = x2.astype(F32) + dot(mixed, w[sec, 3 * width : 4 * width]) * factor
    centre = resid - jnp.mean(resid, axis=-1, keepdims=True)
    scale = lax.rsqrt(jnp.mean(centre * centre, axis=-1, keepdims=True) + 1e-05)
    normed = centre * scale
    xhat[sec] = normed
    rstd[sec] = jnp.broadcast_to(scale, rstd.shape[1:])
    if h_ref is not None:
        h_ref[...] = normed.astype(BF16)


def backward(sec, micro, length, width, grad, x_ref, w, q_t, k, v, tr, p, mixed_t, xhat, rstd, g_t, dq_t, dk, dv, emit, send):
    factor = width ** (-0.5)
    normed = xhat[sec]
    dres = rstd[sec][:, :1] * (
        grad
        - jnp.mean(grad, axis=-1, keepdims=True)
        - normed * jnp.mean(grad * normed, axis=-1, keepdims=True)
    )
    da = dres.astype(BF16)
    emit(sec, 3, dot(mixed_t[sec].astype(BF16), da) * factor)
    g_t[...] = (dot_nt(w[sec, 3 * width : 4 * width], da) * factor).astype(BF16)
    tr[...] = k[sec].T
    heads = width // HEAD

    def spread(index):
        seq, head = divmod(index, heads)
        rows = slice(seq * length, (seq + 1) * length)
        g_ext = padded(g_t[head * HEAD : (head + 1) * HEAD, rows], head % 2)
        return g_ext, dot(v[sec, rows, (head // 2) * PAIR : (head // 2 + 1) * PAIR], g_ext)

    waiting = [spread(index) for index in range(AHEAD)]
    for index in range(micro * heads):
        if index + AHEAD < micro * heads:
            waiting.append(spread(index + AHEAD))
        g_ext, dp = waiting.pop(0)
        seq, head = divmod(index, heads)
        rows = slice(seq * length, (seq + 1) * length)
        feats = slice(head * HEAD, (head + 1) * HEAD)
        q_ext = padded(q_t[sec, feats, rows], head % 2)
        delta = jnp.sum(mixed_t[sec, feats, rows] * g_t[feats, rows].astype(F32), axis=0, keepdims=True)
        prob = p[sec, index]
        ds = (prob * (dp - delta)).astype(BF16)
        gv_part = dot_nt(prob.astype(BF16), g_ext)
        gk_part = dot_nt(ds, q_ext)
        dq_t[feats, rows] = (dot(tr[feats, rows], ds) * HEAD ** (-0.5)).astype(BF16)
        if head % 2 == 0:
            gv, gk = gv_part, gk_part
        else:
            lanes = slice((head // 2) * PAIR, (head // 2 + 1) * PAIR)
            dv[rows, lanes] = (gv + gv_part).astype(BF16)
            dk[rows, lanes] = (gk + gk_part).astype(BF16)
    if send is not None:
        send(sec, (3,))
    dq = dq_t[...].T
    x_t = x_ref[...].T
    emit(sec, 0, dot(x_t, dq) * factor)
    emit(sec, 1, dot(x_t, dk[...]) * factor)
    if send is not None:
        send(sec, (0, 1))
    emit(sec, 2, dot(x_t, dv[...]) * factor)
    if send is not None:
        return None
    back = dot_nt(dq, w[sec, 0:width])
    back += dot_nt(dk[...], w[sec, width : 2 * width])
    back += dot_nt(dv[...], w[sec, 2 * width : 3 * width])
    return (dres + back * factor).astype(BF16)


def ring_spot(index, count):
    return jnp.where(index % 2 == 0, index // 2, count - 1 - index // 2)


def ring_index(spot, count):
    return jnp.where(spot < count // 2, 2 * spot, 2 * (count - 1 - spot) + 1)


def layers(micro, length, width, rows, count, places, live_in, x_in, g_in, *refs):
    size = len(places)
    own_w, other_w = refs[:size], refs[size : 2 * size]
    own_out, near_out, rest_out = refs[2 * size : 2 * size + 3]
    (live_ref, x_ref, g_ref, w, own_g, other_g, hid, q_t, k, v, tr, p, mixed_t, xhat, rstd, g_t, dq_t, dk, dv, in_sem, out_sem, act_sem) = refs[2 * size + 3 :]
    side = lax.axis_index("pipe")
    me = ring_spot(lax.axis_index("dp"), count)
    block = rows if rows else 4 * width
    live_copy = pltpu.make_async_copy(live_in, live_ref, act_sem.at[2])
    x_copy = pltpu.make_async_copy(x_in, x_ref, act_sem.at[0])
    g_copy = pltpu.make_async_copy(g_in, g_ref, act_sem.at[1])
    live_copy.start()
    x_copy.start()
    for sec, group in ((side, own_w), (1 - side, other_w)):
        for i, ((slot, shift), ref) in enumerate(zip(places, group)):
            at = pl.multiple_of(ring_index((me + slot) % count, count) * rows + shift, 16) if rows else 0
            pltpu.make_async_copy(ref, w.at[sec, pl.ds(at, ref.shape[0])], in_sem.at[sec, i]).start()
    tall = rows if rows else width
    g_copy.start()

    def turn_of(index):
        if not rows:
            return index
        return (ring_spot(jnp.int32(index), count) - me + count + count // 2) % count

    def emit(sec, part, value):
        for b in range(width // tall):
            here = pl.ds(pl.multiple_of(turn_of(part * (width // tall) + b) * tall, 16), tall)
            piece = value[b * tall : (b + 1) * tall]
            own_g[sec, here] = piece
            other_g[sec, here] = piece.astype(BF16)

    def send(sec, parts):
        for index in [part * (width // tall) + b for part in parts for b in range(width // tall)]:
            turn = turn_of(index)
            here = pl.ds(pl.multiple_of(turn * tall, 16), tall)

            @pl.when(side == sec)
            def _():
                pltpu.make_async_copy(own_g.at[sec, here], own_out.at[here], out_sem.at[0, index]).start()

            @pl.when((side != sec) & (turn == 0))
            def _():
                pltpu.make_async_copy(other_g.at[sec, here], near_out, out_sem.at[1, index]).start()

            @pl.when((side != sec) & (turn != 0))
            def _():
                there = pl.ds(pl.multiple_of((turn - 1) * tall, 16), tall)
                pltpu.make_async_copy(other_g.at[sec, here], rest_out.at[there], out_sem.at[1, index]).start()

    def sent():
        for index in range(4 * width // tall):
            here = pl.ds(0, tall)
            pltpu.make_async_copy(own_g.at[0, here], own_out.at[here], out_sem.at[0, index]).wait()
            pltpu.make_async_copy(other_g.at[0, here], near_out, out_sem.at[1, index]).wait()

    dims = (micro, length, width)

    def arrived(sec):
        for i, ref in enumerate(own_w):
            pltpu.make_async_copy(ref, w.at[sec, pl.ds(0, ref.shape[0])], in_sem.at[sec, i]).wait()

    live_copy.wait()
    x_copy.wait()
    arrived(0)
    forward(0, *dims, live_ref, x_ref, w, q_t, k, v, tr, p, mixed_t, xhat, rstd, hid)
    arrived(1)
    forward(1, *dims, live_ref, hid, w, q_t, k, v, tr, p, mixed_t, xhat, rstd, None)
    g_copy.wait()
    pieces = []
    for seq in range(micro):
        pos = lax.broadcasted_iota(jnp.int32, (length, width), 0)
        piece = g_ref[seq * length : (seq + 1) * length].astype(F32)
        pieces.append(jnp.where(pos < live_ref[0, seq], piece, 0.0))
    grad = jnp.concatenate(pieces, axis=0)
    back = backward(1, *dims, grad, hid, w, q_t, k, v, tr, p, mixed_t, xhat, rstd, g_t, dq_t, dk, dv, emit, None)
    send(1, (0, 1, 2, 3))
    backward(0, *dims, back.astype(F32), x_ref, w, q_t, k, v, tr, p, mixed_t, xhat, rstd, g_t, dq_t, dk, dv, emit, send)
    send(0, (2,))
    sent()


def run_layers(live, x, target, own, other, places, rows, count, micro, length, width):
    tokens = micro * length
    heads = width // HEAD
    hbm = pl.BlockSpec(memory_space=pl.ANY)
    far = pl.BlockSpec(memory_space=pltpu.HBM)
    first = rows if rows else width
    return pl.pallas_call(
        functools.partial(layers, micro, length, width, rows, count, places),
        out_shape=(
            jax.ShapeDtypeStruct((4 * width, width), F32),
            jax.ShapeDtypeStruct((first, width), BF16),
            jax.ShapeDtypeStruct((4 * width - first, width), BF16),
        ),
        in_specs=[far, far, hbm] + [hbm] * (2 * len(own)),
        out_specs=(hbm, hbm, hbm),
        scratch_shapes=[
            pltpu.SMEM((1, micro), jnp.int32),
            pltpu.VMEM((tokens, width), BF16),
            pltpu.VMEM((tokens, width), BF16),
            pltpu.VMEM((2, 4 * width, width), BF16),
            pltpu.VMEM((2, 4 * width, width), F32),
            pltpu.VMEM((2, 4 * width, width), BF16),
            pltpu.VMEM((tokens, width), BF16),
            pltpu.VMEM((2, width, tokens), BF16),
            pltpu.VMEM((2, tokens, width), BF16),
            pltpu.VMEM((2, tokens, width), BF16),
            pltpu.VMEM((width, tokens), BF16),
            pltpu.VMEM((2, micro * heads, length, length), F32),
            pltpu.VMEM((2, width, tokens), F32),
            pltpu.VMEM((2, tokens, width), F32),
            pltpu.VMEM((2, tokens, PAIR), F32),
            pltpu.VMEM((width, tokens), BF16),
            pltpu.VMEM((width, tokens), BF16),
            pltpu.VMEM((tokens, width), BF16),
            pltpu.VMEM((tokens, width), BF16),
            pltpu.SemaphoreType.DMA((2, len(own))),
            pltpu.SemaphoreType.DMA((2, 4 * width // first)),
            pltpu.SemaphoreType.DMA((3,)),
        ],
        compiler_params=pltpu.CompilerParams(vmem_limit_bytes=40 * 1024 * 1024),
    )(live, x, target, *own, *other)


def swapped(value):
    return lax.ppermute(value, "pipe", [(0, 1), (1, 0)])


def ring_order(count):
    return list(range(0, count, 2)) + list(range(count - 1, 0, -2))


def on_device(inputs, out_grad, lengths, master, moment_first, moment_second):
    count = lax.axis_size("dp")
    weights = master[0]
    rows, width = weights.shape
    micro, length = inputs.shape[1:3]
    ringed = count == 8 and rows % 32 == 0 and width % rows == 0
    ring = ring_order(count)
    onward = [(ring[i], ring[(i + 1) % count]) for i in range(count)]
    backward_way = [(b, a) for a, b in onward]

    def ahead(value):
        return lax.ppermute(value, "dp", onward)

    def behind(value):
        return lax.ppermute(value, "dp", backward_way)

    mine = weights.astype(BF16)
    target = out_grad[0].reshape(micro * length, width)
    x = inputs[0].reshape(micro * length, width)
    half = rows // 2
    if ringed:
        own = [mine]
        places = [(0, 0)]
        fore, aft = mine, mine
        beside = [target, mine]
        crossed = []
        for step in range(1, count // 2 + 1):
            last = step == count // 2
            if step > 1:
                fore, one = lax.optimization_barrier((fore, swapped(beside[0])))
                aft, two = lax.optimization_barrier((aft, swapped(beside[1])))
                crossed += [one, two]
                beside = [own[-2], own[-1]]
            fore, aft = ahead(fore[:half] if last else fore), behind(aft[half:] if last else aft)
            own += [fore, aft]
            places += [(count - step, 0), (step, half if last else 0)]
        crossed += [swapped(value) for value in own[-4:]]
        target, other = crossed[0], crossed[1:]
    else:
        own = [lax.all_gather(mine, "dp", axis=0, tiled=True)]
        places = [(0, 0)]
        target, other = swapped(target), [swapped(own[0])]
    own_g, near_g, rest_g = run_layers(
        lengths, x, target, own, other, places, rows if ringed else 0, count, micro, length, width
    )
    near_g = swapped(near_g)
    if ringed:
        mid = count // 2
        near = (own_g[:rows] + near_g.astype(F32)).astype(BF16)
        rest_g, near = lax.optimization_barrier((rest_g, near))
        fore, aft = ahead(near[:half]), behind(near[half:])
        rest_g = swapped(rest_g)

        def block(index):
            at = (index + mid) % count * rows
            return own_g[at : at + rows] + rest_g[at - rows : at].astype(F32)

        up, down = block(mid - 1), block(mid + 1)
        fore = jnp.concatenate([up[:half] + fore.astype(F32), up[half:]], axis=0).astype(BF16)
        aft = jnp.concatenate([down[:half], down[half:] + aft.astype(F32)], axis=0).astype(BF16)
        for step in range(mid - 2, -1, -1):
            fore, aft = lax.optimization_barrier((fore, aft))
            fore, aft = ahead(fore), behind(aft)
            if step:
                fore = (block(step) + fore.astype(F32)).astype(BF16)
                aft = (block(count - step) + aft.astype(F32)).astype(BF16)
        terms = ((own_g, mid * rows), (rest_g, (mid - 1) * rows), (fore, 0), (aft, 0))
    else:
        total = own_g + jnp.concatenate([near_g, swapped(rest_g)], axis=0).astype(F32)
        terms = ((lax.psum_scatter(total, "dp", scatter_dimension=0, tiled=True), 0),)
    new_first, new_second, update, squares = run_moments(weights, moment_first[0], moment_second[0], terms)
    if ringed:
        hop = 1
        while 2 * hop < count:
            squares = squares + lax.ppermute(squares, "dp", [(i, i ^ hop) for i in range(count)])
            hop *= 2
        pair = (squares, lax.ppermute(squares, "dp", [(i, i ^ hop) for i in range(count)]))
    else:
        pair = (lax.psum(squares, "dp"),)
    new_master = run_master(weights, update, pair)
    return (new_master[None], new_first[None], new_second[None])


def moments(starts, w_in, first_in, second_in, *refs):
    count = len(starts)
    terms_in, refs = refs[:count], refs[count:]
    outs_out, squares_out, refs = refs[:3], refs[3], refs[4:]
    weights, first, second = refs[:3]
    terms, outs, squares, in_sem, out_sem = refs[3 : 3 + count], refs[3 + count : 6 + count], *refs[6 + count :]
    rows, width = weights.shape
    loads = [
        pltpu.make_async_copy(src, dst, in_sem.at[i])
        for i, (src, dst) in enumerate(
            [(src.at[pl.ds(at, rows)], dst) for src, at, dst in zip(terms_in, starts, terms)]
            + [(w_in, weights), (first_in, first), (second_in, second)]
        )
    ]
    for copy in loads:
        copy.start()
    for copy in loads:
        copy.wait()
    pieces = CUTS if rows % (CUTS * 8) == 0 else 1
    tall = rows // pieces
    sums = [jnp.zeros((8, 128), F32), jnp.zeros((8, 128), F32)]
    stores = []
    for piece in range(pieces):
        here = slice(piece * tall, (piece + 1) * tall)
        grad = terms[0][here]
        for term in terms[1:]:
            grad = grad + term[here].astype(F32)
        new_first = 0.9 * first[here] + 0.1 * grad
        new_second = 0.999 * second[here] + 0.001 * grad * grad
        corrected = new_first * (1.0 / (1.0 - 0.9**STEP))
        spread = new_second * (1.0 / (1.0 - 0.999**STEP))
        update = corrected / (jnp.sqrt(spread) + 1e-06) + 0.05 * weights[here]
        for index, value in enumerate((new_first, new_second, update)):
            outs[index][here] = value
            copy = pltpu.make_async_copy(outs[index].at[here], outs_out[index].at[here], out_sem.at[index, piece])
            copy.start()
            stores.append(copy)
        for index, value in enumerate((weights[here], update)):
            square = jnp.sum((value * value).reshape(tall // 8, 8, width), axis=0)
            for start in range(0, width, 128):
                sums[index] = sums[index] + square[:, start : start + 128]
    squares[...] = jnp.concatenate(sums, axis=0)
    copy = pltpu.make_async_copy(squares, squares_out, in_sem.at[0])
    copy.start()
    for store in stores + [copy]:
        store.wait()


def run_moments(weights, first, second, terms):
    free = pl.BlockSpec(memory_space=pl.ANY)
    rows, width = weights.shape
    same = jax.ShapeDtypeStruct(weights.shape, F32)
    return pl.pallas_call(
        functools.partial(moments, tuple(at for _, at in terms)),
        out_shape=(same, same, same, jax.ShapeDtypeStruct((16, 128), F32)),
        in_specs=[free] * (3 + len(terms)),
        out_specs=(free,) * 4,
        scratch_shapes=[pltpu.VMEM((rows, width), F32)] * 3
        + [pltpu.VMEM((rows, width), term.dtype) for term, _ in terms]
        + [pltpu.VMEM((rows, width), F32)] * 3
        + [
            pltpu.VMEM((16, 128), F32),
            pltpu.SemaphoreType.DMA((3 + len(terms),)),
            pltpu.SemaphoreType.DMA((3, CUTS)),
        ],
        compiler_params=pltpu.CompilerParams(vmem_limit_bytes=12 * 1024 * 1024),
    )(weights, first, second, *[term for term, _ in terms])


def master_step(w_in, update_in, *refs):
    count = (len(refs) - 5) // 2
    squares_in, out, refs = refs[:count], refs[count], refs[count + 1 :]
    weights, update, squares, in_sem, out_sem = refs[0], refs[1], refs[2 : 2 + count], *refs[2 + count :]
    loads = [
        pltpu.make_async_copy(src, dst, in_sem.at[i])
        for i, (src, dst) in enumerate([*zip(squares_in, squares), (w_in, weights), (update_in, update)])
    ]
    for copy in loads:
        copy.start()
    for copy in loads:
        copy.wait()
    total = squares[0][...]
    for more in squares[1:]:
        total = total + more[...]
    weight_sq = jnp.sum(total[:8], axis=(0, 1), keepdims=True)
    update_sq = jnp.sum(total[8:], axis=(0, 1), keepdims=True)
    trust = jnp.sqrt(weight_sq) / (jnp.sqrt(update_sq) + 1e-06)
    rows, width = weights.shape
    pieces = CUTS if rows % (CUTS * 8) == 0 else 1
    stores = []
    for piece in range(pieces):
        here = slice(piece * rows // pieces, (piece + 1) * rows // pieces)
        update[here] = weights[here] - 0.05 * trust * update[here]
        copy = pltpu.make_async_copy(update.at[here], out.at[here], out_sem.at[piece])
        copy.start()
        stores.append(copy)
    for copy in stores:
        copy.wait()


def run_master(weights, update, pair):
    free = pl.BlockSpec(memory_space=pl.ANY)
    rows, width = weights.shape
    return pl.pallas_call(
        master_step,
        out_shape=jax.ShapeDtypeStruct(weights.shape, F32),
        in_specs=[free] * (2 + len(pair)),
        out_specs=free,
        scratch_shapes=[pltpu.VMEM((rows, width), F32)] * 2
        + [pltpu.VMEM((16, 128), F32)] * len(pair)
        + [pltpu.SemaphoreType.DMA((2 + len(pair),)), pltpu.SemaphoreType.DMA((CUTS,))],
        compiler_params=pltpu.CompilerParams(vmem_limit_bytes=6 * 1024 * 1024),
    )(weights, update, *pair)


def solution(mesh):
    rows = P("pipe", ("groups", "dp"), None)
    in_specs = (
        P("pipe", ("groups", "dp"), None, None),
        P("pipe", ("groups", "dp"), None, None),
        P("pipe", ("groups", "dp")),
        rows,
        rows,
        rows,
    )
    return jax.shard_map(
        on_device, mesh=mesh, in_specs=in_specs, out_specs=(rows, rows, rows), check_vma=False
    )
```

time: 137 us -> 106 us (0.77)
  Pallas kernels: 39.8 us -> 21.8 us
  other arithmetic: 14.2 us -> 1.98 us
  waiting for transfers between devices: 52.6 us -> 55.2 us
  local copies, waits for them, and re-layouts: 3.27 us -> 1.79 us
    pallas_call x1 -> x3, Pallas kernels: 39.8 us -> 21.8 us  [the longest x1 18.6 us: run_layers(): pl.pallas_call(functools.partial(layers, micro, length, width, rows, coun...]
    another operation x3 -> x2, other arithmetic: 4.38 us -> 0.07 us
    add x3 -> x2, other arithmetic: 2.71 us -> 0.01 us  [on_device(): squares + lax.ppermute(squares, 'dp', [(i, i ^ hop) for i in range(count)])]
    reduce_sum x1 -> x0, other arithmetic: 2.09 us -> none  [on_device(): squares = jnp.stack([jnp.sum(weights * weights), jnp.sum(update * update)])]
    select_n x2 -> x0, other arithmetic: 1.94 us -> none  [the longest x1 1.3 us: on_device(): scalars.append((position - me + count) % count)]
    ppermute x8, starting transfers between devices: 13.9 us -> 12.2 us  [behind(): return lax.ppermute(value, 'dp', backward_way)]
    unnamed x18 -> x10, local copies, waits for them, and re-layouts: 0.04 us -> 1.72 us
    ppermute x11 -> x12, waiting for transfers between devices: 4.02 us -> 4.29 us  [swapped(): return lax.ppermute(value, 'pipe', [(0, 1), (1, 0)])]
  transfers between devices with their start and end apart: 30 -> 31, of which waited for: 18 -> 20; matrix products, arithmetic and copies ran while one was open for 4% -> 1% of each run, Pallas kernels for 0% -> 0%
where the time goes in v2:
time: 106 us; the launch traced here: 105 us
  waiting for transfers between devices  55.2 us (52%)
  starting transfers between devices  23.6 us (22%)
  Pallas kernels  21.8 us (21%)
  other arithmetic  1.98 us (2%)
  local copies, waits for them, and re-layouts  1.79 us (2%)
    ppermute x8, waiting for transfers between devices, behind(): return lax.ppermute(value, 'dp', backward_way)  24.7 us
    ppermute x8, waiting for transfers between devices, ahead(): return lax.ppermute(value, 'dp', onward)  18.8 us
    pallas_call x1, Pallas kernels, run_layers(): pl.pallas_call(functools.partial(layers, micro, length, width, rows, coun...  18.6 us
    ppermute x8, starting transfers between devices, behind(): return lax.ppermute(value, 'dp', backward_way)  12.2 us
    ppermute x3, waiting for transfers between devices, on_device(): lax.ppermute(squares, 'dp', [(i, i ^ hop) for i in range(count)])  7.35 us
    ppermute x8, starting transfers between devices, ahead(): return lax.ppermute(value, 'dp', onward)  5.01 us
    ppermute x3, starting transfers between devices, on_device(): lax.ppermute(squares, 'dp', [(i, i ^ hop) for i in range(count)])  4.57 us
    ppermute x12, waiting for transfers between devices, swapped(): return lax.ppermute(value, 'pipe', [(0, 1), (1, 0)])  4.29 us
  transfers between devices with their start and end apart: 31, of which 20 were waited for; matrix products, arithmetic and copies ran while one was open for 1% of the time, Pallas kernels for 0%

profile of v2, /device:TPU:0, one launch (start us, length us, event | category | flops | bytes accessed | tf_op | source)
XLA Modules:
  0.0 105.3 jit_solution(7382957665407721847)
XLA Ops:
  1.1 1.1 %bitcast_convert_fusion.refs_0_ = bf16[256,512]{1,0:T(8,128)(2,1)S(1)} fusion(f32[1,256,512]{2,1,0:T(8,128)} %param.9), kind=kLoop, calls=%fused_computation.15 | loop fusion | flops 131072 | bytes 786432 | tf_op jit(solution)/shard_map/convert_element_type | solution.py:293
  2.3 2.9 %collective-permute-start.2 = (bf16[256,512]{1,0:T(8,128)(2,1)S(1)}, bf16[256,512]{1,0:T(8,128)(2,1)S(1)}, u32[]{:S(2)}, u32[]{:S(2)}) collective-permute-start(bf16[256,512]{1,0:T(8,128)(2,1)S(1)} %bitcast_convert_fusion.refs_0_), channel_id=1, source_target_pairs={{4,0},{8,4},{12,8},{14,12},{10,14},{6,10},{2,6},{0,2},{5,1},{9,5},... | collective-permute-start | bytes 786440 | tf_op jit(solution)/shard_map/ppermute | solution.py:291
  5.4 6.5 %collective-permute-done.2.refs_2_ = bf16[256,512]{1,0:T(8,128)(2,1)S(1)} collective-permute-done((bf16[256,512]{1,0:T(8,128)(2,1)S(1)}, bf16[256,512]{1,0:T(8,128)(2,1)S(1)}, u32[]{:S(2)}, u32[]{:S(2)}) %collective-permute-start.2) | collective-permute-done | bytes 262176 | tf_op jit(solution)/shard_map/ppermute | solution.py:291
  11.9 1.7 %collective-permute-start.5 = (bf16[256,512]{1,0:T(8,128)(2,1)S(1)}, bf16[256,512]{1,0:T(8,128)(2,1)S(1)}, u32[]{:S(2)}, u32[]{:S(2)}) collective-permute-start(bf16[256,512]{1,0:T(8,128)(2,1)S(1)} %collective-permute-done.2.refs_2_), channel_id=1, source_target_pairs={{4,0},{8,4},{12,8},{14,12},{10,14},{6,10},{2,6},{0,2},{5,1},{9,5},... | collective-permute-start | bytes 786440 | tf_op jit(solution)/shard_map/ppermute | solution.py:291
  14.5 5.2 %collective-permute-done.5.refs_4_ = bf16[256,512]{1,0:T(8,128)(2,1)S(1)} collective-permute-done((bf16[256,512]{1,0:T(8,128)(2,1)S(1)}, bf16[256,512]{1,0:T(8,128)(2,1)S(1)}, u32[]{:S(2)}, u32[]{:S(2)}) %collective-permute-start.5) | collective-permute-done | bytes 262176 | tf_op jit(solution)/shard_map/ppermute | solution.py:291
  19.7 1.3 %collective-permute-start.9 = (bf16[256,512]{1,0:T(8,128)(2,1)S(1)}, bf16[256,512]{1,0:T(8,128)(2,1)S(1)}, u32[]{:S(2)}, u32[]{:S(2)}) collective-permute-start(bf16[256,512]{1,0:T(8,128)(2,1)S(1)} %collective-permute-done.5.refs_4_), channel_id=1, source_target_pairs={{4,0},{8,4},{12,8},{14,12},{10,14},{6,10},{2,6},{0,2},{5,1},{9,5},... | collective-permute-start | bytes 786440 | tf_op jit(solution)/shard_map/ppermute | solution.py:291
  21.0 1.3 %collective-permute-done.3.refs_3_ = bf16[256,512]{1,0:T(8,128)(2,1)S(1)} collective-permute-done((bf16[256,512]{1,0:T(8,128)(2,1)S(1)}, bf16[256,512]{1,0:T(8,128)(2,1)S(1)}, u32[]{:S(2)}, u32[]{:S(2)}) %collective-permute-start.3) | collective-permute-done | bytes 262176 | tf_op jit(solution)/shard_map/ppermute | solution.py:288
  22.7 5.7 %collective-permute-done.9.refs_6_ = bf16[256,512]{1,0:T(8,128)(2,1)S(1)} collective-permute-done((bf16[256,512]{1,0:T(8,128)(2,1)S(1)}, bf16[256,512]{1,0:T(8,128)(2,1)S(1)}, u32[]{:S(2)}, u32[]{:S(2)}) %collective-permute-start.9) | collective-permute-done | bytes 262176 | tf_op jit(solution)/shard_map/ppermute | solution.py:291
  28.4 1.4 %collective-permute-start.13 = (bf16[128,512]{1,0:T(8,128)(2,1)S(1)}, bf16[128,512]{1,0:T(8,128)(2,1)S(1)}, u32[]{:S(2)}, u32[]{:S(2)}) collective-permute-start(bf16[128,512]{1,0:T(8,128)(2,1)S(1)} %slice.66), channel_id=1, source_target_pairs={{4,0},{8,4},{12,8},{14,12},{10,14},{6,10},{2,6},{0,2},{5,1},{9,5},... | collective-permute-start | bytes 393224 | tf_op jit(solution)/shard_map/ppermute | solution.py:291
  30.8 2.8 %collective-permute-done.13.refs_8_ = bf16[128,512]{1,0:T(8,128)(2,1)S(1)} collective-permute-done((bf16[128,512]{1,0:T(8,128)(2,1)S(1)}, bf16[128,512]{1,0:T(8,128)(2,1)S(1)}, u32[]{:S(2)}, u32[]{:S(2)}) %collective-permute-start.13) | collective-permute-done | bytes 131104 | tf_op jit(solution)/shard_map/ppermute | solution.py:291
  33.6 2.2 %collective-permute-done.11.refs_7_ = bf16[128,512]{1,0:T(8,128)(2,1)S(1)} collective-permute-done((bf16[128,512]{1,0:T(8,128)(2,1)S(1)}, bf16[128,512]{1,0:T(8,128)(2,1)S(1)}, u32[]{:S(2)}, u32[]{:S(2)}) %collective-permute-start.11) | collective-permute-done | bytes 131104 | tf_op jit(solution)/shard_map/ppermute | solution.py:288
  35.8 1.3 %collective-permute-done.16.refs_16_ = bf16[128,512]{1,0:T(8,128)(2,1)S(1)} collective-permute-done((bf16[128,512]{1,0:T(8,128)(2,1)S(1)}, bf16[128,512]{1,0:T(8,128)(2,1)S(1)}, u32[]{:S(2)}, u32[]{:S(2)}) %collective-permute-start.16) | collective-permute-done | bytes 131104 | tf_op jit(solution)/shard_map/ppermute | solution.py:270
  38.8 18.6 %shard_map.85 = (f32[2048,512]{1,0:T(8,128)S(1)}, bf16[256,512]{1,0:T(8,128)(2,1)S(1)}, bf16[1792,512]{1,0:T(8,128)(2,1)S(1)}) custom-call(s32[1,2]{1,0:T(1,128)S(1)} %copy-done.4, bf16[512,512]{1,0:T(8,128)(2,1)S(1)} %bitcast.13, bf16[512,512]{1,0:T(8,128)(2,1)S(1)} %collective-permute-done.1.g_in, bf16[256,512]{1,0:T(8,128)(2,1)S(1)} %bitcast_convert_fusion.refs_0_, ...), custom_call_target="tpu_custom_call" | custom-call | tf_op jit(solution)/shard_map/pallas_call | solution.py:232
  57.7 1.4 %collective-permute-done.18 = bf16[256,512]{1,0:T(8,128)(2,1)S(1)} collective-permute-done((bf16[256,512]{1,0:T(8,128)(2,1)S(1)}, bf16[256,512]{1,0:T(8,128)(2,1)S(1)}, u32[]{:S(2)}, u32[]{:S(2)}) %collective-permute-start.18) | collective-permute-done | bytes 262176 | tf_op jit(solution)/shard_map/ppermute | solution.py:270
  59.4 1.6 %collective-permute-start.21 = (bf16[128,512]{1,0:T(8,128)(2,1)S(1)}, bf16[128,512]{1,0:T(8,128)(2,1)S(1)}, u32[]{:S(2)}, u32[]{:S(2)}) collective-permute-start(bf16[128,512]{1,0:T(8,128)(2,1)S(1)} %get-tuple-element.63), channel_id=1, source_target_pairs={{4,0},{8,4},{12,8},{14,12},{10,14},{6,10},{2,6},{0,2},{5,1},{9,5},... | collective-permute-start | bytes 393224 | tf_op jit(solution)/shard_map/ppermute | solution.py:291
  61.5 1.5 %collective-permute-done.19.refs_1_ = bf16[1792,512]{1,0:T(8,128)(2,1)S(1)} collective-permute-done((bf16[1792,512]{1,0:T(8,128)(2,1)S(1)}, bf16[1792,512]{1,0:T(8,128)(2,1)S(1)}, u32[]{:S(2)}, u32[]{:S(2)}) %collective-permute-start.19) | collective-permute-done | bytes 1835040 | tf_op jit(solution)/shard_map/ppermute | solution.py:270
  63.2 2.0 %collective-permute-done.21 = bf16[128,512]{1,0:T(8,128)(2,1)S(1)} collective-permute-done((bf16[128,512]{1,0:T(8,128)(2,1)S(1)}, bf16[128,512]{1,0:T(8,128)(2,1)S(1)}, u32[]{:S(2)}, u32[]{:S(2)}) %collective-permute-start.21) | collective-permute-done | bytes 131104 | tf_op jit(solution)/shard_map/ppermute | solution.py:291
  65.3 1.2 %collective-permute-done.20 = bf16[128,512]{1,0:T(8,128)(2,1)S(1)} collective-permute-done((bf16[128,512]{1,0:T(8,128)(2,1)S(1)}, bf16[128,512]{1,0:T(8,128)(2,1)S(1)}, u32[]{:S(2)}, u32[]{:S(2)}) %collective-permute-start.20) | collective-permute-done | bytes 131104 | tf_op jit(solution)/shard_map/ppermute | solution.py:288
  67.1 1.6 %collective-permute-start.23 = (bf16[256,512]{1,0:T(8,128)(2,1)S(1)}, bf16[256,512]{1,0:T(8,128)(2,1)S(1)}, u32[]{:S(2)}, u32[]{:S(2)}) collective-permute-start(bf16[256,512]{1,0:T(8,128)(2,1)S(1)} %pad_maximum_fusion.1), channel_id=1, source_target_pairs={{4,0},{8,4},{12,8},{14,12},{10,14},{6,10},{2,6},{0,2},{5,1},{9,5},... | collective-permute-start | bytes 786440 | tf_op jit(solution)/shard_map/ppermute | solution.py:291
  68.7 5.4 %collective-permute-done.22 = bf16[256,512]{1,0:T(8,128)(2,1)S(1)} collective-permute-done((bf16[256,512]{1,0:T(8,128)(2,1)S(1)}, bf16[256,512]{1,0:T(8,128)(2,1)S(1)}, u32[]{:S(2)}, u32[]{:S(2)}) %collective-permute-start.22) | collective-permute-done | bytes 262176 | tf_op jit(solution)/shard_map/ppermute | solution.py:288
  75.4 1.2 %collective-permute-start.25 = (bf16[256,512]{1,0:T(8,128)(2,1)S(1)}, bf16[256,512]{1,0:T(8,128)(2,1)S(1)}, u32[]{:S(2)}, u32[]{:S(2)}) collective-permute-start(bf16[256,512]{1,0:T(8,128)(2,1)S(1)} %get-tuple-element.50), channel_id=1, source_target_pairs={{4,0},{8,4},{12,8},{14,12},{10,14},{6,10},{2,6},{0,2},{5,1},{9,5},... | collective-permute-start | bytes 786440 | tf_op jit(solution)/shard_map/ppermute | solution.py:291
  76.6 4.3 %collective-permute-done.24 = bf16[256,512]{1,0:T(8,128)(2,1)S(1)} collective-permute-done((bf16[256,512]{1,0:T(8,128)(2,1)S(1)}, bf16[256,512]{1,0:T(8,128)(2,1)S(1)}, u32[]{:S(2)}, u32[]{:S(2)}) %collective-permute-start.24) | collective-permute-done | bytes 262176 | tf_op jit(solution)/shard_map/ppermute | solution.py:288
  82.0 1.6 %collective-permute-start.26 = (bf16[256,512]{1,0:T(8,128)(2,1)S(1)}, bf16[256,512]{1,0:T(8,128)(2,1)S(1)}, u32[]{:S(2)}, u32[]{:S(2)}) collective-permute-start(bf16[256,512]{1,0:T(8,128)(2,1)S(1)} %get-tuple-element.51), channel_id=1, source_target_pairs={{0,4},{4,8},{8,12},{12,14},{14,10},{10,6},{6,2},{2,0},{1,5},{5,9},... | collective-permute-start | bytes 786440 | tf_op jit(solution)/shard_map/ppermute | solution.py:288
  84.1 4.3 %collective-permute-done.26.refs_2_ = bf16[256,512]{1,0:T(8,128)(2,1)S(1)} collective-permute-done((bf16[256,512]{1,0:T(8,128)(2,1)S(1)}, bf16[256,512]{1,0:T(8,128)(2,1)S(1)}, u32[]{:S(2)}, u32[]{:S(2)}) %collective-permute-start.26) | collective-permute-done | bytes 262176 | tf_op jit(solution)/shard_map/ppermute | solution.py:288
  88.5 1.6 %collective-permute-done.27.refs_3_ = bf16[256,512]{1,0:T(8,128)(2,1)S(1)} collective-permute-done((bf16[256,512]{1,0:T(8,128)(2,1)S(1)}, bf16[256,512]{1,0:T(8,128)(2,1)S(1)}, u32[]{:S(2)}, u32[]{:S(2)}) %collective-permute-start.27) | collective-permute-done | bytes 262176 | tf_op jit(solution)/shard_map/ppermute | solution.py:291
  90.1 2.1 %shard_map.86 = (f32[256,512]{1,0:T(8,128)}, f32[256,512]{1,0:T(8,128)}, f32[256,512]{1,0:T(8,128)S(1)}, f32[16,128]{1,0:T(8,128)S(1)}) custom-call(f32[256,512]{1,0:T(8,128)S(1)} %bitcast.9, f32[256,512]{1,0:T(8,128)S(1)} %bitcast.11, f32[256,512]{1,0:T(8,128)S(1)} %bitcast.12, f32[2048,512]{1,0:T(8,128)S(1)} %get-tuple-element.42.refs_0_, ...), custom_call_target="tpu_custom_call" | custom-call | tf_op jit(solution)/shard_map/pallas_call | solution.py:412
  92.7 3.2 %collective-permute-done.28 = f32[16,128]{1,0:T(8,128)S(1)} collective-permute-done((f32[16,128]{1,0:T(8,128)S(1)}, f32[16,128]{1,0:T(8,128)S(1)}, u32[]{:S(2)}, u32[]{:S(2)}) %collective-permute-start.28) | collective-permute-done | bytes 8224 | tf_op jit(solution)/shard_map/ppermute | solution.py:351
  95.9 1.6 %collective-permute-start.29 = (f32[16,128]{1,0:T(8,128)S(1)}, f32[16,128]{1,0:T(8,128)S(1)}, u32[]{:S(2)}, u32[]{:S(2)}) collective-permute-start(f32[16,128]{1,0:T(8,128)S(1)} %add.58), channel_id=1, source_target_pairs={{0,4},{2,6},{4,0},{6,2},{8,12},{10,14},{12,8},{14,10},{1,5},{3,7},... | collective-permute-start | bytes 24584 | tf_op jit(solution)/shard_map/ppermute | solution.py:351
  97.5 2.1 %collective-permute-done.29 = f32[16,128]{1,0:T(8,128)S(1)} collective-permute-done((f32[16,128]{1,0:T(8,128)S(1)}, f32[16,128]{1,0:T(8,128)S(1)}, u32[]{:S(2)}, u32[]{:S(2)}) %collective-permute-start.29) | collective-permute-done | bytes 8224 | tf_op jit(solution)/shard_map/ppermute | solution.py:351
  99.5 2.5 %collective-permute-start.30 = (f32[16,128]{1,0:T(8,128)S(1)}, f32[16,128]{1,0:T(8,128)S(1)}, u32[]{:S(2)}, u32[]{:S(2)}) collective-permute-start(f32[16,128]{1,0:T(8,128)S(1)} %add.59.refs_0_), channel_id=1, source_target_pairs={{0,8},{2,10},{4,12},{6,14},{8,0},{10,2},{12,4},{14,6},{1,9},{3,11}... | collective-permute-start | bytes 24584 | tf_op jit(solution)/shard_map/ppermute | solution.py:353
  102.0 2.1 %collective-permute-done.30.refs_1_ = f32[16,128]{1,0:T(8,128)S(1)} collective-permute-done((f32[16,128]{1,0:T(8,128)S(1)}, f32[16,128]{1,0:T(8,128)S(1)}, u32[]{:S(2)}, u32[]{:S(2)}) %collective-permute-start.30) | collective-permute-done | bytes 8224 | tf_op jit(solution)/shard_map/ppermute | solution.py:353
  104.1 1.1 %shard_map.87 = f32[256,512]{1,0:T(8,128)} custom-call(f32[256,512]{1,0:T(8,128)S(1)} %bitcast.10, f32[256,512]{1,0:T(8,128)S(1)} %get-tuple-element.53.update_in, f32[16,128]{1,0:T(8,128)S(1)} %add.59.refs_0_, f32[16,128]{1,0:T(8,128)S(1)} %collective-permute-done.30.refs_1_), custom_call_target="tpu_custom_call" | custom-call | tf_op jit(solution)/shard_map/pallas_call | solution.py:463
  (59 shorter events, 9.8 us)
Async XLA Ops:
  0.6 13.5 %collective-permute-start.1 = (bf16[512,512]{1,0:T(8,128)(2,1)}, bf16[512,512]{1,0:T(8,128)(2,1)S(1)}, u32[]{:S(2)}, u32[]{:S(2)}) collective-permute-start(bf16[512,512]{1,0:T(8,128)(2,1)} %bitcast.15), channel_id=1, source_target_pairs={{0,1},{1,0},{2,3},{3,2},{4,5},{5,4},{6,7},{7,6},{8,9},{9,8},{10,11... | collective-permute-start | bytes 1572872 | tf_op jit(solution)/shard_map/ppermute | solution.py:270
  2.2 3.2 %collective-permute-start.4 = (bf16[256,512]{1,0:T(8,128)(2,1)S(1)}, bf16[256,512]{1,0:T(8,128)(2,1)S(1)}, u32[]{:S(2)}, u32[]{:S(2)}) collective-permute-start(bf16[256,512]{1,0:T(8,128)(2,1)S(1)} %bitcast_convert_fusion.refs_0_), channel_id=1, source_target_pairs={{0,1},{1,0},{2,3},{3,2},{4,5},{5,4},{6,7},{7,6},{8,9},{9,8},{10,11... | collective-permute-start | bytes 786440 | tf_op jit(solution)/shard_map/ppermute | solution.py:270
  2.3 9.6 %collective-permute-start.2 = (bf16[256,512]{1,0:T(8,128)(2,1)S(1)}, bf16[256,512]{1,0:T(8,128)(2,1)S(1)}, u32[]{:S(2)}, u32[]{:S(2)}) collective-permute-start(bf16[256,512]{1,0:T(8,128)(2,1)S(1)} %bitcast_convert_fusion.refs_0_), channel_id=1, source_target_pairs={{4,0},{8,4},{12,8},{14,12},{10,14},{6,10},{2,6},{0,2},{5,1},{9,5},... | collective-permute-start | bytes 786440 | tf_op jit(solution)/shard_map/ppermute | solution.py:291
  5.3 8.3 %collective-permute-start = (bf16[256,512]{1,0:T(8,128)(2,1)S(1)}, bf16[256,512]{1,0:T(8,128)(2,1)S(1)}, u32[]{:S(2)}, u32[]{:S(2)}) collective-permute-start(bf16[256,512]{1,0:T(8,128)(2,1)S(1)} %bitcast_convert_fusion.refs_0_), channel_id=1, source_target_pairs={{0,4},{4,8},{8,12},{12,14},{14,10},{10,6},{6,2},{2,0},{1,5},{5,9},... | collective-permute-start | bytes 786440 | tf_op jit(solution)/shard_map/ppermute | solution.py:288
  11.9 7.8 %collective-permute-start.5 = (bf16[256,512]{1,0:T(8,128)(2,1)S(1)}, bf16[256,512]{1,0:T(8,128)(2,1)S(1)}, u32[]{:S(2)}, u32[]{:S(2)}) collective-permute-start(bf16[256,512]{1,0:T(8,128)(2,1)S(1)} %collective-permute-done.2.refs_2_), channel_id=1, source_target_pairs={{4,0},{8,4},{12,8},{14,12},{10,14},{6,10},{2,6},{0,2},{5,1},{9,5},... | collective-permute-start | bytes 786440 | tf_op jit(solution)/shard_map/ppermute | solution.py:291
  13.6 6.1 %collective-permute-start.8 = (bf16[256,512]{1,0:T(8,128)(2,1)S(1)}, bf16[256,512]{1,0:T(8,128)(2,1)S(1)}, u32[]{:S(2)}, u32[]{:S(2)}) collective-permute-start(bf16[256,512]{1,0:T(8,128)(2,1)S(1)} %collective-permute-done.2.refs_2_), channel_id=1, source_target_pairs={{0,1},{1,0},{2,3},{3,2},{4,5},{5,4},{6,7},{7,6},{8,9},{9,8},{10,11... | collective-permute-start | bytes 786440 | tf_op jit(solution)/shard_map/ppermute | solution.py:270
  13.6 7.4 %collective-permute-start.6 = (bf16[256,512]{1,0:T(8,128)(2,1)S(1)}, bf16[256,512]{1,0:T(8,128)(2,1)S(1)}, u32[]{:S(2)}, u32[]{:S(2)}) collective-permute-start(bf16[256,512]{1,0:T(8,128)(2,1)S(1)} %collective-permute-done.refs_1_), channel_id=1, source_target_pairs={{0,1},{1,0},{2,3},{3,2},{4,5},{5,4},{6,7},{7,6},{8,9},{9,8},{10,11... | collective-permute-start | bytes 786440 | tf_op jit(solution)/shard_map/ppermute | solution.py:270
  14.1 8.3 %collective-permute-start.3 = (bf16[256,512]{1,0:T(8,128)(2,1)S(1)}, bf16[256,512]{1,0:T(8,128)(2,1)S(1)}, u32[]{:S(2)}, u32[]{:S(2)}) collective-permute-start(bf16[256,512]{1,0:T(8,128)(2,1)S(1)} %collective-permute-done.refs_1_), channel_id=1, source_target_pairs={{0,4},{4,8},{8,12},{12,14},{14,10},{10,6},{6,2},{2,0},{1,5},{5,9},... | collective-permute-start | bytes 786440 | tf_op jit(solution)/shard_map/ppermute | solution.py:288
  19.7 3.1 %collective-permute-start.12 = (bf16[256,512]{1,0:T(8,128)(2,1)S(1)}, bf16[256,512]{1,0:T(8,128)(2,1)S(1)}, u32[]{:S(2)}, u32[]{:S(2)}) collective-permute-start(bf16[256,512]{1,0:T(8,128)(2,1)S(1)} %collective-permute-done.5.refs_4_), channel_id=1, source_target_pairs={{0,1},{1,0},{2,3},{3,2},{4,5},{5,4},{6,7},{7,6},{8,9},{9,8},{10,11... | collective-permute-start | bytes 786440 | tf_op jit(solution)/shard_map/ppermute | solution.py:270
  19.7 8.7 %collective-permute-start.9 = (bf16[256,512]{1,0:T(8,128)(2,1)S(1)}, bf16[256,512]{1,0:T(8,128)(2,1)S(1)}, u32[]{:S(2)}, u32[]{:S(2)}) collective-permute-start(bf16[256,512]{1,0:T(8,128)(2,1)S(1)} %collective-permute-done.5.refs_4_), channel_id=1, source_target_pairs={{4,0},{8,4},{12,8},{14,12},{10,14},{6,10},{2,6},{0,2},{5,1},{9,5},... | collective-permute-start | bytes 786440 | tf_op jit(solution)/shard_map/ppermute | solution.py:291
  22.3 7.4 %collective-permute-start.7 = (bf16[256,512]{1,0:T(8,128)(2,1)S(1)}, bf16[256,512]{1,0:T(8,128)(2,1)S(1)}, u32[]{:S(2)}, u32[]{:S(2)}) collective-permute-start(bf16[256,512]{1,0:T(8,128)(2,1)S(1)} %collective-permute-done.3.refs_3_), channel_id=1, source_target_pairs={{0,4},{4,8},{8,12},{12,14},{14,10},{10,6},{6,2},{2,0},{1,5},{5,9},... | collective-permute-start | bytes 786440 | tf_op jit(solution)/shard_map/ppermute | solution.py:288
  22.7 7.1 %collective-permute-start.10 = (bf16[256,512]{1,0:T(8,128)(2,1)S(1)}, bf16[256,512]{1,0:T(8,128)(2,1)S(1)}, u32[]{:S(2)}, u32[]{:S(2)}) collective-permute-start(bf16[256,512]{1,0:T(8,128)(2,1)S(1)} %collective-permute-done.3.refs_3_), channel_id=1, source_target_pairs={{0,1},{1,0},{2,3},{3,2},{4,5},{5,4},{6,7},{7,6},{8,9},{9,8},{10,11... | collective-permute-start | bytes 786440 | tf_op jit(solution)/shard_map/ppermute | solution.py:270
  28.4 5.2 %collective-permute-start.13 = (bf16[128,512]{1,0:T(8,128)(2,1)S(1)}, bf16[128,512]{1,0:T(8,128)(2,1)S(1)}, u32[]{:S(2)}, u32[]{:S(2)}) collective-permute-start(bf16[128,512]{1,0:T(8,128)(2,1)S(1)} %slice.66), channel_id=1, source_target_pairs={{4,0},{8,4},{12,8},{14,12},{10,14},{6,10},{2,6},{0,2},{5,1},{9,5},... | collective-permute-start | bytes 393224 | tf_op jit(solution)/shard_map/ppermute | solution.py:291
  29.8 6.0 %collective-permute-start.15 = (bf16[256,512]{1,0:T(8,128)(2,1)S(1)}, bf16[256,512]{1,0:T(8,128)(2,1)S(1)}, u32[]{:S(2)}, u32[]{:S(2)}) collective-permute-start(bf16[256,512]{1,0:T(8,128)(2,1)S(1)} %collective-permute-done.9.refs_6_), channel_id=1, source_target_pairs={{0,1},{1,0},{2,3},{3,2},{4,5},{5,4},{6,7},{7,6},{8,9},{9,8},{10,11... | collective-permute-start | bytes 786440 | tf_op jit(solution)/shard_map/ppermute | solution.py:270
  29.8 6.0 %collective-permute-start.11 = (bf16[128,512]{1,0:T(8,128)(2,1)S(1)}, bf16[128,512]{1,0:T(8,128)(2,1)S(1)}, u32[]{:S(2)}, u32[]{:S(2)}) collective-permute-start(bf16[128,512]{1,0:T(8,128)(2,1)S(1)} %slice.65), channel_id=1, source_target_pairs={{0,4},{4,8},{8,12},{12,14},{14,10},{10,6},{6,2},{2,0},{1,5},{5,9},... | collective-permute-start | bytes 393224 | tf_op jit(solution)/shard_map/ppermute | solution.py:288
  30.6 6.6 %collective-permute-start.14 = (bf16[256,512]{1,0:T(8,128)(2,1)S(1)}, bf16[256,512]{1,0:T(8,128)(2,1)S(1)}, u32[]{:S(2)}, u32[]{:S(2)}) collective-permute-start(bf16[256,512]{1,0:T(8,128)(2,1)S(1)} %collective-permute-done.7.refs_5_), channel_id=1, source_target_pairs={{0,1},{1,0},{2,3},{3,2},{4,5},{5,4},{6,7},{7,6},{8,9},{9,8},{10,11... | collective-permute-start | bytes 786440 | tf_op jit(solution)/shard_map/ppermute | solution.py:270
  33.6 2.2 %collective-permute-start.17 = (bf16[128,512]{1,0:T(8,128)(2,1)S(1)}, bf16[128,512]{1,0:T(8,128)(2,1)S(1)}, u32[]{:S(2)}, u32[]{:S(2)}) collective-permute-start(bf16[128,512]{1,0:T(8,128)(2,1)S(1)} %collective-permute-done.13.refs_8_), channel_id=1, source_target_pairs={{0,1},{1,0},{2,3},{3,2},{4,5},{5,4},{6,7},{7,6},{8,9},{9,8},{10,11... | collective-permute-start | bytes 393224 | tf_op jit(solution)/shard_map/ppermute | solution.py:270
  35.8 1.3 %collective-permute-start.16 = (bf16[128,512]{1,0:T(8,128)(2,1)S(1)}, bf16[128,512]{1,0:T(8,128)(2,1)S(1)}, u32[]{:S(2)}, u32[]{:S(2)}) collective-permute-start(bf16[128,512]{1,0:T(8,128)(2,1)S(1)} %collective-permute-done.11.refs_7_), channel_id=1, source_target_pairs={{0,1},{1,0},{2,3},{3,2},{4,5},{5,4},{6,7},{7,6},{8,9},{9,8},{10,11... | collective-permute-start | bytes 393224 | tf_op jit(solution)/shard_map/ppermute | solution.py:270
  57.5 1.6 %collective-permute-start.18 = (bf16[256,512]{1,0:T(8,128)(2,1)S(1)}, bf16[256,512]{1,0:T(8,128)(2,1)S(1)}, u32[]{:S(2)}, u32[]{:S(2)}) collective-permute-start(bf16[256,512]{1,0:T(8,128)(2,1)S(1)} %get-tuple-element.44), channel_id=1, source_target_pairs={{0,1},{1,0},{2,3},{3,2},{4,5},{5,4},{6,7},{7,6},{8,9},{9,8},{10,11... | collective-permute-start | bytes 786440 | tf_op jit(solution)/shard_map/ppermute | solution.py:270
  59.2 3.9 %collective-permute-start.19 = (bf16[1792,512]{1,0:T(8,128)(2,1)S(1)}, bf16[1792,512]{1,0:T(8,128)(2,1)S(1)}, u32[]{:S(2)}, u32[]{:S(2)}) collective-permute-start(bf16[1792,512]{1,0:T(8,128)(2,1)S(1)} %get-tuple-element.45), channel_id=1, source_target_pairs={{0,1},{1,0},{2,3},{3,2},{4,5},{5,4},{6,7},{7,6},{8,9},{9,8},{10,11... | collective-permute-start | bytes 5505032 | tf_op jit(solution)/shard_map/ppermute | solution.py:270
  59.4 5.8 %collective-permute-start.21 = (bf16[128,512]{1,0:T(8,128)(2,1)S(1)}, bf16[128,512]{1,0:T(8,128)(2,1)S(1)}, u32[]{:S(2)}, u32[]{:S(2)}) collective-permute-start(bf16[128,512]{1,0:T(8,128)(2,1)S(1)} %get-tuple-element.63), channel_id=1, source_target_pairs={{4,0},{8,4},{12,8},{14,12},{10,14},{6,10},{2,6},{0,2},{5,1},{9,5},... | collective-permute-start | bytes 393224 | tf_op jit(solution)/shard_map/ppermute | solution.py:291
  61.0 5.5 %collective-permute-start.20 = (bf16[128,512]{1,0:T(8,128)(2,1)S(1)}, bf16[128,512]{1,0:T(8,128)(2,1)S(1)}, u32[]{:S(2)}, u32[]{:S(2)}) collective-permute-start(bf16[128,512]{1,0:T(8,128)(2,1)S(1)} %get-tuple-element.64), channel_id=1, source_target_pairs={{0,4},{4,8},{8,12},{12,14},{14,10},{10,6},{6,2},{2,0},{1,5},{5,9},... | collective-permute-start | bytes 393224 | tf_op jit(solution)/shard_map/ppermute | solution.py:288
  63.2 26.9 %copy-start = (f32[1,256,512]{2,1,0:T(8,128)S(1)}, f32[1,256,512]{2,1,0:T(8,128)}, u32[]{:S(2)}) copy-start(f32[1,256,512]{2,1,0:T(8,128)} %param.9) | copy-start | bytes 1572868
  66.6 7.5 %collective-permute-start.22 = (bf16[256,512]{1,0:T(8,128)(2,1)S(1)}, bf16[256,512]{1,0:T(8,128)(2,1)S(1)}, u32[]{:S(2)}, u32[]{:S(2)}) collective-permute-start(bf16[256,512]{1,0:T(8,128)(2,1)S(1)} %pad_maximum_fusion), channel_id=1, source_target_pairs={{0,4},{4,8},{8,12},{12,14},{14,10},{10,6},{6,2},{2,0},{1,5},{5,9},... | collective-permute-start | bytes 786440 | tf_op jit(solution)/shard_map/ppermute | solution.py:288
  67.1 7.2 %collective-permute-start.23 = (bf16[256,512]{1,0:T(8,128)(2,1)S(1)}, bf16[256,512]{1,0:T(8,128)(2,1)S(1)}, u32[]{:S(2)}, u32[]{:S(2)}) collective-permute-start(bf16[256,512]{1,0:T(8,128)(2,1)S(1)} %pad_maximum_fusion.1), channel_id=1, source_target_pairs={{4,0},{8,4},{12,8},{14,12},{10,14},{6,10},{2,6},{0,2},{5,1},{9,5},... | collective-permute-start | bytes 786440 | tf_op jit(solution)/shard_map/ppermute | solution.py:291
  74.5 6.4 %collective-permute-start.24 = (bf16[256,512]{1,0:T(8,128)(2,1)S(1)}, bf16[256,512]{1,0:T(8,128)(2,1)S(1)}, u32[]{:S(2)}, u32[]{:S(2)}) collective-permute-start(bf16[256,512]{1,0:T(8,128)(2,1)S(1)} %get-tuple-element.49), channel_id=1, source_target_pairs={{0,4},{4,8},{8,12},{12,14},{14,10},{10,6},{6,2},{2,0},{1,5},{5,9},... | collective-permute-start | bytes 786440 | tf_op jit(solution)/shard_map/ppermute | solution.py:288
  75.4 6.4 %collective-permute-start.25 = (bf16[256,512]{1,0:T(8,128)(2,1)S(1)}, bf16[256,512]{1,0:T(8,128)(2,1)S(1)}, u32[]{:S(2)}, u32[]{:S(2)}) collective-permute-start(bf16[256,512]{1,0:T(8,128)(2,1)S(1)} %get-tuple-element.50), channel_id=1, source_target_pairs={{4,0},{8,4},{12,8},{14,12},{10,14},{6,10},{2,6},{0,2},{5,1},{9,5},... | collective-permute-start | bytes 786440 | tf_op jit(solution)/shard_map/ppermute | solution.py:291
  82.0 6.4 %collective-permute-start.26 = (bf16[256,512]{1,0:T(8,128)(2,1)S(1)}, bf16[256,512]{1,0:T(8,128)(2,1)S(1)}, u32[]{:S(2)}, u32[]{:S(2)}) collective-permute-start(bf16[256,512]{1,0:T(8,128)(2,1)S(1)} %get-tuple-element.51), channel_id=1, source_target_pairs={{0,4},{4,8},{8,12},{12,14},{14,10},{10,6},{6,2},{2,0},{1,5},{5,9},... | collective-permute-start | bytes 786440 | tf_op jit(solution)/shard_map/ppermute | solution.py:288
  83.7 6.4 %collective-permute-start.27 = (bf16[256,512]{1,0:T(8,128)(2,1)S(1)}, bf16[256,512]{1,0:T(8,128)(2,1)S(1)}, u32[]{:S(2)}, u32[]{:S(2)}) collective-permute-start(bf16[256,512]{1,0:T(8,128)(2,1)S(1)} %get-tuple-element.52), channel_id=1, source_target_pairs={{4,0},{8,4},{12,8},{14,12},{10,14},{6,10},{2,6},{0,2},{5,1},{9,5},... | collective-permute-start | bytes 786440 | tf_op jit(solution)/shard_map/ppermute | solution.py:291
  92.2 3.7 %collective-permute-start.28 = (f32[16,128]{1,0:T(8,128)S(1)}, f32[16,128]{1,0:T(8,128)S(1)}, u32[]{:S(2)}, u32[]{:S(2)}) collective-permute-start(f32[16,128]{1,0:T(8,128)S(1)} %get-tuple-element.54), channel_id=1, source_target_pairs={{0,2},{2,0},{4,6},{6,4},{8,10},{10,8},{12,14},{14,12},{1,3},{3,1},... | collective-permute-start | bytes 24584 | tf_op jit(solution)/shard_map/ppermute | solution.py:351
  95.9 3.7 %collective-permute-start.29 = (f32[16,128]{1,0:T(8,128)S(1)}, f32[16,128]{1,0:T(8,128)S(1)}, u32[]{:S(2)}, u32[]{:S(2)}) collective-permute-start(f32[16,128]{1,0:T(8,128)S(1)} %add.58), channel_id=1, source_target_pairs={{0,4},{2,6},{4,0},{6,2},{8,12},{10,14},{12,8},{14,10},{1,5},{3,7},... | collective-permute-start | bytes 24584 | tf_op jit(solution)/shard_map/ppermute | solution.py:351
  99.5 4.5 %collective-permute-start.30 = (f32[16,128]{1,0:T(8,128)S(1)}, f32[16,128]{1,0:T(8,128)S(1)}, u32[]{:S(2)}, u32[]{:S(2)}) collective-permute-start(f32[16,128]{1,0:T(8,128)S(1)} %add.59.refs_0_), channel_id=1, source_target_pairs={{0,8},{2,10},{4,12},{6,14},{8,0},{10,2},{12,4},{14,6},{1,9},{3,11}... | collective-permute-start | bytes 24584 | tf_op jit(solution)/shard_map/ppermute | solution.py:353
  (4 other events, 55.4 us)

commit v3 on v2

--- a/solution.py
+++ b/solution.py
@@ -9,7 +9,7 @@
 
 HEAD = 64
 PAIR = 128
-AHEAD = 2
+AHEAD = 4
 CUTS = 4
 STEP = 10
 F32 = jnp.float32
@@ -141,11 +141,13 @@
     return jnp.where(spot < count // 2, 2 * spot, 2 * (count - 1 - spot) + 1)
 
 
-def layers(micro, length, width, rows, count, places, live_in, x_in, g_in, *refs):
-    size = len(places)
-    own_w, other_w = refs[:size], refs[size : 2 * size]
-    own_out, near_out, rest_out = refs[2 * size : 2 * size + 3]
-    (live_ref, x_ref, g_ref, w, own_g, other_g, hid, q_t, k, v, tr, p, mixed_t, xhat, rstd, g_t, dq_t, dk, dv, in_sem, out_sem, act_sem) = refs[2 * size + 3 :]
+def layers(micro, length, width, rows, count, plan, groups, live_in, x_in, g_in, *refs):
+    sizes = [len(part) for part in plan]
+    size = sum(sizes)
+    own_w = [(refs[i], piece) for i, part in enumerate(plan[0]) for piece in part]
+    other_w = [(refs[sizes[0] + i], piece) for i, part in enumerate(plan[1]) for piece in part]
+    own_out, other_outs = refs[size], refs[size + 1 : size + 1 + len(groups)]
+    (live_ref, x_ref, g_ref, w, own_g, other_g, hid, q_t, k, v, tr, p, mixed_t, xhat, rstd, g_t, dq_t, dk, dv, in_sem, out_sem, act_sem) = refs[size + 1 + len(groups) :]
     side = lax.axis_index("pipe")
     me = ring_spot(lax.axis_index("dp"), count)
     block = rows if rows else 4 * width
@@ -154,17 +156,32 @@
     g_copy = pltpu.make_async_copy(g_in, g_ref, act_sem.at[1])
     live_copy.start()
     x_copy.start()
-    for sec, group in ((side, own_w), (1 - side, other_w)):
-        for i, ((slot, shift), ref) in enumerate(zip(places, group)):
+    def load(sec, group):
+        for i, (ref, (slot, shift, start, tall)) in enumerate(group):
             at = pl.multiple_of(ring_index((me + slot) % count, count) * rows + shift, 16) if rows else 0
-            pltpu.make_async_copy(ref, w.at[sec, pl.ds(at, ref.shape[0])], in_sem.at[sec, i]).start()
+            there = w.at[sec, pl.ds(at, tall)]
+            pltpu.make_async_copy(ref.at[pl.ds(start, tall)], there, in_sem.at[sec, i]).start()
+
+    @pl.when(side == 0)
+    def _():
+        load(0, own_w)
+        load(1, other_w)
+
+    @pl.when(side != 0)
+    def _():
+        load(0, other_w)
+        load(1, own_w)
+
     tall = rows if rows else width
     g_copy.start()
+
+    starts = [sum(groups[:i]) for i in range(len(groups))]
 
     def turn_of(index):
         if not rows:
             return index
-        return (ring_spot(jnp.int32(index), count) - me + count + count // 2) % count
+        away = (ring_spot(jnp.int32(index), count) - me + count) % count - count // 2
+        return jnp.where(away < 0, -2 * away - 1, 2 * away)
 
     def emit(sec, part, value):
         for b in range(width // tall):
@@ -182,26 +199,25 @@
             def _():
                 pltpu.make_async_copy(own_g.at[sec, here], own_out.at[here], out_sem.at[0, index]).start()
 
-            @pl.when((side != sec) & (turn == 0))
-            def _():
-                pltpu.make_async_copy(other_g.at[sec, here], near_out, out_sem.at[1, index]).start()
-
-            @pl.when((side != sec) & (turn != 0))
-            def _():
-                there = pl.ds(pl.multiple_of((turn - 1) * tall, 16), tall)
-                pltpu.make_async_copy(other_g.at[sec, here], rest_out.at[there], out_sem.at[1, index]).start()
+            for start, blocks, out in zip(starts, groups, other_outs):
+
+                @pl.when((side != sec) & (turn >= start) & (turn < start + blocks))
+                def _():
+                    there = pl.ds(pl.multiple_of((turn - start) * tall, 16), tall)
+                    pltpu.make_async_copy(other_g.at[sec, here], out.at[there], out_sem.at[1, index]).start()
 
     def sent():
         for index in range(4 * width // tall):
             here = pl.ds(0, tall)
             pltpu.make_async_copy(own_g.at[0, here], own_out.at[here], out_sem.at[0, index]).wait()
-            pltpu.make_async_copy(other_g.at[0, here], near_out, out_sem.at[1, index]).wait()
+            pltpu.make_async_copy(other_g.at[0, here], other_outs[0], out_sem.at[1, index]).wait()
 
     dims = (micro, length, width)
 
     def arrived(sec):
-        for i, ref in enumerate(own_w):
-            pltpu.make_async_copy(ref, w.at[sec, pl.ds(0, ref.shape[0])], in_sem.at[sec, i]).wait()
+        for i, (ref, (slot, shift, start, tall)) in enumerate(own_w):
+            there = w.at[sec, pl.ds(0, tall)]
+            pltpu.make_async_copy(ref.at[pl.ds(start, tall)], there, in_sem.at[sec, i]).wait()
 
     live_copy.wait()
     x_copy.wait()
@@ -223,21 +239,20 @@
     sent()
 
 
-def run_layers(live, x, target, own, other, places, rows, count, micro, length, width):
+def run_layers(live, x, target, own, other, plan, groups, rows, count, micro, length, width):
     tokens = micro * length
     heads = width // HEAD
     hbm = pl.BlockSpec(memory_space=pl.ANY)
     far = pl.BlockSpec(memory_space=pltpu.HBM)
     first = rows if rows else width
     return pl.pallas_call(
-        functools.partial(layers, micro, length, width, rows, count, places),
+        functools.partial(layers, micro, length, width, rows, count, plan, groups),
         out_shape=(
             jax.ShapeDtypeStruct((4 * width, width), F32),
-            jax.ShapeDtypeStruct((first, width), BF16),
-            jax.ShapeDtypeStruct((4 * width - first, width), BF16),
+            *[jax.ShapeDtypeStruct((blocks * first, width), BF16) for blocks in groups],
         ),
-        in_specs=[far, far, hbm] + [hbm] * (2 * len(own)),
-        out_specs=(hbm, hbm, hbm),
+        in_specs=[far, far, hbm] + [hbm] * (len(own) + len(other)),
+        out_specs=(hbm,) * (1 + len(groups)),
         scratch_shapes=[
             pltpu.SMEM((1, micro), jnp.int32),
             pltpu.VMEM((tokens, width), BF16),
@@ -258,12 +273,12 @@
             pltpu.VMEM((width, tokens), BF16),
             pltpu.VMEM((tokens, width), BF16),
             pltpu.VMEM((tokens, width), BF16),
-            pltpu.SemaphoreType.DMA((2, len(own))),
+            pltpu.SemaphoreType.DMA((2, sum(len(part) for part in plan[0]))),
             pltpu.SemaphoreType.DMA((2, 4 * width // first)),
             pltpu.SemaphoreType.DMA((3,)),
         ],
         compiler_params=pltpu.CompilerParams(vmem_limit_bytes=40 * 1024 * 1024),
-    )(live, x, target, *own, *other)
+    )(pltpu.with_memory_space_constraint(live, pltpu.HBM), pltpu.with_memory_space_constraint(x, pltpu.HBM), target, *own, *other)
 
 
 def swapped(value):
@@ -294,55 +309,56 @@
     target = out_grad[0].reshape(micro * length, width)
     x = inputs[0].reshape(micro * length, width)
     half = rows // 2
+    mid = count // 2
     if ringed:
-        own = [mine]
-        places = [(0, 0)]
+        own, plan_own = [mine], [((0, 0, 0, rows),)]
         fore, aft = mine, mine
-        beside = [target, mine]
-        crossed = []
-        for step in range(1, count // 2 + 1):
-            last = step == count // 2
-            if step > 1:
-                fore, one = lax.optimization_barrier((fore, swapped(beside[0])))
-                aft, two = lax.optimization_barrier((aft, swapped(beside[1])))
-                crossed += [one, two]
-                beside = [own[-2], own[-1]]
+        target, other, plan_other = swapped(target), [swapped(mine)], [((0, 0, 0, rows),)]
+        for step in range(1, mid + 1):
+            last = step == mid
+            size = half if last else rows
             fore, aft = ahead(fore[:half] if last else fore), behind(aft[half:] if last else aft)
             own += [fore, aft]
-            places += [(count - step, 0), (step, half if last else 0)]
-        crossed += [swapped(value) for value in own[-4:]]
-        target, other = crossed[0], crossed[1:]
+            places = ((count - step, 0), (step, half if last else 0))
+            plan_own += [((*place, 0, size),) for place in places]
+            if last:
+                other += [swapped(fore), swapped(aft)]
+                plan_other += [((*place, 0, size),) for place in places]
+            else:
+                other.append(swapped(jnp.concatenate([fore, aft], axis=0)))
+                plan_other.append(tuple((*place, i * size, size) for i, place in enumerate(places)))
     else:
         own = [lax.all_gather(mine, "dp", axis=0, tiled=True)]
-        places = [(0, 0)]
         target, other = swapped(target), [swapped(own[0])]
-    own_g, near_g, rest_g = run_layers(
-        lengths, x, target, own, other, places, rows if ringed else 0, count, micro, length, width
+        plan_own = plan_other = [((0, 0, 0, 4 * width),)]
+    plan = (tuple(plan_own), tuple(plan_other))
+    groups = (1, count - 1) if ringed else (4,)
+    own_g, *far_g = run_layers(
+        lengths, x, target, own, other, plan, groups, rows if ringed else 0, count, micro, length, width
     )
-    near_g = swapped(near_g)
+    far_g[0] = swapped(far_g[0])
     if ringed:
-        mid = count // 2
-        near = (own_g[:rows] + near_g.astype(F32)).astype(BF16)
-        rest_g, near = lax.optimization_barrier((rest_g, near))
+        near = (own_g[:rows] + far_g[0].astype(F32)).astype(BF16)
+        far_g[1], near = lax.optimization_barrier((far_g[1], near))
         fore, aft = ahead(near[:half]), behind(near[half:])
-        rest_g = swapped(rest_g)
+        far = swapped(far_g[1])
 
         def block(index):
-            at = (index + mid) % count * rows
-            return own_g[at : at + rows] + rest_g[at - rows : at].astype(F32)
-
-        up, down = block(mid - 1), block(mid + 1)
-        fore = jnp.concatenate([up[:half] + fore.astype(F32), up[half:]], axis=0).astype(BF16)
-        aft = jnp.concatenate([down[:half], down[half:] + aft.astype(F32)], axis=0).astype(BF16)
-        for step in range(mid - 2, -1, -1):
-            fore, aft = lax.optimization_barrier((fore, aft))
+            at = index * rows
+            return own_g[at : at + rows] + far[at - rows : at].astype(F32)
+
+        for step in range(1, mid):
+            up, down = block(2 * step - 1), block(2 * step)
+            if step == 1:
+                up = jnp.concatenate([up[:half] + fore.astype(F32), up[half:]], axis=0)
+                down = jnp.concatenate([down[:half], down[half:] + aft.astype(F32)], axis=0)
+            else:
+                up, down = up + fore.astype(F32), down + aft.astype(F32)
+            fore, aft = lax.optimization_barrier((up.astype(BF16), down.astype(BF16)))
             fore, aft = ahead(fore), behind(aft)
-            if step:
-                fore = (block(step) + fore.astype(F32)).astype(BF16)
-                aft = (block(count - step) + aft.astype(F32)).astype(BF16)
-        terms = ((own_g, mid * rows), (rest_g, (mid - 1) * rows), (fore, 0), (aft, 0))
+        terms = ((own_g, (count - 1) * rows), (far, (count - 2) * rows), (fore, 0), (aft, 0))
     else:
-        total = own_g + jnp.concatenate([near_g, swapped(rest_g)], axis=0).astype(F32)
+        total = own_g + far_g[0].astype(F32)
         terms = ((lax.psum_scatter(total, "dp", scatter_dimension=0, tiled=True), 0),)
     new_first, new_second, update, squares = run_moments(weights, moment_first[0], moment_second[0], terms)
     if ringed:

time: 106 us -> 99.6 us (0.940)
  waiting for transfers between devices: 55.2 us -> 51.1 us
  local copies, waits for them, and re-layouts: 1.79 us -> 0.1 us
    ppermute x8, waiting for transfers between devices: 24.7 us -> 22.7 us  [behind(): return lax.ppermute(value, 'dp', backward_way)]
    unnamed x10 -> x6, local copies, waits for them, and re-layouts: 1.72 us -> 0.02 us
    ppermute x8, starting transfers between devices: 12.2 us -> 13.8 us  [behind(): return lax.ppermute(value, 'dp', backward_way)]
    ppermute x8, starting transfers between devices: 5.01 us -> 3.84 us  [ahead(): return lax.ppermute(value, 'dp', onward)]
    ppermute x8, waiting for transfers between devices: 18.8 us -> 17.7 us  [ahead(): return lax.ppermute(value, 'dp', onward)]
    ppermute x12 -> x9, waiting for transfers between devices: 4.29 us -> 4.29 us  [swapped(): return lax.ppermute(value, 'pipe', [(0, 1), (1, 0)])]
  transfers between devices with their start and end apart: 31 -> 28, of which waited for: 20 -> 20; matrix products, arithmetic and copies ran while one was open for 1% -> 0% of each run, Pallas kernels for 0% -> 0%
where the time goes in v3:
time: 99.6 us; the launch traced here: 99.5 us
  waiting for transfers between devices  51.1 us (51%)
  starting transfers between devices  24.2 us (24%)
  Pallas kernels  21.1 us (21%)
  other arithmetic  1.96 us (2%)
  between operations  1 us (1%)
    ppermute x8, waiting for transfers between devices, behind(): return lax.ppermute(value, 'dp', backward_way)  22.7 us
    pallas_call x1, Pallas kernels, run_layers(): pl.pallas_call(functools.partial(layers, micro, length, width, rows, coun...  17.9 us
    ppermute x8, waiting for transfers between devices, ahead(): return lax.ppermute(value, 'dp', onward)  17.7 us
    ppermute x8, starting transfers between devices, behind(): return lax.ppermute(value, 'dp', backward_way)  13.8 us
    ppermute x3, waiting for transfers between devices, on_device(): lax.ppermute(squares, 'dp', [(i, i ^ hop) for i in range(count)])  6.33 us
    ppermute x3, starting transfers between devices, on_device(): lax.ppermute(squares, 'dp', [(i, i ^ hop) for i in range(count)])  5.58 us
    ppermute x9, waiting for transfers between devices, swapped(): return lax.ppermute(value, 'pipe', [(0, 1), (1, 0)])  4.29 us
    ppermute x8, starting transfers between devices, ahead(): return lax.ppermute(value, 'dp', onward)  3.84 us
  transfers between devices with their start and end apart: 28, of which 20 were waited for; matrix products, arithmetic and copies ran while one was open for 0% of the time, Pallas kernels for 0%

profile of v3, /device:TPU:0, one launch (start us, length us, event | category | flops | bytes accessed | tf_op | source)
XLA Modules:
  0.0 99.5 jit_solution(2280813480254385127)
XLA Ops:
  0.6 1.1 %bitcast_convert_fusion.refs_0_ = bf16[256,512]{1,0:T(8,128)(2,1)S(1)} fusion(f32[1,256,512]{2,1,0:T(8,128)} %param.9), kind=kLoop, calls=%fused_computation.18 | loop fusion | flops 131072 | bytes 786432 | tf_op jit(solution)/shard_map/convert_element_type | solution.py:308
  1.7 3.0 %collective-permute-start.2 = (bf16[256,512]{1,0:T(8,128)(2,1)S(1)}, bf16[256,512]{1,0:T(8,128)(2,1)S(1)}, u32[]{:S(2)}, u32[]{:S(2)}) collective-permute-start(bf16[256,512]{1,0:T(8,128)(2,1)S(1)} %bitcast_convert_fusion.refs_0_), channel_id=1, source_target_pairs={{4,0},{8,4},{12,8},{14,12},{10,14},{6,10},{2,6},{0,2},{5,1},{9,5},... | collective-permute-start | bytes 786440 | tf_op jit(solution)/shard_map/ppermute | solution.py:306
  4.9 6.2 %collective-permute-done.2.refs_2_ = bf16[256,512]{1,0:T(8,128)(2,1)S(1)} collective-permute-done((bf16[256,512]{1,0:T(8,128)(2,1)S(1)}, bf16[256,512]{1,0:T(8,128)(2,1)S(1)}, u32[]{:S(2)}, u32[]{:S(2)}) %collective-permute-start.2) | collective-permute-done | bytes 262176 | tf_op jit(solution)/shard_map/ppermute | solution.py:306
  11.1 1.7 %collective-permute-start.4 = (bf16[256,512]{1,0:T(8,128)(2,1)S(1)}, bf16[256,512]{1,0:T(8,128)(2,1)S(1)}, u32[]{:S(2)}, u32[]{:S(2)}) collective-permute-start(bf16[256,512]{1,0:T(8,128)(2,1)S(1)} %collective-permute-done.2.refs_2_), channel_id=1, source_target_pairs={{4,0},{8,4},{12,8},{14,12},{10,14},{6,10},{2,6},{0,2},{5,1},{9,5},... | collective-permute-start | bytes 786440 | tf_op jit(solution)/shard_map/ppermute | solution.py:306
  13.1 5.5 %collective-permute-done.4.refs_4_ = bf16[256,512]{1,0:T(8,128)(2,1)S(1)} collective-permute-done((bf16[256,512]{1,0:T(8,128)(2,1)S(1)}, bf16[256,512]{1,0:T(8,128)(2,1)S(1)}, u32[]{:S(2)}, u32[]{:S(2)}) %collective-permute-start.4) | collective-permute-done | bytes 262176 | tf_op jit(solution)/shard_map/ppermute | solution.py:306
  18.6 1.3 %collective-permute-start.6 = (bf16[256,512]{1,0:T(8,128)(2,1)S(1)}, bf16[256,512]{1,0:T(8,128)(2,1)S(1)}, u32[]{:S(2)}, u32[]{:S(2)}) collective-permute-start(bf16[256,512]{1,0:T(8,128)(2,1)S(1)} %collective-permute-done.4.refs_4_), channel_id=1, source_target_pairs={{4,0},{8,4},{12,8},{14,12},{10,14},{6,10},{2,6},{0,2},{5,1},{9,5},... | collective-permute-start | bytes 786440 | tf_op jit(solution)/shard_map/ppermute | solution.py:306
  21.3 3.9 %collective-permute-done.6.refs_6_ = bf16[256,512]{1,0:T(8,128)(2,1)S(1)} collective-permute-done((bf16[256,512]{1,0:T(8,128)(2,1)S(1)}, bf16[256,512]{1,0:T(8,128)(2,1)S(1)}, u32[]{:S(2)}, u32[]{:S(2)}) %collective-permute-start.6) | collective-permute-done | bytes 262176 | tf_op jit(solution)/shard_map/ppermute | solution.py:306
  25.2 1.1 %collective-permute-done.5.refs_5_ = bf16[256,512]{1,0:T(8,128)(2,1)S(1)} collective-permute-done((bf16[256,512]{1,0:T(8,128)(2,1)S(1)}, bf16[256,512]{1,0:T(8,128)(2,1)S(1)}, u32[]{:S(2)}, u32[]{:S(2)}) %collective-permute-start.5) | collective-permute-done | bytes 262176 | tf_op jit(solution)/shard_map/ppermute | solution.py:303
  26.5 1.6 %collective-permute-start.8 = (bf16[128,512]{1,0:T(8,128)(2,1)S(1)}, bf16[128,512]{1,0:T(8,128)(2,1)S(1)}, u32[]{:S(2)}, u32[]{:S(2)}) collective-permute-start(bf16[128,512]{1,0:T(8,128)(2,1)S(1)} %slice.87), channel_id=1, source_target_pairs={{4,0},{8,4},{12,8},{14,12},{10,14},{6,10},{2,6},{0,2},{5,1},{9,5},... | collective-permute-start | bytes 393224 | tf_op jit(solution)/shard_map/ppermute | solution.py:306
  28.5 3.9 %collective-permute-done.8.refs_8_ = bf16[128,512]{1,0:T(8,128)(2,1)S(1)} collective-permute-done((bf16[128,512]{1,0:T(8,128)(2,1)S(1)}, bf16[128,512]{1,0:T(8,128)(2,1)S(1)}, u32[]{:S(2)}, u32[]{:S(2)}) %collective-permute-start.8) | collective-permute-done | bytes 131104 | tf_op jit(solution)/shard_map/ppermute | solution.py:306
  32.4 1.3 %collective-permute-done.7.refs_7_ = bf16[128,512]{1,0:T(8,128)(2,1)S(1)} collective-permute-done((bf16[128,512]{1,0:T(8,128)(2,1)S(1)}, bf16[128,512]{1,0:T(8,128)(2,1)S(1)}, u32[]{:S(2)}, u32[]{:S(2)}) %collective-permute-start.7) | collective-permute-done | bytes 131104 | tf_op jit(solution)/shard_map/ppermute | solution.py:303
  33.8 1.3 %collective-permute-done.13.refs_13_ = bf16[128,512]{1,0:T(8,128)(2,1)S(1)} collective-permute-done((bf16[128,512]{1,0:T(8,128)(2,1)S(1)}, bf16[128,512]{1,0:T(8,128)(2,1)S(1)}, u32[]{:S(2)}, u32[]{:S(2)}) %collective-permute-start.13) | collective-permute-done | bytes 131104 | tf_op jit(solution)/shard_map/ppermute | solution.py:285
  35.1 17.9 %shard_map.85 = (f32[2048,512]{1,0:T(8,128)S(1)}, bf16[256,512]{1,0:T(8,128)(2,1)S(1)}, bf16[1792,512]{1,0:T(8,128)(2,1)S(1)}) custom-call(s32[1,2]{1,0:T(1,128)} %live_in.1, bf16[512,512]{1,0:T(8,128)(2,1)} %bitcast.14, bf16[512,512]{1,0:T(8,128)(2,1)S(1)} %collective-permute-done.g_in, bf16[256,512]{1,0:T(8,128)(2,1)S(1)} %bitcast_convert_fusion.refs_0_, ...), custom_call_target="tpu_custom_call" | custom-call | tf_op jit(solution)/shard_map/pallas_call | solution.py:248
  53.2 1.4 %collective-permute-done.15 = bf16[256,512]{1,0:T(8,128)(2,1)S(1)} collective-permute-done((bf16[256,512]{1,0:T(8,128)(2,1)S(1)}, bf16[256,512]{1,0:T(8,128)(2,1)S(1)}, u32[]{:S(2)}, u32[]{:S(2)}) %collective-permute-start.15) | collective-permute-done | bytes 262176 | tf_op jit(solution)/shard_map/ppermute | solution.py:285
  54.9 1.6 %collective-permute-start.18 = (bf16[128,512]{1,0:T(8,128)(2,1)S(1)}, bf16[128,512]{1,0:T(8,128)(2,1)S(1)}, u32[]{:S(2)}, u32[]{:S(2)}) collective-permute-start(bf16[128,512]{1,0:T(8,128)(2,1)S(1)} %get-tuple-element.39), channel_id=1, source_target_pairs={{4,0},{8,4},{12,8},{14,12},{10,14},{6,10},{2,6},{0,2},{5,1},{9,5},... | collective-permute-start | bytes 393224 | tf_op jit(solution)/shard_map/ppermute | solution.py:306
  57.0 1.5 %collective-permute-done.16.refs_1_ = bf16[1792,512]{1,0:T(8,128)(2,1)S(1)} collective-permute-done((bf16[1792,512]{1,0:T(8,128)(2,1)S(1)}, bf16[1792,512]{1,0:T(8,128)(2,1)S(1)}, u32[]{:S(2)}, u32[]{:S(2)}) %collective-permute-start.16) | collective-permute-done | bytes 1835040 | tf_op jit(solution)/shard_map/ppermute | solution.py:285
  58.8 2.0 %collective-permute-done.18 = bf16[128,512]{1,0:T(8,128)(2,1)S(1)} collective-permute-done((bf16[128,512]{1,0:T(8,128)(2,1)S(1)}, bf16[128,512]{1,0:T(8,128)(2,1)S(1)}, u32[]{:S(2)}, u32[]{:S(2)}) %collective-permute-start.18) | collective-permute-done | bytes 131104 | tf_op jit(solution)/shard_map/ppermute | solution.py:306
  60.8 1.2 %collective-permute-done.17 = bf16[128,512]{1,0:T(8,128)(2,1)S(1)} collective-permute-done((bf16[128,512]{1,0:T(8,128)(2,1)S(1)}, bf16[128,512]{1,0:T(8,128)(2,1)S(1)}, u32[]{:S(2)}, u32[]{:S(2)}) %collective-permute-start.17) | collective-permute-done | bytes 131104 | tf_op jit(solution)/shard_map/ppermute | solution.py:303
  62.6 1.6 %collective-permute-start.20 = (bf16[256,512]{1,0:T(8,128)(2,1)S(1)}, bf16[256,512]{1,0:T(8,128)(2,1)S(1)}, u32[]{:S(2)}, u32[]{:S(2)}) collective-permute-start(bf16[256,512]{1,0:T(8,128)(2,1)S(1)} %pad_maximum_fusion.4), channel_id=1, source_target_pairs={{4,0},{8,4},{12,8},{14,12},{10,14},{6,10},{2,6},{0,2},{5,1},{9,5},... | collective-permute-start | bytes 786440 | tf_op jit(solution)/shard_map/ppermute | solution.py:306
  64.2 5.4 %collective-permute-done.19 = bf16[256,512]{1,0:T(8,128)(2,1)S(1)} collective-permute-done((bf16[256,512]{1,0:T(8,128)(2,1)S(1)}, bf16[256,512]{1,0:T(8,128)(2,1)S(1)}, u32[]{:S(2)}, u32[]{:S(2)}) %collective-permute-start.19) | collective-permute-done | bytes 262176 | tf_op jit(solution)/shard_map/ppermute | solution.py:303
  70.5 1.6 %collective-permute-start.22 = (bf16[256,512]{1,0:T(8,128)(2,1)S(1)}, bf16[256,512]{1,0:T(8,128)(2,1)S(1)}, u32[]{:S(2)}, u32[]{:S(2)}) collective-permute-start(bf16[256,512]{1,0:T(8,128)(2,1)S(1)} %get-tuple-element.26), channel_id=1, source_target_pairs={{4,0},{8,4},{12,8},{14,12},{10,14},{6,10},{2,6},{0,2},{5,1},{9,5},... | collective-permute-start | bytes 786440 | tf_op jit(solution)/shard_map/ppermute | solution.py:306
  72.1 4.3 %collective-permute-done.21 = bf16[256,512]{1,0:T(8,128)(2,1)S(1)} collective-permute-done((bf16[256,512]{1,0:T(8,128)(2,1)S(1)}, bf16[256,512]{1,0:T(8,128)(2,1)S(1)}, u32[]{:S(2)}, u32[]{:S(2)}) %collective-permute-start.21) | collective-permute-done | bytes 262176 | tf_op jit(solution)/shard_map/ppermute | solution.py:303
  77.8 1.3 %collective-permute-start.24 = (bf16[256,512]{1,0:T(8,128)(2,1)S(1)}, bf16[256,512]{1,0:T(8,128)(2,1)S(1)}, u32[]{:S(2)}, u32[]{:S(2)}) collective-permute-start(bf16[256,512]{1,0:T(8,128)(2,1)S(1)} %get-tuple-element.28), channel_id=1, source_target_pairs={{4,0},{8,4},{12,8},{14,12},{10,14},{6,10},{2,6},{0,2},{5,1},{9,5},... | collective-permute-start | bytes 786440 | tf_op jit(solution)/shard_map/ppermute | solution.py:306
  79.1 4.3 %collective-permute-done.23.refs_2_ = bf16[256,512]{1,0:T(8,128)(2,1)S(1)} collective-permute-done((bf16[256,512]{1,0:T(8,128)(2,1)S(1)}, bf16[256,512]{1,0:T(8,128)(2,1)S(1)}, u32[]{:S(2)}, u32[]{:S(2)}) %collective-permute-start.23) | collective-permute-done | bytes 262176 | tf_op jit(solution)/shard_map/ppermute | solution.py:303
  84.2 2.1 %shard_map.86 = (f32[256,512]{1,0:T(8,128)}, f32[256,512]{1,0:T(8,128)}, f32[256,512]{1,0:T(8,128)S(1)}, f32[16,128]{1,0:T(8,128)S(1)}) custom-call(f32[256,512]{1,0:T(8,128)S(1)} %bitcast.9, f32[256,512]{1,0:T(8,128)S(1)} %bitcast.11, f32[256,512]{1,0:T(8,128)S(1)} %bitcast.12, f32[2048,512]{1,0:T(8,128)S(1)} %get-tuple-element.18.refs_0_, ...), custom_call_target="tpu_custom_call" | custom-call | tf_op jit(solution)/shard_map/pallas_call | solution.py:428
  86.3 1.4 %collective-permute-start.25 = (f32[16,128]{1,0:T(8,128)S(1)}, f32[16,128]{1,0:T(8,128)S(1)}, u32[]{:S(2)}, u32[]{:S(2)}) collective-permute-start(f32[16,128]{1,0:T(8,128)S(1)} %get-tuple-element.30), channel_id=1, source_target_pairs={{0,2},{2,0},{4,6},{6,4},{8,10},{10,8},{12,14},{14,12},{1,3},{3,1},... | collective-permute-start | bytes 24584 | tf_op jit(solution)/shard_map/ppermute | solution.py:367
  87.7 2.3 %collective-permute-done.25 = f32[16,128]{1,0:T(8,128)S(1)} collective-permute-done((f32[16,128]{1,0:T(8,128)S(1)}, f32[16,128]{1,0:T(8,128)S(1)}, u32[]{:S(2)}, u32[]{:S(2)}) %collective-permute-start.25) | collective-permute-done | bytes 8224 | tf_op jit(solution)/shard_map/ppermute | solution.py:367
  90.0 1.5 %collective-permute-start.26 = (f32[16,128]{1,0:T(8,128)S(1)}, f32[16,128]{1,0:T(8,128)S(1)}, u32[]{:S(2)}, u32[]{:S(2)}) collective-permute-start(f32[16,128]{1,0:T(8,128)S(1)} %add.58), channel_id=1, source_target_pairs={{0,4},{2,6},{4,0},{6,2},{8,12},{10,14},{12,8},{14,10},{1,5},{3,7},... | collective-permute-start | bytes 24584 | tf_op jit(solution)/shard_map/ppermute | solution.py:367
  91.6 2.1 %collective-permute-done.26 = f32[16,128]{1,0:T(8,128)S(1)} collective-permute-done((f32[16,128]{1,0:T(8,128)S(1)}, f32[16,128]{1,0:T(8,128)S(1)}, u32[]{:S(2)}, u32[]{:S(2)}) %collective-permute-start.26) | collective-permute-done | bytes 8224 | tf_op jit(solution)/shard_map/ppermute | solution.py:367
  93.7 2.6 %collective-permute-start.27 = (f32[16,128]{1,0:T(8,128)S(1)}, f32[16,128]{1,0:T(8,128)S(1)}, u32[]{:S(2)}, u32[]{:S(2)}) collective-permute-start(f32[16,128]{1,0:T(8,128)S(1)} %add.59.refs_0_), channel_id=1, source_target_pairs={{0,8},{2,10},{4,12},{6,14},{8,0},{10,2},{12,4},{14,6},{1,9},{3,11}... | collective-permute-start | bytes 24584 | tf_op jit(solution)/shard_map/ppermute | solution.py:369
  96.3 1.9 %collective-permute-done.27.refs_1_ = f32[16,128]{1,0:T(8,128)S(1)} collective-permute-done((f32[16,128]{1,0:T(8,128)S(1)}, f32[16,128]{1,0:T(8,128)S(1)}, u32[]{:S(2)}, u32[]{:S(2)}) %collective-permute-start.27) | collective-permute-done | bytes 8224 | tf_op jit(solution)/shard_map/ppermute | solution.py:369
  98.2 1.1 %shard_map.87 = f32[256,512]{1,0:T(8,128)} custom-call(f32[256,512]{1,0:T(8,128)S(1)} %bitcast.10, f32[256,512]{1,0:T(8,128)S(1)} %get-tuple-element.29.update_in, f32[16,128]{1,0:T(8,128)S(1)} %add.59.refs_0_, f32[16,128]{1,0:T(8,128)S(1)} %collective-permute-done.27.refs_1_), custom_call_target="tpu_custom_call" | custom-call | tf_op jit(solution)/shard_map/pallas_call | solution.py:479
  (52 shorter events, 7.2 us)
Async XLA Ops:
  1.7 9.4 %collective-permute-start.2 = (bf16[256,512]{1,0:T(8,128)(2,1)S(1)}, bf16[256,512]{1,0:T(8,128)(2,1)S(1)}, u32[]{:S(2)}, u32[]{:S(2)}) collective-permute-start(bf16[256,512]{1,0:T(8,128)(2,1)S(1)} %bitcast_convert_fusion.refs_0_), channel_id=1, source_target_pairs={{4,0},{8,4},{12,8},{14,12},{10,14},{6,10},{2,6},{0,2},{5,1},{9,5},... | collective-permute-start | bytes 786440 | tf_op jit(solution)/shard_map/ppermute | solution.py:306
  4.7 8.0 %collective-permute-start.1 = (bf16[256,512]{1,0:T(8,128)(2,1)S(1)}, bf16[256,512]{1,0:T(8,128)(2,1)S(1)}, u32[]{:S(2)}, u32[]{:S(2)}) collective-permute-start(bf16[256,512]{1,0:T(8,128)(2,1)S(1)} %bitcast_convert_fusion.refs_0_), channel_id=1, source_target_pairs={{0,4},{4,8},{8,12},{12,14},{14,10},{10,6},{6,2},{2,0},{1,5},{5,9},... | collective-permute-start | bytes 786440 | tf_op jit(solution)/shard_map/ppermute | solution.py:303
  11.1 7.5 %collective-permute-start.4 = (bf16[256,512]{1,0:T(8,128)(2,1)S(1)}, bf16[256,512]{1,0:T(8,128)(2,1)S(1)}, u32[]{:S(2)}, u32[]{:S(2)}) collective-permute-start(bf16[256,512]{1,0:T(8,128)(2,1)S(1)} %collective-permute-done.2.refs_2_), channel_id=1, source_target_pairs={{4,0},{8,4},{12,8},{14,12},{10,14},{6,10},{2,6},{0,2},{5,1},{9,5},... | collective-permute-start | bytes 786440 | tf_op jit(solution)/shard_map/ppermute | solution.py:306
  12.7 7.2 %collective-permute-start.3 = (bf16[256,512]{1,0:T(8,128)(2,1)S(1)}, bf16[256,512]{1,0:T(8,128)(2,1)S(1)}, u32[]{:S(2)}, u32[]{:S(2)}) collective-permute-start(bf16[256,512]{1,0:T(8,128)(2,1)S(1)} %collective-permute-done.1.refs_1_), channel_id=1, source_target_pairs={{0,4},{4,8},{8,12},{12,14},{14,10},{10,6},{6,2},{2,0},{1,5},{5,9},... | collective-permute-start | bytes 786440 | tf_op jit(solution)/shard_map/ppermute | solution.py:303
  18.6 6.6 %collective-permute-start.6 = (bf16[256,512]{1,0:T(8,128)(2,1)S(1)}, bf16[256,512]{1,0:T(8,128)(2,1)S(1)}, u32[]{:S(2)}, u32[]{:S(2)}) collective-permute-start(bf16[256,512]{1,0:T(8,128)(2,1)S(1)} %collective-permute-done.4.refs_4_), channel_id=1, source_target_pairs={{4,0},{8,4},{12,8},{14,12},{10,14},{6,10},{2,6},{0,2},{5,1},{9,5},... | collective-permute-start | bytes 786440 | tf_op jit(solution)/shard_map/ppermute | solution.py:306
  19.9 6.4 %collective-permute-start.5 = (bf16[256,512]{1,0:T(8,128)(2,1)S(1)}, bf16[256,512]{1,0:T(8,128)(2,1)S(1)}, u32[]{:S(2)}, u32[]{:S(2)}) collective-permute-start(bf16[256,512]{1,0:T(8,128)(2,1)S(1)} %collective-permute-done.3.refs_3_), channel_id=1, source_target_pairs={{0,4},{4,8},{8,12},{12,14},{14,10},{10,6},{6,2},{2,0},{1,5},{5,9},... | collective-permute-start | bytes 786440 | tf_op jit(solution)/shard_map/ppermute | solution.py:303
  20.6 5.8 %collective-permute-start.9 = (bf16[256,512]{1,0:T(8,128)(2,1)S(1)}, bf16[256,512]{1,0:T(8,128)(2,1)S(1)}, u32[]{:S(2)}, u32[]{:S(2)}) collective-permute-start(bf16[256,512]{1,0:T(8,128)(2,1)S(1)} %bitcast_convert_fusion.refs_0_), channel_id=1, source_target_pairs={{0,1},{1,0},{2,3},{3,2},{4,5},{5,4},{6,7},{7,6},{8,9},{9,8},{10,11... | collective-permute-start | bytes 786440 | tf_op jit(solution)/shard_map/ppermute | solution.py:285
  20.6 7.5 %collective-permute-start = (bf16[512,512]{1,0:T(8,128)(2,1)}, bf16[512,512]{1,0:T(8,128)(2,1)S(1)}, u32[]{:S(2)}, u32[]{:S(2)}) collective-permute-start(bf16[512,512]{1,0:T(8,128)(2,1)} %bitcast.15), channel_id=1, source_target_pairs={{0,1},{1,0},{2,3},{3,2},{4,5},{5,4},{6,7},{7,6},{8,9},{9,8},{10,11... | collective-permute-start | bytes 1572872 | tf_op jit(solution)/shard_map/ppermute | solution.py:285
  21.2 12.6 %collective-permute-start.10 = (bf16[512,512]{1,0:T(8,128)(2,1)S(1)}, bf16[512,512]{1,0:T(8,128)(2,1)S(1)}, u32[]{:S(2)}, u32[]{:S(2)}) collective-permute-start(bf16[512,512]{1,0:T(8,128)(2,1)S(1)} %pad_maximum_fusion), channel_id=1, source_target_pairs={{0,1},{1,0},{2,3},{3,2},{4,5},{5,4},{6,7},{7,6},{8,9},{9,8},{10,11... | collective-permute-start | bytes 1572872 | tf_op jit(solution)/shard_map/ppermute | solution.py:285
  25.2 9.9 %collective-permute-start.11 = (bf16[512,512]{1,0:T(8,128)(2,1)S(1)}, bf16[512,512]{1,0:T(8,128)(2,1)S(1)}, u32[]{:S(2)}, u32[]{:S(2)}) collective-permute-start(bf16[512,512]{1,0:T(8,128)(2,1)S(1)} %pad_maximum_fusion.1), channel_id=1, source_target_pairs={{0,1},{1,0},{2,3},{3,2},{4,5},{5,4},{6,7},{7,6},{8,9},{9,8},{10,11... | collective-permute-start | bytes 1572872 | tf_op jit(solution)/shard_map/ppermute | solution.py:285
  26.3 8.7 %collective-permute-start.12 = (bf16[512,512]{1,0:T(8,128)(2,1)S(1)}, bf16[512,512]{1,0:T(8,128)(2,1)S(1)}, u32[]{:S(2)}, u32[]{:S(2)}) collective-permute-start(bf16[512,512]{1,0:T(8,128)(2,1)S(1)} %pad_maximum_fusion.2), channel_id=1, source_target_pairs={{0,1},{1,0},{2,3},{3,2},{4,5},{5,4},{6,7},{7,6},{8,9},{9,8},{10,11... | collective-permute-start | bytes 1572872 | tf_op jit(solution)/shard_map/ppermute | solution.py:285
  26.5 5.9 %collective-permute-start.8 = (bf16[128,512]{1,0:T(8,128)(2,1)S(1)}, bf16[128,512]{1,0:T(8,128)(2,1)S(1)}, u32[]{:S(2)}, u32[]{:S(2)}) collective-permute-start(bf16[128,512]{1,0:T(8,128)(2,1)S(1)} %slice.87), channel_id=1, source_target_pairs={{4,0},{8,4},{12,8},{14,12},{10,14},{6,10},{2,6},{0,2},{5,1},{9,5},... | collective-permute-start | bytes 393224 | tf_op jit(solution)/shard_map/ppermute | solution.py:306
  28.1 5.6 %collective-permute-start.7 = (bf16[128,512]{1,0:T(8,128)(2,1)S(1)}, bf16[128,512]{1,0:T(8,128)(2,1)S(1)}, u32[]{:S(2)}, u32[]{:S(2)}) collective-permute-start(bf16[128,512]{1,0:T(8,128)(2,1)S(1)} %slice.86), channel_id=1, source_target_pairs={{0,4},{4,8},{8,12},{12,14},{14,10},{10,6},{6,2},{2,0},{1,5},{5,9},... | collective-permute-start | bytes 393224 | tf_op jit(solution)/shard_map/ppermute | solution.py:303
  32.4 1.3 %collective-permute-start.14 = (bf16[128,512]{1,0:T(8,128)(2,1)S(1)}, bf16[128,512]{1,0:T(8,128)(2,1)S(1)}, u32[]{:S(2)}, u32[]{:S(2)}) collective-permute-start(bf16[128,512]{1,0:T(8,128)(2,1)S(1)} %collective-permute-done.8.refs_8_), channel_id=1, source_target_pairs={{0,1},{1,0},{2,3},{3,2},{4,5},{5,4},{6,7},{7,6},{8,9},{9,8},{10,11... | collective-permute-start | bytes 393224 | tf_op jit(solution)/shard_map/ppermute | solution.py:285
  33.7 1.3 %collective-permute-start.13 = (bf16[128,512]{1,0:T(8,128)(2,1)S(1)}, bf16[128,512]{1,0:T(8,128)(2,1)S(1)}, u32[]{:S(2)}, u32[]{:S(2)}) collective-permute-start(bf16[128,512]{1,0:T(8,128)(2,1)S(1)} %collective-permute-done.7.refs_7_), channel_id=1, source_target_pairs={{0,1},{1,0},{2,3},{3,2},{4,5},{5,4},{6,7},{7,6},{8,9},{9,8},{10,11... | collective-permute-start | bytes 393224 | tf_op jit(solution)/shard_map/ppermute | solution.py:285
  53.0 1.6 %collective-permute-start.15 = (bf16[256,512]{1,0:T(8,128)(2,1)S(1)}, bf16[256,512]{1,0:T(8,128)(2,1)S(1)}, u32[]{:S(2)}, u32[]{:S(2)}) collective-permute-start(bf16[256,512]{1,0:T(8,128)(2,1)S(1)} %get-tuple-element.20), channel_id=1, source_target_pairs={{0,1},{1,0},{2,3},{3,2},{4,5},{5,4},{6,7},{7,6},{8,9},{9,8},{10,11... | collective-permute-start | bytes 786440 | tf_op jit(solution)/shard_map/ppermute | solution.py:285
  54.7 3.9 %collective-permute-start.16 = (bf16[1792,512]{1,0:T(8,128)(2,1)S(1)}, bf16[1792,512]{1,0:T(8,128)(2,1)S(1)}, u32[]{:S(2)}, u32[]{:S(2)}) collective-permute-start(bf16[1792,512]{1,0:T(8,128)(2,1)S(1)} %get-tuple-element.21), channel_id=1, source_target_pairs={{0,1},{1,0},{2,3},{3,2},{4,5},{5,4},{6,7},{7,6},{8,9},{9,8},{10,11... | collective-permute-start | bytes 5505032 | tf_op jit(solution)/shard_map/ppermute | solution.py:285
  54.9 5.8 %collective-permute-start.18 = (bf16[128,512]{1,0:T(8,128)(2,1)S(1)}, bf16[128,512]{1,0:T(8,128)(2,1)S(1)}, u32[]{:S(2)}, u32[]{:S(2)}) collective-permute-start(bf16[128,512]{1,0:T(8,128)(2,1)S(1)} %get-tuple-element.39), channel_id=1, source_target_pairs={{4,0},{8,4},{12,8},{14,12},{10,14},{6,10},{2,6},{0,2},{5,1},{9,5},... | collective-permute-start | bytes 393224 | tf_op jit(solution)/shard_map/ppermute | solution.py:306
  56.6 5.5 %collective-permute-start.17 = (bf16[128,512]{1,0:T(8,128)(2,1)S(1)}, bf16[128,512]{1,0:T(8,128)(2,1)S(1)}, u32[]{:S(2)}, u32[]{:S(2)}) collective-permute-start(bf16[128,512]{1,0:T(8,128)(2,1)S(1)} %get-tuple-element.40), channel_id=1, source_target_pairs={{0,4},{4,8},{8,12},{12,14},{14,10},{10,6},{6,2},{2,0},{1,5},{5,9},... | collective-permute-start | bytes 393224 | tf_op jit(solution)/shard_map/ppermute | solution.py:303
  58.7 25.5 %copy-start = (f32[1,256,512]{2,1,0:T(8,128)S(1)}, f32[1,256,512]{2,1,0:T(8,128)}, u32[]{:S(2)}) copy-start(f32[1,256,512]{2,1,0:T(8,128)} %param.9) | copy-start | bytes 1572868
  58.7 25.5 %copy-start.1 = (f32[1,256,512]{2,1,0:T(8,128)S(1)}, f32[1,256,512]{2,1,0:T(8,128)}, u32[]{:S(2)}) copy-start(f32[1,256,512]{2,1,0:T(8,128)} %param.10) | copy-start | bytes 1572868
  58.7 25.4 %copy-start.2 = (f32[1,256,512]{2,1,0:T(8,128)S(1)}, f32[1,256,512]{2,1,0:T(8,128)}, u32[]{:S(2)}) copy-start(f32[1,256,512]{2,1,0:T(8,128)} %param.11) | copy-start | bytes 1572868
  62.1 7.5 %collective-permute-start.19 = (bf16[256,512]{1,0:T(8,128)(2,1)S(1)}, bf16[256,512]{1,0:T(8,128)(2,1)S(1)}, u32[]{:S(2)}, u32[]{:S(2)}) collective-permute-start(bf16[256,512]{1,0:T(8,128)(2,1)S(1)} %pad_maximum_fusion.3), channel_id=1, source_target_pairs={{0,4},{4,8},{8,12},{12,14},{14,10},{10,6},{6,2},{2,0},{1,5},{5,9},... | collective-permute-start | bytes 786440 | tf_op jit(solution)/shard_map/ppermute | solution.py:303
  62.6 7.2 %collective-permute-start.20 = (bf16[256,512]{1,0:T(8,128)(2,1)S(1)}, bf16[256,512]{1,0:T(8,128)(2,1)S(1)}, u32[]{:S(2)}, u32[]{:S(2)}) collective-permute-start(bf16[256,512]{1,0:T(8,128)(2,1)S(1)} %pad_maximum_fusion.4), channel_id=1, source_target_pairs={{4,0},{8,4},{12,8},{14,12},{10,14},{6,10},{2,6},{0,2},{5,1},{9,5},... | collective-permute-start | bytes 786440 | tf_op jit(solution)/shard_map/ppermute | solution.py:306
  70.0 6.4 %collective-permute-start.21 = (bf16[256,512]{1,0:T(8,128)(2,1)S(1)}, bf16[256,512]{1,0:T(8,128)(2,1)S(1)}, u32[]{:S(2)}, u32[]{:S(2)}) collective-permute-start(bf16[256,512]{1,0:T(8,128)(2,1)S(1)} %get-tuple-element.25), channel_id=1, source_target_pairs={{0,4},{4,8},{8,12},{12,14},{14,10},{10,6},{6,2},{2,0},{1,5},{5,9},... | collective-permute-start | bytes 786440 | tf_op jit(solution)/shard_map/ppermute | solution.py:303
  70.5 6.4 %collective-permute-start.22 = (bf16[256,512]{1,0:T(8,128)(2,1)S(1)}, bf16[256,512]{1,0:T(8,128)(2,1)S(1)}, u32[]{:S(2)}, u32[]{:S(2)}) collective-permute-start(bf16[256,512]{1,0:T(8,128)(2,1)S(1)} %get-tuple-element.26), channel_id=1, source_target_pairs={{4,0},{8,4},{12,8},{14,12},{10,14},{6,10},{2,6},{0,2},{5,1},{9,5},... | collective-permute-start | bytes 786440 | tf_op jit(solution)/shard_map/ppermute | solution.py:306
  77.1 6.4 %collective-permute-start.23 = (bf16[256,512]{1,0:T(8,128)(2,1)S(1)}, bf16[256,512]{1,0:T(8,128)(2,1)S(1)}, u32[]{:S(2)}, u32[]{:S(2)}) collective-permute-start(bf16[256,512]{1,0:T(8,128)(2,1)S(1)} %get-tuple-element.27), channel_id=1, source_target_pairs={{0,4},{4,8},{8,12},{12,14},{14,10},{10,6},{6,2},{2,0},{1,5},{5,9},... | collective-permute-start | bytes 786440 | tf_op jit(solution)/shard_map/ppermute | solution.py:303
  77.8 6.4 %collective-permute-start.24 = (bf16[256,512]{1,0:T(8,128)(2,1)S(1)}, bf16[256,512]{1,0:T(8,128)(2,1)S(1)}, u32[]{:S(2)}, u32[]{:S(2)}) collective-permute-start(bf16[256,512]{1,0:T(8,128)(2,1)S(1)} %get-tuple-element.28), channel_id=1, source_target_pairs={{4,0},{8,4},{12,8},{14,12},{10,14},{6,10},{2,6},{0,2},{5,1},{9,5},... | collective-permute-start | bytes 786440 | tf_op jit(solution)/shard_map/ppermute | solution.py:306
  86.3 3.7 %collective-permute-start.25 = (f32[16,128]{1,0:T(8,128)S(1)}, f32[16,128]{1,0:T(8,128)S(1)}, u32[]{:S(2)}, u32[]{:S(2)}) collective-permute-start(f32[16,128]{1,0:T(8,128)S(1)} %get-tuple-element.30), channel_id=1, source_target_pairs={{0,2},{2,0},{4,6},{6,4},{8,10},{10,8},{12,14},{14,12},{1,3},{3,1},... | collective-permute-start | bytes 24584 | tf_op jit(solution)/shard_map/ppermute | solution.py:367
  90.0 3.7 %collective-permute-start.26 = (f32[16,128]{1,0:T(8,128)S(1)}, f32[16,128]{1,0:T(8,128)S(1)}, u32[]{:S(2)}, u32[]{:S(2)}) collective-permute-start(f32[16,128]{1,0:T(8,128)S(1)} %add.58), channel_id=1, source_target_pairs={{0,4},{2,6},{4,0},{6,2},{8,12},{10,14},{12,8},{14,10},{1,5},{3,7},... | collective-permute-start | bytes 24584 | tf_op jit(solution)/shard_map/ppermute | solution.py:367
  93.7 4.5 %collective-permute-start.27 = (f32[16,128]{1,0:T(8,128)S(1)}, f32[16,128]{1,0:T(8,128)S(1)}, u32[]{:S(2)}, u32[]{:S(2)}) collective-permute-start(f32[16,128]{1,0:T(8,128)S(1)} %add.59.refs_0_), channel_id=1, source_target_pairs={{0,8},{2,10},{4,12},{6,14},{8,0},{10,2},{12,4},{14,6},{1,9},{3,11}... | collective-permute-start | bytes 24584 | tf_op jit(solution)/shard_map/ppermute | solution.py:369

commit v4 on v3

--- a/solution.py
+++ b/solution.py
@@ -9,8 +9,8 @@
 
 HEAD = 64
 PAIR = 128
-AHEAD = 4
-CUTS = 4
+AHEAD = 6
+CUTS = 1
 STEP = 10
 F32 = jnp.float32
 BF16 = jnp.bfloat16

time: 99.6 us -> 98.4 us (0.988)
  Pallas kernels: 21.1 us -> 19.8 us
where the time goes in v4:
time: 98.4 us; the launch traced here: 98.2 us
  waiting for transfers between devices  50.9 us (52%)
  starting transfers between devices  24.4 us (25%)
  Pallas kernels  19.8 us (20%)
  other arithmetic  1.96 us (2%)
  between operations  1 us (1%)
    ppermute x8, waiting for transfers between devices, behind(): return lax.ppermute(value, 'dp', backward_way)  22.7 us
    ppermute x8, waiting for transfers between devices, ahead(): return lax.ppermute(value, 'dp', onward)  17.8 us
    pallas_call x1, Pallas kernels, run_layers(): pl.pallas_call(functools.partial(layers, micro, length, width, rows, coun...  17.3 us
    ppermute x8, starting transfers between devices, behind(): return lax.ppermute(value, 'dp', backward_way)  13.8 us
    ppermute x3, waiting for transfers between devices, on_device(): lax.ppermute(squares, 'dp', [(i, i ^ hop) for i in range(count)])  6.23 us
    ppermute x3, starting transfers between devices, on_device(): lax.ppermute(squares, 'dp', [(i, i ^ hop) for i in range(count)])  5.68 us
    ppermute x9, waiting for transfers between devices, swapped(): return lax.ppermute(value, 'pipe', [(0, 1), (1, 0)])  4.25 us
    ppermute x8, starting transfers between devices, ahead(): return lax.ppermute(value, 'dp', onward)  3.81 us
  transfers between devices with their start and end apart: 28, of which 20 were waited for; matrix products, arithmetic and copies ran while one was open for 0% of the time, Pallas kernels for 0%

profile of v4, /device:TPU:0, one launch (start us, length us, event | category | flops | bytes accessed | tf_op | source)
XLA Modules:
  0.0 98.2 jit_solution(4443978240794086476)
XLA Ops:
  0.6 1.1 %bitcast_convert_fusion.refs_0_ = bf16[256,512]{1,0:T(8,128)(2,1)S(1)} fusion(f32[1,256,512]{2,1,0:T(8,128)} %param.9), kind=kLoop, calls=%fused_computation.18 | loop fusion | flops 131072 | bytes 786432 | tf_op jit(solution)/shard_map/convert_element_type | solution.py:308
  1.7 3.0 %collective-permute-start.2 = (bf16[256,512]{1,0:T(8,128)(2,1)S(1)}, bf16[256,512]{1,0:T(8,128)(2,1)S(1)}, u32[]{:S(2)}, u32[]{:S(2)}) collective-permute-start(bf16[256,512]{1,0:T(8,128)(2,1)S(1)} %bitcast_convert_fusion.refs_0_), channel_id=1, source_target_pairs={{4,0},{8,4},{12,8},{14,12},{10,14},{6,10},{2,6},{0,2},{5,1},{9,5},... | collective-permute-start | bytes 786440 | tf_op jit(solution)/shard_map/ppermute | solution.py:306
  4.9 6.2 %collective-permute-done.2.refs_2_ = bf16[256,512]{1,0:T(8,128)(2,1)S(1)} collective-permute-done((bf16[256,512]{1,0:T(8,128)(2,1)S(1)}, bf16[256,512]{1,0:T(8,128)(2,1)S(1)}, u32[]{:S(2)}, u32[]{:S(2)}) %collective-permute-start.2) | collective-permute-done | bytes 262176 | tf_op jit(solution)/shard_map/ppermute | solution.py:306
  11.1 1.7 %collective-permute-start.4 = (bf16[256,512]{1,0:T(8,128)(2,1)S(1)}, bf16[256,512]{1,0:T(8,128)(2,1)S(1)}, u32[]{:S(2)}, u32[]{:S(2)}) collective-permute-start(bf16[256,512]{1,0:T(8,128)(2,1)S(1)} %collective-permute-done.2.refs_2_), channel_id=1, source_target_pairs={{4,0},{8,4},{12,8},{14,12},{10,14},{6,10},{2,6},{0,2},{5,1},{9,5},... | collective-permute-start | bytes 786440 | tf_op jit(solution)/shard_map/ppermute | solution.py:306
  13.1 5.5 %collective-permute-done.4.refs_4_ = bf16[256,512]{1,0:T(8,128)(2,1)S(1)} collective-permute-done((bf16[256,512]{1,0:T(8,128)(2,1)S(1)}, bf16[256,512]{1,0:T(8,128)(2,1)S(1)}, u32[]{:S(2)}, u32[]{:S(2)}) %collective-permute-start.4) | collective-permute-done | bytes 262176 | tf_op jit(solution)/shard_map/ppermute | solution.py:306
  18.6 1.3 %collective-permute-start.6 = (bf16[256,512]{1,0:T(8,128)(2,1)S(1)}, bf16[256,512]{1,0:T(8,128)(2,1)S(1)}, u32[]{:S(2)}, u32[]{:S(2)}) collective-permute-start(bf16[256,512]{1,0:T(8,128)(2,1)S(1)} %collective-permute-done.4.refs_4_), channel_id=1, source_target_pairs={{4,0},{8,4},{12,8},{14,12},{10,14},{6,10},{2,6},{0,2},{5,1},{9,5},... | collective-permute-start | bytes 786440 | tf_op jit(solution)/shard_map/ppermute | solution.py:306
  21.3 3.9 %collective-permute-done.6.refs_6_ = bf16[256,512]{1,0:T(8,128)(2,1)S(1)} collective-permute-done((bf16[256,512]{1,0:T(8,128)(2,1)S(1)}, bf16[256,512]{1,0:T(8,128)(2,1)S(1)}, u32[]{:S(2)}, u32[]{:S(2)}) %collective-permute-start.6) | collective-permute-done | bytes 262176 | tf_op jit(solution)/shard_map/ppermute | solution.py:306
  25.2 1.1 %collective-permute-done.5.refs_5_ = bf16[256,512]{1,0:T(8,128)(2,1)S(1)} collective-permute-done((bf16[256,512]{1,0:T(8,128)(2,1)S(1)}, bf16[256,512]{1,0:T(8,128)(2,1)S(1)}, u32[]{:S(2)}, u32[]{:S(2)}) %collective-permute-start.5) | collective-permute-done | bytes 262176 | tf_op jit(solution)/shard_map/ppermute | solution.py:303
  26.5 1.6 %collective-permute-start.8 = (bf16[128,512]{1,0:T(8,128)(2,1)S(1)}, bf16[128,512]{1,0:T(8,128)(2,1)S(1)}, u32[]{:S(2)}, u32[]{:S(2)}) collective-permute-start(bf16[128,512]{1,0:T(8,128)(2,1)S(1)} %slice.87), channel_id=1, source_target_pairs={{4,0},{8,4},{12,8},{14,12},{10,14},{6,10},{2,6},{0,2},{5,1},{9,5},... | collective-permute-start | bytes 393224 | tf_op jit(solution)/shard_map/ppermute | solution.py:306
  28.5 3.9 %collective-permute-done.8.refs_8_ = bf16[128,512]{1,0:T(8,128)(2,1)S(1)} collective-permute-done((bf16[128,512]{1,0:T(8,128)(2,1)S(1)}, bf16[128,512]{1,0:T(8,128)(2,1)S(1)}, u32[]{:S(2)}, u32[]{:S(2)}) %collective-permute-start.8) | collective-permute-done | bytes 131104 | tf_op jit(solution)/shard_map/ppermute | solution.py:306
  32.4 1.3 %collective-permute-done.7.refs_7_ = bf16[128,512]{1,0:T(8,128)(2,1)S(1)} collective-permute-done((bf16[128,512]{1,0:T(8,128)(2,1)S(1)}, bf16[128,512]{1,0:T(8,128)(2,1)S(1)}, u32[]{:S(2)}, u32[]{:S(2)}) %collective-permute-start.7) | collective-permute-done | bytes 131104 | tf_op jit(solution)/shard_map/ppermute | solution.py:303
  33.8 1.3 %collective-permute-done.13.refs_13_ = bf16[128,512]{1,0:T(8,128)(2,1)S(1)} collective-permute-done((bf16[128,512]{1,0:T(8,128)(2,1)S(1)}, bf16[128,512]{1,0:T(8,128)(2,1)S(1)}, u32[]{:S(2)}, u32[]{:S(2)}) %collective-permute-start.13) | collective-permute-done | bytes 131104 | tf_op jit(solution)/shard_map/ppermute | solution.py:285
  35.1 17.3 %shard_map.85 = (f32[2048,512]{1,0:T(8,128)S(1)}, bf16[256,512]{1,0:T(8,128)(2,1)S(1)}, bf16[1792,512]{1,0:T(8,128)(2,1)S(1)}) custom-call(s32[1,2]{1,0:T(1,128)} %live_in.1, bf16[512,512]{1,0:T(8,128)(2,1)} %bitcast.14, bf16[512,512]{1,0:T(8,128)(2,1)S(1)} %collective-permute-done.g_in, bf16[256,512]{1,0:T(8,128)(2,1)S(1)} %bitcast_convert_fusion.refs_0_, ...), custom_call_target="tpu_custom_call" | custom-call | tf_op jit(solution)/shard_map/pallas_call | solution.py:248
  52.6 1.4 %collective-permute-done.15 = bf16[256,512]{1,0:T(8,128)(2,1)S(1)} collective-permute-done((bf16[256,512]{1,0:T(8,128)(2,1)S(1)}, bf16[256,512]{1,0:T(8,128)(2,1)S(1)}, u32[]{:S(2)}, u32[]{:S(2)}) %collective-permute-start.15) | collective-permute-done | bytes 262176 | tf_op jit(solution)/shard_map/ppermute | solution.py:285
  54.3 1.6 %collective-permute-start.18 = (bf16[128,512]{1,0:T(8,128)(2,1)S(1)}, bf16[128,512]{1,0:T(8,128)(2,1)S(1)}, u32[]{:S(2)}, u32[]{:S(2)}) collective-permute-start(bf16[128,512]{1,0:T(8,128)(2,1)S(1)} %get-tuple-element.39), channel_id=1, source_target_pairs={{4,0},{8,4},{12,8},{14,12},{10,14},{6,10},{2,6},{0,2},{5,1},{9,5},... | collective-permute-start | bytes 393224 | tf_op jit(solution)/shard_map/ppermute | solution.py:306
  56.4 1.5 %collective-permute-done.16.refs_1_ = bf16[1792,512]{1,0:T(8,128)(2,1)S(1)} collective-permute-done((bf16[1792,512]{1,0:T(8,128)(2,1)S(1)}, bf16[1792,512]{1,0:T(8,128)(2,1)S(1)}, u32[]{:S(2)}, u32[]{:S(2)}) %collective-permute-start.16) | collective-permute-done | bytes 1835040 | tf_op jit(solution)/shard_map/ppermute | solution.py:285
  58.1 2.0 %collective-permute-done.18 = bf16[128,512]{1,0:T(8,128)(2,1)S(1)} collective-permute-done((bf16[128,512]{1,0:T(8,128)(2,1)S(1)}, bf16[128,512]{1,0:T(8,128)(2,1)S(1)}, u32[]{:S(2)}, u32[]{:S(2)}) %collective-permute-start.18) | collective-permute-done | bytes 131104 | tf_op jit(solution)/shard_map/ppermute | solution.py:306
  60.2 1.2 %collective-permute-done.17 = bf16[128,512]{1,0:T(8,128)(2,1)S(1)} collective-permute-done((bf16[128,512]{1,0:T(8,128)(2,1)S(1)}, bf16[128,512]{1,0:T(8,128)(2,1)S(1)}, u32[]{:S(2)}, u32[]{:S(2)}) %collective-permute-start.17) | collective-permute-done | bytes 131104 | tf_op jit(solution)/shard_map/ppermute | solution.py:303
  62.0 1.6 %collective-permute-start.20 = (bf16[256,512]{1,0:T(8,128)(2,1)S(1)}, bf16[256,512]{1,0:T(8,128)(2,1)S(1)}, u32[]{:S(2)}, u32[]{:S(2)}) collective-permute-start(bf16[256,512]{1,0:T(8,128)(2,1)S(1)} %pad_maximum_fusion.4), channel_id=1, source_target_pairs={{4,0},{8,4},{12,8},{14,12},{10,14},{6,10},{2,6},{0,2},{5,1},{9,5},... | collective-permute-start | bytes 786440 | tf_op jit(solution)/shard_map/ppermute | solution.py:306
  63.5 5.4 %collective-permute-done.19 = bf16[256,512]{1,0:T(8,128)(2,1)S(1)} collective-permute-done((bf16[256,512]{1,0:T(8,128)(2,1)S(1)}, bf16[256,512]{1,0:T(8,128)(2,1)S(1)}, u32[]{:S(2)}, u32[]{:S(2)}) %collective-permute-start.19) | collective-permute-done | bytes 262176 | tf_op jit(solution)/shard_map/ppermute | solution.py:303
  69.8 1.6 %collective-permute-start.22 = (bf16[256,512]{1,0:T(8,128)(2,1)S(1)}, bf16[256,512]{1,0:T(8,128)(2,1)S(1)}, u32[]{:S(2)}, u32[]{:S(2)}) collective-permute-start(bf16[256,512]{1,0:T(8,128)(2,1)S(1)} %get-tuple-element.26), channel_id=1, source_target_pairs={{4,0},{8,4},{12,8},{14,12},{10,14},{6,10},{2,6},{0,2},{5,1},{9,5},... | collective-permute-start | bytes 786440 | tf_op jit(solution)/shard_map/ppermute | solution.py:306
  71.4 4.4 %collective-permute-done.21 = bf16[256,512]{1,0:T(8,128)(2,1)S(1)} collective-permute-done((bf16[256,512]{1,0:T(8,128)(2,1)S(1)}, bf16[256,512]{1,0:T(8,128)(2,1)S(1)}, u32[]{:S(2)}, u32[]{:S(2)}) %collective-permute-start.21) | collective-permute-done | bytes 262176 | tf_op jit(solution)/shard_map/ppermute | solution.py:303
  77.1 1.3 %collective-permute-start.24 = (bf16[256,512]{1,0:T(8,128)(2,1)S(1)}, bf16[256,512]{1,0:T(8,128)(2,1)S(1)}, u32[]{:S(2)}, u32[]{:S(2)}) collective-permute-start(bf16[256,512]{1,0:T(8,128)(2,1)S(1)} %get-tuple-element.28), channel_id=1, source_target_pairs={{4,0},{8,4},{12,8},{14,12},{10,14},{6,10},{2,6},{0,2},{5,1},{9,5},... | collective-permute-start | bytes 786440 | tf_op jit(solution)/shard_map/ppermute | solution.py:306
  78.5 4.3 %collective-permute-done.23.refs_2_ = bf16[256,512]{1,0:T(8,128)(2,1)S(1)} collective-permute-done((bf16[256,512]{1,0:T(8,128)(2,1)S(1)}, bf16[256,512]{1,0:T(8,128)(2,1)S(1)}, u32[]{:S(2)}, u32[]{:S(2)}) %collective-permute-start.23) | collective-permute-done | bytes 262176 | tf_op jit(solution)/shard_map/ppermute | solution.py:303
  83.5 1.4 %shard_map.86 = (f32[256,512]{1,0:T(8,128)}, f32[256,512]{1,0:T(8,128)}, f32[256,512]{1,0:T(8,128)S(1)}, f32[16,128]{1,0:T(8,128)S(1)}) custom-call(f32[256,512]{1,0:T(8,128)S(1)} %bitcast.9, f32[256,512]{1,0:T(8,128)S(1)} %bitcast.11, f32[256,512]{1,0:T(8,128)S(1)} %bitcast.12, f32[2048,512]{1,0:T(8,128)S(1)} %get-tuple-element.18.refs_0_, ...), custom_call_target="tpu_custom_call" | custom-call | tf_op jit(solution)/shard_map/pallas_call | solution.py:428
  85.0 1.5 %collective-permute-start.25 = (f32[16,128]{1,0:T(8,128)S(1)}, f32[16,128]{1,0:T(8,128)S(1)}, u32[]{:S(2)}, u32[]{:S(2)}) collective-permute-start(f32[16,128]{1,0:T(8,128)S(1)} %get-tuple-element.30), channel_id=1, source_target_pairs={{0,2},{2,0},{4,6},{6,4},{8,10},{10,8},{12,14},{14,12},{1,3},{3,1},... | collective-permute-start | bytes 24584 | tf_op jit(solution)/shard_map/ppermute | solution.py:367
  86.5 2.2 %collective-permute-done.25 = f32[16,128]{1,0:T(8,128)S(1)} collective-permute-done((f32[16,128]{1,0:T(8,128)S(1)}, f32[16,128]{1,0:T(8,128)S(1)}, u32[]{:S(2)}, u32[]{:S(2)}) %collective-permute-start.25) | collective-permute-done | bytes 8224 | tf_op jit(solution)/shard_map/ppermute | solution.py:367
  88.7 1.6 %collective-permute-start.26 = (f32[16,128]{1,0:T(8,128)S(1)}, f32[16,128]{1,0:T(8,128)S(1)}, u32[]{:S(2)}, u32[]{:S(2)}) collective-permute-start(f32[16,128]{1,0:T(8,128)S(1)} %add.58), channel_id=1, source_target_pairs={{0,4},{2,6},{4,0},{6,2},{8,12},{10,14},{12,8},{14,10},{1,5},{3,7},... | collective-permute-start | bytes 24584 | tf_op jit(solution)/shard_map/ppermute | solution.py:367
  90.2 2.1 %collective-permute-done.26 = f32[16,128]{1,0:T(8,128)S(1)} collective-permute-done((f32[16,128]{1,0:T(8,128)S(1)}, f32[16,128]{1,0:T(8,128)S(1)}, u32[]{:S(2)}, u32[]{:S(2)}) %collective-permute-start.26) | collective-permute-done | bytes 8224 | tf_op jit(solution)/shard_map/ppermute | solution.py:367
  92.3 2.6 %collective-permute-start.27 = (f32[16,128]{1,0:T(8,128)S(1)}, f32[16,128]{1,0:T(8,128)S(1)}, u32[]{:S(2)}, u32[]{:S(2)}) collective-permute-start(f32[16,128]{1,0:T(8,128)S(1)} %add.59.refs_0_), channel_id=1, source_target_pairs={{0,8},{2,10},{4,12},{6,14},{8,0},{10,2},{12,4},{14,6},{1,9},{3,11}... | collective-permute-start | bytes 24584 | tf_op jit(solution)/shard_map/ppermute | solution.py:369
  95.0 1.9 %collective-permute-done.27.refs_1_ = f32[16,128]{1,0:T(8,128)S(1)} collective-permute-done((f32[16,128]{1,0:T(8,128)S(1)}, f32[16,128]{1,0:T(8,128)S(1)}, u32[]{:S(2)}, u32[]{:S(2)}) %collective-permute-start.27) | collective-permute-done | bytes 8224 | tf_op jit(solution)/shard_map/ppermute | solution.py:369
  96.9 1.1 %shard_map.87 = f32[256,512]{1,0:T(8,128)} custom-call(f32[256,512]{1,0:T(8,128)S(1)} %bitcast.10, f32[256,512]{1,0:T(8,128)S(1)} %get-tuple-element.29.update_in, f32[16,128]{1,0:T(8,128)S(1)} %add.59.refs_0_, f32[16,128]{1,0:T(8,128)S(1)} %collective-permute-done.27.refs_1_), custom_call_target="tpu_custom_call" | custom-call | tf_op jit(solution)/shard_map/pallas_call | solution.py:479
  (52 shorter events, 7.2 us)
Async XLA Ops:
  1.7 9.4 %collective-permute-start.2 = (bf16[256,512]{1,0:T(8,128)(2,1)S(1)}, bf16[256,512]{1,0:T(8,128)(2,1)S(1)}, u32[]{:S(2)}, u32[]{:S(2)}) collective-permute-start(bf16[256,512]{1,0:T(8,128)(2,1)S(1)} %bitcast_convert_fusion.refs_0_), channel_id=1, source_target_pairs={{4,0},{8,4},{12,8},{14,12},{10,14},{6,10},{2,6},{0,2},{5,1},{9,5},... | collective-permute-start | bytes 786440 | tf_op jit(solution)/shard_map/ppermute | solution.py:306
  4.7 8.0 %collective-permute-start.1 = (bf16[256,512]{1,0:T(8,128)(2,1)S(1)}, bf16[256,512]{1,0:T(8,128)(2,1)S(1)}, u32[]{:S(2)}, u32[]{:S(2)}) collective-permute-start(bf16[256,512]{1,0:T(8,128)(2,1)S(1)} %bitcast_convert_fusion.refs_0_), channel_id=1, source_target_pairs={{0,4},{4,8},{8,12},{12,14},{14,10},{10,6},{6,2},{2,0},{1,5},{5,9},... | collective-permute-start | bytes 786440 | tf_op jit(solution)/shard_map/ppermute | solution.py:303
  11.1 7.5 %collective-permute-start.4 = (bf16[256,512]{1,0:T(8,128)(2,1)S(1)}, bf16[256,512]{1,0:T(8,128)(2,1)S(1)}, u32[]{:S(2)}, u32[]{:S(2)}) collective-permute-start(bf16[256,512]{1,0:T(8,128)(2,1)S(1)} %collective-permute-done.2.refs_2_), channel_id=1, source_target_pairs={{4,0},{8,4},{12,8},{14,12},{10,14},{6,10},{2,6},{0,2},{5,1},{9,5},... | collective-permute-start | bytes 786440 | tf_op jit(solution)/shard_map/ppermute | solution.py:306
  12.7 7.2 %collective-permute-start.3 = (bf16[256,512]{1,0:T(8,128)(2,1)S(1)}, bf16[256,512]{1,0:T(8,128)(2,1)S(1)}, u32[]{:S(2)}, u32[]{:S(2)}) collective-permute-start(bf16[256,512]{1,0:T(8,128)(2,1)S(1)} %collective-permute-done.1.refs_1_), channel_id=1, source_target_pairs={{0,4},{4,8},{8,12},{12,14},{14,10},{10,6},{6,2},{2,0},{1,5},{5,9},... | collective-permute-start | bytes 786440 | tf_op jit(solution)/shard_map/ppermute | solution.py:303
  18.6 6.6 %collective-permute-start.6 = (bf16[256,512]{1,0:T(8,128)(2,1)S(1)}, bf16[256,512]{1,0:T(8,128)(2,1)S(1)}, u32[]{:S(2)}, u32[]{:S(2)}) collective-permute-start(bf16[256,512]{1,0:T(8,128)(2,1)S(1)} %collective-permute-done.4.refs_4_), channel_id=1, source_target_pairs={{4,0},{8,4},{12,8},{14,12},{10,14},{6,10},{2,6},{0,2},{5,1},{9,5},... | collective-permute-start | bytes 786440 | tf_op jit(solution)/shard_map/ppermute | solution.py:306
  19.9 6.4 %collective-permute-start.5 = (bf16[256,512]{1,0:T(8,128)(2,1)S(1)}, bf16[256,512]{1,0:T(8,128)(2,1)S(1)}, u32[]{:S(2)}, u32[]{:S(2)}) collective-permute-start(bf16[256,512]{1,0:T(8,128)(2,1)S(1)} %collective-permute-done.3.refs_3_), channel_id=1, source_target_pairs={{0,4},{4,8},{8,12},{12,14},{14,10},{10,6},{6,2},{2,0},{1,5},{5,9},... | collective-permute-start | bytes 786440 | tf_op jit(solution)/shard_map/ppermute | solution.py:303
  20.6 5.8 %collective-permute-start.9 = (bf16[256,512]{1,0:T(8,128)(2,1)S(1)}, bf16[256,512]{1,0:T(8,128)(2,1)S(1)}, u32[]{:S(2)}, u32[]{:S(2)}) collective-permute-start(bf16[256,512]{1,0:T(8,128)(2,1)S(1)} %bitcast_convert_fusion.refs_0_), channel_id=1, source_target_pairs={{0,1},{1,0},{2,3},{3,2},{4,5},{5,4},{6,7},{7,6},{8,9},{9,8},{10,11... | collective-permute-start | bytes 786440 | tf_op jit(solution)/shard_map/ppermute | solution.py:285
  20.6 7.5 %collective-permute-start = (bf16[512,512]{1,0:T(8,128)(2,1)}, bf16[512,512]{1,0:T(8,128)(2,1)S(1)}, u32[]{:S(2)}, u32[]{:S(2)}) collective-permute-start(bf16[512,512]{1,0:T(8,128)(2,1)} %bitcast.15), channel_id=1, source_target_pairs={{0,1},{1,0},{2,3},{3,2},{4,5},{5,4},{6,7},{7,6},{8,9},{9,8},{10,11... | collective-permute-start | bytes 1572872 | tf_op jit(solution)/shard_map/ppermute | solution.py:285
  21.2 12.6 %collective-permute-start.10 = (bf16[512,512]{1,0:T(8,128)(2,1)S(1)}, bf16[512,512]{1,0:T(8,128)(2,1)S(1)}, u32[]{:S(2)}, u32[]{:S(2)}) collective-permute-start(bf16[512,512]{1,0:T(8,128)(2,1)S(1)} %pad_maximum_fusion), channel_id=1, source_target_pairs={{0,1},{1,0},{2,3},{3,2},{4,5},{5,4},{6,7},{7,6},{8,9},{9,8},{10,11... | collective-permute-start | bytes 1572872 | tf_op jit(solution)/shard_map/ppermute | solution.py:285
  25.2 9.9 %collective-permute-start.11 = (bf16[512,512]{1,0:T(8,128)(2,1)S(1)}, bf16[512,512]{1,0:T(8,128)(2,1)S(1)}, u32[]{:S(2)}, u32[]{:S(2)}) collective-permute-start(bf16[512,512]{1,0:T(8,128)(2,1)S(1)} %pad_maximum_fusion.1), channel_id=1, source_target_pairs={{0,1},{1,0},{2,3},{3,2},{4,5},{5,4},{6,7},{7,6},{8,9},{9,8},{10,11... | collective-permute-start | bytes 1572872 | tf_op jit(solution)/shard_map/ppermute | solution.py:285
  26.3 8.7 %collective-permute-start.12 = (bf16[512,512]{1,0:T(8,128)(2,1)S(1)}, bf16[512,512]{1,0:T(8,128)(2,1)S(1)}, u32[]{:S(2)}, u32[]{:S(2)}) collective-permute-start(bf16[512,512]{1,0:T(8,128)(2,1)S(1)} %pad_maximum_fusion.2), channel_id=1, source_target_pairs={{0,1},{1,0},{2,3},{3,2},{4,5},{5,4},{6,7},{7,6},{8,9},{9,8},{10,11... | collective-permute-start | bytes 1572872 | tf_op jit(solution)/shard_map/ppermute | solution.py:285
  26.5 5.9 %collective-permute-start.8 = (bf16[128,512]{1,0:T(8,128)(2,1)S(1)}, bf16[128,512]{1,0:T(8,128)(2,1)S(1)}, u32[]{:S(2)}, u32[]{:S(2)}) collective-permute-start(bf16[128,512]{1,0:T(8,128)(2,1)S(1)} %slice.87), channel_id=1, source_target_pairs={{4,0},{8,4},{12,8},{14,12},{10,14},{6,10},{2,6},{0,2},{5,1},{9,5},... | collective-permute-start | bytes 393224 | tf_op jit(solution)/shard_map/ppermute | solution.py:306
  28.1 5.6 %collective-permute-start.7 = (bf16[128,512]{1,0:T(8,128)(2,1)S(1)}, bf16[128,512]{1,0:T(8,128)(2,1)S(1)}, u32[]{:S(2)}, u32[]{:S(2)}) collective-permute-start(bf16[128,512]{1,0:T(8,128)(2,1)S(1)} %slice.86), channel_id=1, source_target_pairs={{0,4},{4,8},{8,12},{12,14},{14,10},{10,6},{6,2},{2,0},{1,5},{5,9},... | collective-permute-start | bytes 393224 | tf_op jit(solution)/shard_map/ppermute | solution.py:303
  32.4 1.3 %collective-permute-start.14 = (bf16[128,512]{1,0:T(8,128)(2,1)S(1)}, bf16[128,512]{1,0:T(8,128)(2,1)S(1)}, u32[]{:S(2)}, u32[]{:S(2)}) collective-permute-start(bf16[128,512]{1,0:T(8,128)(2,1)S(1)} %collective-permute-done.8.refs_8_), channel_id=1, source_target_pairs={{0,1},{1,0},{2,3},{3,2},{4,5},{5,4},{6,7},{7,6},{8,9},{9,8},{10,11... | collective-permute-start | bytes 393224 | tf_op jit(solution)/shard_map/ppermute | solution.py:285
  33.7 1.3 %collective-permute-start.13 = (bf16[128,512]{1,0:T(8,128)(2,1)S(1)}, bf16[128,512]{1,0:T(8,128)(2,1)S(1)}, u32[]{:S(2)}, u32[]{:S(2)}) collective-permute-start(bf16[128,512]{1,0:T(8,128)(2,1)S(1)} %collective-permute-done.7.refs_7_), channel_id=1, source_target_pairs={{0,1},{1,0},{2,3},{3,2},{4,5},{5,4},{6,7},{7,6},{8,9},{9,8},{10,11... | collective-permute-start | bytes 393224 | tf_op jit(solution)/shard_map/ppermute | solution.py:285
  52.4 1.6 %collective-permute-start.15 = (bf16[256,512]{1,0:T(8,128)(2,1)S(1)}, bf16[256,512]{1,0:T(8,128)(2,1)S(1)}, u32[]{:S(2)}, u32[]{:S(2)}) collective-permute-start(bf16[256,512]{1,0:T(8,128)(2,1)S(1)} %get-tuple-element.20), channel_id=1, source_target_pairs={{0,1},{1,0},{2,3},{3,2},{4,5},{5,4},{6,7},{7,6},{8,9},{9,8},{10,11... | collective-permute-start | bytes 786440 | tf_op jit(solution)/shard_map/ppermute | solution.py:285
  54.0 3.9 %collective-permute-start.16 = (bf16[1792,512]{1,0:T(8,128)(2,1)S(1)}, bf16[1792,512]{1,0:T(8,128)(2,1)S(1)}, u32[]{:S(2)}, u32[]{:S(2)}) collective-permute-start(bf16[1792,512]{1,0:T(8,128)(2,1)S(1)} %get-tuple-element.21), channel_id=1, source_target_pairs={{0,1},{1,0},{2,3},{3,2},{4,5},{5,4},{6,7},{7,6},{8,9},{9,8},{10,11... | collective-permute-start | bytes 5505032 | tf_op jit(solution)/shard_map/ppermute | solution.py:285
  54.3 5.8 %collective-permute-start.18 = (bf16[128,512]{1,0:T(8,128)(2,1)S(1)}, bf16[128,512]{1,0:T(8,128)(2,1)S(1)}, u32[]{:S(2)}, u32[]{:S(2)}) collective-permute-start(bf16[128,512]{1,0:T(8,128)(2,1)S(1)} %get-tuple-element.39), channel_id=1, source_target_pairs={{4,0},{8,4},{12,8},{14,12},{10,14},{6,10},{2,6},{0,2},{5,1},{9,5},... | collective-permute-start | bytes 393224 | tf_op jit(solution)/shard_map/ppermute | solution.py:306
  55.9 5.5 %collective-permute-start.17 = (bf16[128,512]{1,0:T(8,128)(2,1)S(1)}, bf16[128,512]{1,0:T(8,128)(2,1)S(1)}, u32[]{:S(2)}, u32[]{:S(2)}) collective-permute-start(bf16[128,512]{1,0:T(8,128)(2,1)S(1)} %get-tuple-element.40), channel_id=1, source_target_pairs={{0,4},{4,8},{8,12},{12,14},{14,10},{10,6},{6,2},{2,0},{1,5},{5,9},... | collective-permute-start | bytes 393224 | tf_op jit(solution)/shard_map/ppermute | solution.py:303
  58.1 25.4 %copy-start = (f32[1,256,512]{2,1,0:T(8,128)S(1)}, f32[1,256,512]{2,1,0:T(8,128)}, u32[]{:S(2)}) copy-start(f32[1,256,512]{2,1,0:T(8,128)} %param.9) | copy-start | bytes 1572868
  58.1 25.4 %copy-start.1 = (f32[1,256,512]{2,1,0:T(8,128)S(1)}, f32[1,256,512]{2,1,0:T(8,128)}, u32[]{:S(2)}) copy-start(f32[1,256,512]{2,1,0:T(8,128)} %param.10) | copy-start | bytes 1572868
  58.1 25.4 %copy-start.2 = (f32[1,256,512]{2,1,0:T(8,128)S(1)}, f32[1,256,512]{2,1,0:T(8,128)}, u32[]{:S(2)}) copy-start(f32[1,256,512]{2,1,0:T(8,128)} %param.11) | copy-start | bytes 1572868
  61.5 7.5 %collective-permute-start.19 = (bf16[256,512]{1,0:T(8,128)(2,1)S(1)}, bf16[256,512]{1,0:T(8,128)(2,1)S(1)}, u32[]{:S(2)}, u32[]{:S(2)}) collective-permute-start(bf16[256,512]{1,0:T(8,128)(2,1)S(1)} %pad_maximum_fusion.3), channel_id=1, source_target_pairs={{0,4},{4,8},{8,12},{12,14},{14,10},{10,6},{6,2},{2,0},{1,5},{5,9},... | collective-permute-start | bytes 786440 | tf_op jit(solution)/shard_map/ppermute | solution.py:303
  62.0 7.2 %collective-permute-start.20 = (bf16[256,512]{1,0:T(8,128)(2,1)S(1)}, bf16[256,512]{1,0:T(8,128)(2,1)S(1)}, u32[]{:S(2)}, u32[]{:S(2)}) collective-permute-start(bf16[256,512]{1,0:T(8,128)(2,1)S(1)} %pad_maximum_fusion.4), channel_id=1, source_target_pairs={{4,0},{8,4},{12,8},{14,12},{10,14},{6,10},{2,6},{0,2},{5,1},{9,5},... | collective-permute-start | bytes 786440 | tf_op jit(solution)/shard_map/ppermute | solution.py:306
  69.3 6.4 %collective-permute-start.21 = (bf16[256,512]{1,0:T(8,128)(2,1)S(1)}, bf16[256,512]{1,0:T(8,128)(2,1)S(1)}, u32[]{:S(2)}, u32[]{:S(2)}) collective-permute-start(bf16[256,512]{1,0:T(8,128)(2,1)S(1)} %get-tuple-element.25), channel_id=1, source_target_pairs={{0,4},{4,8},{8,12},{12,14},{14,10},{10,6},{6,2},{2,0},{1,5},{5,9},... | collective-permute-start | bytes 786440 | tf_op jit(solution)/shard_map/ppermute | solution.py:303
  69.8 6.4 %collective-permute-start.22 = (bf16[256,512]{1,0:T(8,128)(2,1)S(1)}, bf16[256,512]{1,0:T(8,128)(2,1)S(1)}, u32[]{:S(2)}, u32[]{:S(2)}) collective-permute-start(bf16[256,512]{1,0:T(8,128)(2,1)S(1)} %get-tuple-element.26), channel_id=1, source_target_pairs={{4,0},{8,4},{12,8},{14,12},{10,14},{6,10},{2,6},{0,2},{5,1},{9,5},... | collective-permute-start | bytes 786440 | tf_op jit(solution)/shard_map/ppermute | solution.py:306
  76.4 6.4 %collective-permute-start.23 = (bf16[256,512]{1,0:T(8,128)(2,1)S(1)}, bf16[256,512]{1,0:T(8,128)(2,1)S(1)}, u32[]{:S(2)}, u32[]{:S(2)}) collective-permute-start(bf16[256,512]{1,0:T(8,128)(2,1)S(1)} %get-tuple-element.27), channel_id=1, source_target_pairs={{0,4},{4,8},{8,12},{12,14},{14,10},{10,6},{6,2},{2,0},{1,5},{5,9},... | collective-permute-start | bytes 786440 | tf_op jit(solution)/shard_map/ppermute | solution.py:303
  77.1 6.4 %collective-permute-start.24 = (bf16[256,512]{1,0:T(8,128)(2,1)S(1)}, bf16[256,512]{1,0:T(8,128)(2,1)S(1)}, u32[]{:S(2)}, u32[]{:S(2)}) collective-permute-start(bf16[256,512]{1,0:T(8,128)(2,1)S(1)} %get-tuple-element.28), channel_id=1, source_target_pairs={{4,0},{8,4},{12,8},{14,12},{10,14},{6,10},{2,6},{0,2},{5,1},{9,5},... | collective-permute-start | bytes 786440 | tf_op jit(solution)/shard_map/ppermute | solution.py:306
  85.0 3.7 %collective-permute-start.25 = (f32[16,128]{1,0:T(8,128)S(1)}, f32[16,128]{1,0:T(8,128)S(1)}, u32[]{:S(2)}, u32[]{:S(2)}) collective-permute-start(f32[16,128]{1,0:T(8,128)S(1)} %get-tuple-element.30), channel_id=1, source_target_pairs={{0,2},{2,0},{4,6},{6,4},{8,10},{10,8},{12,14},{14,12},{1,3},{3,1},... | collective-permute-start | bytes 24584 | tf_op jit(solution)/shard_map/ppermute | solution.py:367
  88.7 3.7 %collective-permute-start.26 = (f32[16,128]{1,0:T(8,128)S(1)}, f32[16,128]{1,0:T(8,128)S(1)}, u32[]{:S(2)}, u32[]{:S(2)}) collective-permute-start(f32[16,128]{1,0:T(8,128)S(1)} %add.58), channel_id=1, source_target_pairs={{0,4},{2,6},{4,0},{6,2},{8,12},{10,14},{12,8},{14,10},{1,5},{3,7},... | collective-permute-start | bytes 24584 | tf_op jit(solution)/shard_map/ppermute | solution.py:367
  92.3 4.5 %collective-permute-start.27 = (f32[16,128]{1,0:T(8,128)S(1)}, f32[16,128]{1,0:T(8,128)S(1)}, u32[]{:S(2)}, u32[]{:S(2)}) collective-permute-start(f32[16,128]{1,0:T(8,128)S(1)} %add.59.refs_0_), channel_id=1, source_target_pairs={{0,8},{2,10},{4,12},{6,14},{8,0},{10,2},{12,4},{14,6},{1,9},{3,11}... | collective-permute-start | bytes 24584 | tf_op jit(solution)/shard_map/ppermute | solution.py:369
